TPU v7x, 128 devices: a whole 4x4x4 slice. The times are simulated.
128 devices in a mesh: dp: 32 (over z_hi, y, x), mp: 4 (over z_lo, core).
Axes of the slice: x: 4, y: 4, z: 4 (z_hi: 2, z_lo: 2; z = z_hi * 2 + z_lo), core: 2. Of those that a mesh axis runs over, the one named last changes fastest.
Arguments:
- attention: bfloat16 [16384, 2048], P('dp', 'mp')
- out_proj: bfloat16 [2048, 5376], P('mp'), may hold values from -0.125 to 0.125
- post_gain: float32 [5376], replicated, may hold values from 0.5 to 1.5
- residual: bfloat16 [16384, 5376], P('dp', 'mp'), may hold values from -6 to 6
- cotangent: bfloat16 [16384, 5376], P('dp', 'mp'), may hold values from -6 to 6
- counted: int32 [30], replicated, may hold values from 0 to 31, as said below
- master: float32 [4, 512, 5376], P('mp', 'dp'), may hold values from -0.125 to 0.125
- moment: float32 [4, 512, 5376], P('mp', 'dp'), may hold values from -12 to 12
- second: float32 [4, 512, 5376], P('mp', 'dp'), may hold values from 1 to 100
Outputs:
- layer_out: bfloat16 [16384, 5376], P('dp', 'mp')
- attn_grad: bfloat16 [16384, 2048], P('dp', 'mp')
- new_proj: bfloat16 [2048, 5376], P('mp')
- new_master: float32 [4, 512, 5376], P('mp', 'dp')
- new_moment: float32 [4, 512, 5376], P('mp', 'dp')
- new_second: float32 [4, 512, 5376], P('mp', 'dp')
Inputs may be any that keep to these rules, and one draw needn't show every extreme that they name: 30 distinct replica indices; the first and the last replica are always counted.
All inputs are finite; a program needn't handle non-finite values.
Results may differ from a plain program's by a relative error of at most 0.0049.
Values may be sent and summed in bfloat16 or wider, within the bound.
No kernel may reach another device: no remote copies, remote signals or barrier semaphores. Data moves between devices by JAX's collectives and lax.ppermute only.
A program may use at most 128 MiB of HBM per device.

v0:
```python
import jax
import jax.numpy as jnp
from jax import lax
from jax.sharding import PartitionSpec as P

norm_eps = 1e-06
beta_one = 0.9
beta_two = 0.999
adam_eps = 1e-08
learn_rate = 0.01
weight_decay = 0.1
step_number = 100.0


def local(attention, out_proj, post_gain, residual, cotangent, counted, master, moment, second):
    part_width = residual.shape[1]
    full_width = post_gain.shape[0]
    col_start = lax.axis_index("mp") * part_width
    gain_part = lax.dynamic_slice_in_dim(post_gain, col_start, part_width, 0)
    counted_flag = jnp.sum((counted == lax.axis_index("dp")).astype(jnp.float32))
    partial_value = jnp.dot(attention, out_proj, preferred_element_type=jnp.float32)
    summed = lax.psum(partial_value, "mp")
    cot_full = lax.all_gather(cotangent, "mp", axis=1, tiled=True)
    scaled = cot_full.astype(jnp.float32) * post_gain[None, :]
    inv_rms = lax.rsqrt(jnp.sum(summed * summed, axis=1, keepdims=True) / full_width + norm_eps)
    proj = jnp.sum(scaled * summed, axis=1, keepdims=True) / full_width
    normed = lax.dynamic_slice_in_dim(summed, col_start, part_width, 1) * inv_rms
    layer_out = (residual.astype(jnp.float32) + gain_part[None, :] * normed).astype(jnp.bfloat16)
    pre_grad = (inv_rms * scaled - summed * inv_rms**3 * proj).astype(jnp.bfloat16)
    attn_grad = lax.dot_general(
        pre_grad, out_proj, (((1,), (1,)), ((), ())), preferred_element_type=jnp.float32
    ).astype(jnp.bfloat16)
    left = (attention.astype(jnp.float32) * counted_flag).astype(jnp.bfloat16)
    grad_term = lax.dot_general(
        left, pre_grad, (((0,), (0,)), ((), ())), preferred_element_type=jnp.float32
    )
    owned_sum = lax.psum_scatter(grad_term, "dp", scatter_dimension=0, tiled=True)
    mean_grad = (owned_sum / counted.shape[0])[None, :, :]
    new_moment = beta_one * moment + (1.0 - beta_one) * mean_grad
    new_second = beta_two * second + (1.0 - beta_two) * mean_grad * mean_grad
    update = (
        new_moment
        / (1.0 - beta_one**step_number)
        / (jnp.sqrt(new_second / (1.0 - beta_two**step_number)) + adam_eps)
    )
    new_master = master - learn_rate * (update + weight_decay * master)
    new_proj = lax.all_gather(new_master[0].astype(jnp.bfloat16), "dp", axis=0, tiled=True)
    return (layer_out, attn_grad, new_proj, new_master, new_moment, new_second)


def solution(mesh):
    placed = (
        P("dp", "mp"),
        P("mp", None),
        P(),
        P("dp", "mp"),
        P("dp", "mp"),
        P(),
        P("mp", "dp", None),
        P("mp", "dp", None),
        P("mp", "dp", None),
    )
    return jax.shard_map(
        local,
        mesh=mesh,
        in_specs=placed,
        out_specs=(
            P("dp", "mp"),
            P("dp", "mp"),
            P("mp", None),
            P("mp", "dp", None),
            P("mp", "dp", None),
            P("mp", "dp", None),
        ),
        check_vma=False,
    )
```

profile of v0, /device:TPU:6, one launch (start us, length us, event | category | flops | bytes accessed | tf_op | source)
XLA Modules:
  0.0 653.3 jit_solution(4792624550130288608)
XLA Ops:
  7.2 0.0 all-gather.4.cloned.1.call-start
  7.2 0.7 all-gather.4.cloned.1.call-update
  7.9 0.0 all-reduce.2.cloned.1.call-start
  7.9 9.8 %fusion.4 = f32[512,5376]{1,0:T(8,128)} fusion(bf16[512,512]{1,0:T(8,128)(2,1)} %param.9, bf16[512,5376]{1,0:T(8,128)(2,1)} %param.10), kind=kOutput, calls=%fused_computation.18 | convolution fusion | flops 2818572288 | bytes 17039360 | tf_op jit(solution)/shard_map/dot_general | solution.py:21
  17.8 0.0 reduce-scatter.2.cloned.1.call-start
  17.8 0.6 copy-done.6
  18.4 0.6 fusion.2
  19.0 49.8 %all-gather.4.cloned.1.call-done = bf16[512,5376]{0,1:T(8,128)(2,1)} async-done(((bf16[512,1344]{0,1:T(8,128)(2,1)}), bf16[512,5376]{0,1:T(8,128)(2,1)}) %all-gather.4.cloned.1.call-update) | async-done | bytes 5505040 | tf_op jit(solution)/shard_map/all_gather | solution.py:23
  68.7 8.3 %copy.19 = bf16[512,5376]{1,0:T(8,128)(2,1)} copy(bf16[512,5376]{0,1:T(8,128)(2,1)} %all-gather.4.cloned.1.call-done) | data formatting | bytes 11010048 | tf_op jit(solution)/shard_map/all_gather | solution.py:23
  77.0 197.3 %all-reduce.2.cloned.1.call-done = f32[512,5376]{1,0:T(8,128)} async-done(((f32[512,5376]{1,0:T(8,128)}), f32[512,5376]{1,0:T(8,128)}) %all-reduce.2.cloned.1.call-update) | async-done | bytes 11010064 | tf_op jit(solution)/shard_map/psum | solution.py:22
  274.3 7.9 %multiply_reduce_fusion = (f32[512]{0:T(512)S(1)}, f32[512]{0:T(512)S(1)}) fusion(f32[512,5376]{1,0:T(8,128)} %all-reduce.2.cloned.1.call-done, bf16[512,5376]{1,0:T(8,128)(2,1)} %copy.19, f32[5376]{0:T(1024)S(1)} %copy-done.5), kind=kLoop, calls=%fused_computation.1 | loop fusion | flops 16514048 | bytes 16540672 | tf_op jit(solution)/shard_map/reduce_sum | solution.py:26
  282.3 12.2 %subtract_convert_fusion = bf16[512,5376]{1,0:T(8,128)(2,1)} fusion(f32[512,5376]{1,0:T(8,128)} %all-reduce.2.cloned.1.call-done, bf16[512,5376]{1,0:T(8,128)(2,1)} %copy.19, f32[512]{0:T(512)S(1)} %get-tuple-element.26, f32[512]{0:T(512)S(1)} %get-tuple-element.24, f32[5376]{0:T(1024)S(1)} %copy-done.5, f32[512]{0:T(512)S(1)} %get-tuple-element.25), kind=kLoop, calls=%fused_computation | loop fusion | flops 19267584 | bytes 22047744 | tf_op jit(solution)/shard_map/convert_element_type | solution.py:29
  294.4 8.9 %fusion = f32[512,5376]{1,0:T(8,128)} fusion(bf16[512,5376]{1,0:T(8,128)(2,1)} %subtract_convert_fusion, bf16[512,512]{1,0:T(8,128)(2,1)S(1)} %copy-done, f32[]{:T(128)} %fusion.2), kind=kOutput, calls=%fused_computation.7 | convolution fusion | flops 2819358720 | bytes 17039364 | tf_op jit(solution)/shard_map/dot_general | solution.py:34
  303.3 0.0 reduce-scatter.2.cloned.1.call-update
  303.4 0.2 all-gather.6.cloned.1.call-start
  303.6 247.6 %reduce-scatter.2.cloned.1.call-done = f32[16,5376]{1,0:T(8,128)} async-done(((f32[512,5376]{1,0:T(8,128)}), f32[16,5376]{1,0:T(8,128)}) %reduce-scatter.2.cloned.1.call-update) | async-done | bytes 344080 | tf_op jit(solution)/shard_map/reduce_scatter | solution.py:37
  551.2 2.2 fusion.3
  553.4 0.8 copy.18
  554.2 0.1 dynamic_slice.6
  554.3 2.9 add_convert_fusion
  557.2 1.5 copy.20
  558.7 8.0 %convolution_convert_fusion = bf16[512,512]{1,0:T(8,128)(2,1)} fusion(bf16[512,5376]{1,0:T(8,128)(2,1)} %subtract_convert_fusion, bf16[512,5376]{1,0:T(8,128)(2,1)} %param.10), kind=kOutput, calls=%fused_computation.5 | convolution fusion | flops 2818834432 | bytes 11534336 | tf_op jit(solution)/shard_map/dot_general | solution.py:30
  566.7 74.7 %all-gather.6.cloned.1.call-done = bf16[1,512,5376]{2,1,0:T(8,128)(2,1)} async-done(((bf16[1,16,5376]{2,1,0:T(8,128)(2,1)}), bf16[1,512,5376]{2,1,0:T(8,128)(2,1)}) %all-gather.6.cloned.1.call-update) | async-done | bytes 5505040 | tf_op jit(solution)/shard_map/all_gather | solution.py:47
  641.4 5.4 copy.23
  (16 shorter events, 0.1 us)
Async XLA Ops:
  7.2 61.6 %all-gather.4.cloned.1.call-start = ((), (), s32[]{:S(2)}) async-start(), calls=%async_computation.2 | async-start | bytes 6881280 | tf_op jit(solution)/shard_map/all_gather | solution.py:23
  7.9 266.4 %all-reduce.2.cloned.1.call-start = ((), (), s32[]{:S(2)}) async-start(), calls=%async_computation.1 | async-start | bytes 22020096 | tf_op jit(solution)/shard_map/psum | solution.py:22
  17.7 0.7 copy-start.6
  17.8 533.4 %reduce-scatter.2.cloned.1.call-start = ((), (), s32[]{:S(2)}) async-start(), calls=%async_computation.3 | async-start | bytes 11354112 | tf_op jit(solution)/shard_map/reduce_scatter | solution.py:37
  19.0 255.3 %copy-start.5 = (f32[5376]{0:T(1024)S(1)}, f32[5376]{0:T(1024)}, u32[]{:S(2)}) copy-start(f32[5376]{0:T(1024)} %param.11) | copy-start | bytes 64516
  282.3 12.2 %copy-start = (bf16[512,512]{1,0:T(8,128)(2,1)S(1)}, bf16[512,512]{1,0:T(8,128)(2,1)}, u32[]{:S(2)}) copy-start(bf16[512,512]{1,0:T(8,128)(2,1)} %param.9) | copy-start | bytes 1572868
  303.3 247.9 %copy-start.2 = (f32[1,16,5376]{2,1,0:T(8,128)S(1)}, f32[1,16,5376]{2,1,0:T(8,128)}, u32[]{:S(2)}) copy-start(f32[1,16,5376]{2,1,0:T(8,128)} %param.15) | copy-start | bytes 1032196
  303.3 247.9 %copy-start.3 = (f32[1,16,5376]{2,1,0:T(8,128)S(1)}, f32[1,16,5376]{2,1,0:T(8,128)}, u32[]{:S(2)}) copy-start(f32[1,16,5376]{2,1,0:T(8,128)} %param.16) | copy-start | bytes 1032196
  303.3 247.9 %copy-start.4 = (f32[1,16,5376]{2,1,0:T(8,128)S(1)}, f32[1,16,5376]{2,1,0:T(8,128)}, u32[]{:S(2)}) copy-start(f32[1,16,5376]{2,1,0:T(8,128)} %param.17) | copy-start | bytes 1032196
  303.3 250.1 %copy-start.1 = (bf16[512,1344]{0,1:T(8,128)(2,1)S(1)}, bf16[512,1344]{0,1:T(8,128)(2,1)}, u32[]{:S(2)}) copy-start(bf16[512,1344]{0,1:T(8,128)(2,1)} %param.12) | copy-start | bytes 4128772
  303.4 338.0 %all-gather.6.cloned.1.call-start = ((), (), s32[]{:S(2)}) async-start(), calls=%async_computation.4 | async-start | bytes 5677056 | tf_op jit(solution)/shard_map/all_gather | solution.py:47
Sparse Core Ops, SparseCore 0:
  9.7 59.0 all-gather.3
  71.4 202.8 all-reduce.1
  303.5 247.6 reduce-scatter.1
  554.4 86.9 all-gather.5
where the time goes:
time: 655 us; the launch traced here: 653 us
  waiting for transfers between devices  570 us (87%)
  matrix products  26.7 us (4%)
  other arithmetic  25.8 us (4%)
  local copies, waits for them, and re-layouts  16.6 us (3%)
  between operations  13.8 us (2%)
    reduce_scatter x1, waiting for transfers between devices, local(): lax.psum_scatter(grad_term, 'dp', scatter_dimension=0, tiled=True)  248 us
    psum x1, waiting for transfers between devices, local(): summed = lax.psum(partial_value, 'mp')  197 us
    all_gather x1, waiting for transfers between devices, local(): lax.all_gather(new_master[0].astype(jnp.bfloat16), 'dp', axis=0, tiled=True)  74.7 us
    all_gather x1, waiting for transfers between devices, local(): cot_full = lax.all_gather(cotangent, 'mp', axis=1, tiled=True)  49.8 us
  transfers between devices with their start and end apart: 4, of which 4 were waited for; matrix products, arithmetic and copies ran while one was open for 5% of the time, Pallas kernels for 0%

commit v1 on v0

v1 whole, which is shorter than its diff:
```python
import jax
import jax.numpy as jnp
from jax import lax
from jax.sharding import Mesh, PartitionSpec as P

norm_eps = 1e-06
beta_one = 0.9
beta_two = 0.999
adam_eps = 1e-08
learn_rate = 0.01
weight_decay = 0.1
step_number = 100.0

axes = ("zh", "y", "x", "zl", "c")
bf16 = jnp.bfloat16
f32 = jnp.float32


def pick(stacked, index, axis=0):
    return lax.dynamic_index_in_dim(stacked, index, axis, keepdims=False)


def ring_step(value, axis, step):
    size = 4
    return lax.ppermute(value, axis, [(i, (i + step) % size) for i in range(size)])


def flip(value, axis):
    return lax.ppermute(value, axis, [(0, 1), (1, 0)])


def flip_mp(value, bits):
    return lax.ppermute(value, ("zl", "c"), [(i, i ^ bits) for i in range(4)])


def ring_sum(pieces, axis):
    place = lax.axis_index(axis)
    dim = {"y": 2, "x": 3}[axis]
    dim = min(dim, pieces.ndim - 3)
    got = [ring_step(pick(pieces, (place + s) % 4, dim), axis, s) for s in (2, 1, 3)]
    total = pick(pieces, place, dim).astype(f32)
    for one in got:
        total = total + one.astype(f32)
    return total.astype(bf16)


def local(attention, out_proj, post_gain, residual, cotangent, counted, master, moment, second):
    zh, y, x, zl, c = (lax.axis_index(a) for a in axes)
    place = zl * 2 + c
    replica = (zh * 4 + y) * 4 + x
    tokens, part_width = residual.shape
    heads = attention.shape[1]
    full_width = post_gain.shape[0]
    gain_part = lax.dynamic_slice_in_dim(post_gain, place * part_width, part_width, 0)[None, :]
    counted_flag = jnp.sum((counted == replica).astype(f32))

    columns = jnp.stack([out_proj[:, j * part_width : (j + 1) * part_width] for j in range(4)])
    columns = lax.optimization_barrier(columns)
    weights = [
        pick(columns, place),
        flip(pick(columns, place ^ 1), "c"),
        lax.ppermute(
            pick(columns, place ^ 2), ("zh", "zl"), [(i, (i + 1) % 4) for i in range(4)]
        ),
        lax.ppermute(
            pick(columns, place ^ 3),
            ("zh", "zl", "c"),
            [(i * 2 + j, ((i + 3) % 4) * 2 + 1 - j) for i in range(4) for j in range(2)],
        ),
    ]
    far = flip(attention, "zl")
    near = flip(attention, "c")
    features = [attention, near, far, flip(far, "c")]

    pre = 0.0
    for feature, weight in zip(features, weights):
        pre = pre + jnp.dot(feature, weight, preferred_element_type=f32)
    scaled = cotangent.astype(f32) * gain_part
    stats = jnp.stack([jnp.sum(pre * pre, axis=1), jnp.sum(scaled * pre, axis=1)])
    stats = stats + flip(stats, "c")
    stats = stats + flip(stats, "zl")
    inv_rms = lax.rsqrt(stats[0] / full_width + norm_eps)[:, None]
    proj = (stats[1] / full_width)[:, None]
    layer_out = (residual.astype(f32) + gain_part * (pre * inv_rms)).astype(bf16)
    pre_grad = (inv_rms * scaled - pre * inv_rms**3 * proj).astype(bf16)

    halves = []
    for pair in (0, 2):
        left = jnp.concatenate([features[pair], features[pair + 1]], axis=1)
        left = (left.astype(f32) * counted_flag).astype(bf16)
        term = lax.dot_general(left, pre_grad, (((0,), (0,)), ((), ())), preferred_element_type=f32)
        halves.append(term.astype(bf16).reshape(2, 2, 4, 4, 16, part_width))
    first = ring_sum(halves[0], "x")
    second_half = ring_sum(halves[1], "y")
    first = ring_sum(first, "y")
    second_half = ring_sum(second_half, "x")
    both = jnp.concatenate([first, second_half])
    gathered = []
    for k in range(4):
        mine = []
        for h in range(2):
            block = pick(both[k], zh ^ h)
            if h == 0 and k == 0:
                mine.append(block.astype(f32))
                continue
            moves = [
                (((i * 2 + j) * 2 + l), ((i ^ h) * 2 + (j ^ (k >> 1))) * 2 + (l ^ (k & 1)))
                for i in range(2)
                for j in range(2)
                for l in range(2)
            ]
            mine.append(lax.ppermute(block, ("zh", "zl", "c"), moves).astype(f32))
        gathered.append(mine[0] + mine[1])
    gathered = jnp.stack(gathered)
    owned_sum = jnp.concatenate([pick(gathered, place ^ j) for j in range(4)], axis=1)

    mean_grad = (owned_sum / counted.shape[0])[None, :, :]
    new_moment = beta_one * moment + (1.0 - beta_one) * mean_grad
    new_second = beta_two * second + (1.0 - beta_two) * mean_grad * mean_grad
    update = (
        new_moment
        / (1.0 - beta_one**step_number)
        / (jnp.sqrt(new_second / (1.0 - beta_two**step_number)) + adam_eps)
    )
    new_master = master - learn_rate * (update + weight_decay * master)

    own = new_master[0].astype(bf16)
    other = flip(own, "zh")
    rows = jnp.where(zh == 0, jnp.stack([own, other]), jnp.stack([other, own]))
    cut = full_width // 2
    parts = []
    for order, piece in ((("y", "x"), rows[:, :, :cut]), (("x", "y"), rows[:, :, cut:])):
        for axis in order:
            spot = lax.axis_index(axis)
            stacked = jnp.stack([piece] + [ring_step(piece, axis, s) for s in (1, 2, 3)])
            piece = jnp.stack([pick(stacked, (spot - j) % 4) for j in range(4)])
        parts.append(piece)
    left_cols = jnp.transpose(parts[0], (2, 1, 0, 3, 4))
    right_cols = jnp.transpose(parts[1], (2, 0, 1, 3, 4))
    new_proj = jnp.concatenate([left_cols, right_cols], axis=-1).reshape(heads, full_width)

    partial = [
        lax.dot_general(pre_grad, w, (((1,), (1,)), ((), ())), preferred_element_type=f32)
        for w in weights
    ]
    attn_grad = partial[0]
    for k in (1, 2, 3):
        attn_grad = attn_grad + flip_mp(partial[k].astype(bf16), k).astype(f32)
    return (layer_out, attn_grad.astype(bf16), new_proj, new_master, new_moment, new_second)


def solution(mesh):
    wide = Mesh(mesh.devices.reshape(2, 4, 4, 2, 2), axes)
    dp, mp = ("zh", "y", "x"), ("zl", "c")
    return jax.shard_map(
        local,
        mesh=wide,
        in_specs=(
            P(dp, mp),
            P(mp, None),
            P(),
            P(dp, mp),
            P(dp, mp),
            P(),
            P(mp, dp, None),
            P(mp, dp, None),
            P(mp, dp, None),
        ),
        out_specs=(
            P(dp, mp),
            P(dp, mp),
            P(mp, None),
            P(mp, dp, None),
            P(mp, dp, None),
            P(mp, dp, None),
        ),
        check_vma=False,
    )
```

time: 655 us -> 276 us (0.42)
  waiting for transfers between devices: 570 us -> 154 us
  starting transfers between devices: 0.34 us -> 42.7 us
  between operations: 13.8 us -> 1.3 us
  local copies, waits for them, and re-layouts: 16.6 us -> 28.4 us
  other arithmetic: 25.8 us -> 18 us
    reduce_scatter x1 -> x0, waiting for transfers between devices: 248 us -> none  [local(): lax.psum_scatter(grad_term, 'dp', scatter_dimension=0, tiled=True)]
    psum x1 -> x0, waiting for transfers between devices: 197 us -> none  [local(): summed = lax.psum(partial_value, 'mp')]
    ppermute x0 -> x43, waiting for transfers between devices: none -> 154 us  [the longest x24 99.3 us: ring_step(): lax.ppermute(value, axis, [(i, (i + step) % size) for i in range(size)])]
    all_gather x2 -> x0, waiting for transfers between devices: 124 us -> none  [the longest x1 74.7 us: local(): lax.all_gather(new_master[0].astype(jnp.bfloat16), 'dp', axis=0, tiled=True)]
    ppermute x0 -> x43, starting transfers between devices: none -> 42.7 us  [the longest x24 27.8 us: ring_step(): lax.ppermute(value, axis, [(i, (i + step) % size) for i in range(size)])]
    dynamic_slice x1 -> x10, local copies, waits for them, and re-layouts: 0.08 us -> 10.6 us  [the longest x9 9.81 us: pick(): return lax.dynamic_index_in_dim(stacked, index, axis, keepdims=False)]
    all_gather x1 -> x0, local copies, waits for them, and re-layouts: 8.26 us -> none  [local(): cot_full = lax.all_gather(cotangent, 'mp', axis=1, tiled=True)]
    reduce_sum x2 -> x1, other arithmetic: 8.53 us -> 0.6 us  [local(): counted_flag = jnp.sum((counted == replica).astype(f32))]
  transfers between devices with their start and end apart: 4 -> 43, of which waited for: 4 -> 21; matrix products, arithmetic and copies ran while one was open for 5% -> 16% of each run, Pallas kernels for 0% -> 0%
where the time goes in v1:
time: 276 us; the launch traced here: 273 us
  waiting for transfers between devices  154 us (56%)
  starting transfers between devices  42.7 us (15%)
  local copies, waits for them, and re-layouts  28.4 us (10%)
  matrix products  28.2 us (10%)
  other arithmetic  18 us (7%)
    ppermute x24, waiting for transfers between devices, ring_step(): lax.ppermute(value, axis, [(i, (i + step) % size) for i in range(size)])  99.3 us
    ppermute x7, waiting for transfers between devices, flip(): return lax.ppermute(value, axis, [(0, 1), (1, 0)])  45.8 us
    ppermute x24, starting transfers between devices, ring_step(): lax.ppermute(value, axis, [(i, (i + step) % size) for i in range(size)])  27.8 us
    dot_general x4, matrix products, local(): lax.dot_general(pre_grad, w, (((1,), (1,)), ((), ())), preferred_element_...  11.1 us
    dynamic_slice x9, local copies, waits for them, and re-layouts, pick(): return lax.dynamic_index_in_dim(stacked, index, axis, keepdims=False)  9.81 us
    ppermute x7, waiting for transfers between devices, local(): mine.append(lax.ppermute(block, ('zh', 'zl', 'c'), moves).astype(f32))  9.15 us
    dot_general x2, matrix products, local(): lax.dot_general(left, pre_grad, (((0,), (0,)), ((), ())), preferred_eleme...  8.7 us
    dot_general x4, matrix products, local(): pre = pre + jnp.dot(feature, weight, preferred_element_type=f32)  8.43 us
  transfers between devices with their start and end apart: 43, of which 21 were waited for; matrix products, arithmetic and copies ran while one was open for 16% of the time, Pallas kernels for 0%

profile of v1, /device:TPU:6, one launch (start us, length us, event | category | flops | bytes accessed | tf_op | source)
XLA Modules:
  0.0 272.8 jit_solution(5696102003491331835)
XLA Ops:
  0.7 4.3 %slice_bitcast_fusion.3 = (bf16[1,512,1344]{2,1,0:T(8,128)(2,1)S(1)}, bf16[1,512,1344]{2,1,0:T(8,128)(2,1)S(1)}, bf16[1,512,1344]{2,1,0:T(8,128)(2,1)S(1)}, bf16[1,512,1344]{2,1,0:T(8,128)(2,1)S(1)}) fusion(bf16[512,5376]{1,0:T(8,128)(2,1)} %param.10), kind=kLoop, calls=%fused_computation.34 | loop fusion | bytes 11010048 | tf_op jit(solution)/shard_map/stack | solution.py:57
  4.9 3.4 %pad_maximum_fusion = bf16[4,512,1344]{2,1,0:T(8,128)(2,1)} fusion(bf16[1,512,1344]{2,1,0:T(8,128)(2,1)S(1)} %get-tuple-element.17, bf16[1,512,1344]{2,1,0:T(8,128)(2,1)S(1)} %get-tuple-element.18, bf16[1,512,1344]{2,1,0:T(8,128)(2,1)S(1)} %get-tuple-element.16, bf16[1,512,1344]{2,1,0:T(8,128)(2,1)S(1)} %get-tuple-element.15), kind=kLoop, calls=%fused_computation | loop fusion | flops 8257536 | bytes 11010048 | tf_op jit(solution)/shard_map/stack | solution.py:57
  8.3 3.6 %constant_dynamic-slice_fusion.20 = (bf16[1,512,1344]{2,1,0:T(8,128)(2,1)S(1)}, bf16[1,512,1344]{2,1,0:T(8,128)(2,1)S(1)}, bf16[1,512,1344]{2,1,0:T(8,128)(2,1)}) fusion(bf16[4,512,1344]{2,1,0:T(8,128)(2,1)} %pad_maximum_fusion, s32[]{:T(128)S(6)} %select_n.202, s32[]{:T(128)S(6)} %select_n.201, s32[]{:T(128)S(6)} %select_n.200), kind=kLoop, calls=%fused_computation.111 | loop fusion | bytes 8257548 | tf_op jit(solution)/shard_map/jit(dynamic_index_in_dim)/dynamic_slice | solution.py:20
  25.5 37.8 %collective-permute-done.3 = bf16[512,512]{1,0:T(8,128)(2,1)S(1)} collective-permute-done((bf16[512,512]{1,0:T(8,128)(2,1)}, bf16[512,512]{1,0:T(8,128)(2,1)S(1)}, u32[]{:S(2)}, u32[]{:S(2)}) %collective-permute-start.3) | collective-permute-done | bytes 524320 | tf_op jit(solution)/shard_map/ppermute | solution.py:29
  71.9 3.4 %collective-permute-done.7 = f32[2,512]{1,0:T(2,128)S(1)} collective-permute-done((f32[2,512]{1,0:T(2,128)S(1)}, f32[2,512]{1,0:T(2,128)S(1)}, u32[]{:S(2)}, u32[]{:S(2)}) %collective-permute-start.7) | collective-permute-done | bytes 4128 | tf_op jit(solution)/shard_map/ppermute | solution.py:29
  75.3 3.9 %subtract_convert_fusion = (bf16[512,1344]{0,1:T(8,128)(2,1)S(1)}, bf16[512,1344]{0,1:T(8,128)(2,1)}) fusion(f32[512,1344]{0,1:T(8,128)S(1)} %get-tuple-element.73, bf16[512,1344]{0,1:T(8,128)(2,1)} %param.13, f32[512]{0:T(512)S(1)} %bitcast.164, f32[512]{0:T(512)S(1)} %multiply_multiply_fusion, f32[512]{0:T(512)S(1)} %bitcast.163, ...), kind=kLoop, calls=%fused_computation.12 | loop fusion | flops 8257536 | bytes 8269056 | tf_op jit(solution)/shard_map/convert_element_type | solution.py:85
  79.2 3.7 %convolution_convert_fusion.2 = bf16[512,512]{1,0:T(8,128)(2,1)} fusion(bf16[512,1344]{0,1:T(8,128)(2,1)S(1)} %get-tuple-element.25, bf16[512,1344]{0,1:T(8,128)(2,1)} %collective-permute-done.4), kind=kOutput, calls=%fused_computation.35 | convolution fusion | flops 704905216 | bytes 3276800 | tf_op jit(solution)/shard_map/dot_general | solution.py:143
  85.5 3.8 %convolution_convert_fusion = bf16[1024,1344]{0,1:T(8,128)(2,1)} fusion(bf16[512,1344]{0,1:T(8,128)(2,1)S(1)} %get-tuple-element.25, bf16[512,512]{1,0:T(8,128)(2,1)S(1)} %copy-done.11, bf16[512,512]{1,0:T(8,128)(2,1)S(1)} %copy-done.9, f32[]{:T(128)} %fusion.32), kind=kOutput, calls=%fused_computation.2 | convolution fusion | flops 1413808128 | bytes 5177348 | tf_op jit(solution)/shard_map/dot_general | solution.py:91
  89.4 3.3 %copy.36 = bf16[1024,1344]{1,0:T(8,128)(2,1)S(1)} copy(bf16[1024,1344]{0,1:T(8,128)(2,1)} %convolution_convert_fusion) | data formatting | bytes 5505024 | tf_op jit(solution)/shard_map/convert_element_type | solution.py:92
  99.3 4.9 %convolution_convert_fusion.1 = bf16[1024,1344]{0,1:T(8,128)(2,1)} fusion(bf16[512,1344]{0,1:T(8,128)(2,1)S(1)} %copy-done.5, bf16[512,512]{1,0:T(8,128)(2,1)S(1)} %collective-permute-done.1, bf16[512,512]{1,0:T(8,128)(2,1)} %param.9, f32[]{:T(128)} %fusion.32), kind=kOutput, calls=%fused_computation.3 | convolution fusion | flops 1413808128 | bytes 5177348 | tf_op jit(solution)/shard_map/dot_general | solution.py:91
  104.2 3.3 %copy.35 = bf16[1024,1344]{1,0:T(8,128)(2,1)S(1)} copy(bf16[1024,1344]{0,1:T(8,128)(2,1)} %convolution_convert_fusion.1) | data formatting | bytes 5505024 | tf_op jit(solution)/shard_map/convert_element_type | solution.py:92
  108.8 3.1 %convolution_convert_fusion.4 = bf16[512,512]{1,0:T(8,128)(2,1)} fusion(bf16[512,1344]{0,1:T(8,128)(2,1)S(1)} %copy-done.6, bf16[512,1344]{0,1:T(8,128)(2,1)} %collective-permute-done), kind=kOutput, calls=%fused_computation.37 | convolution fusion | flops 704905216 | bytes 3276800 | tf_op jit(solution)/shard_map/dot_general | solution.py:143
  112.0 17.2 %collective-permute-done.22 = bf16[2,2,4,16,1344]{4,3,2,1,0:T(8,128)(2,1)} collective-permute-done((bf16[2,2,4,16,1344]{4,3,2,1,0:T(8,128)(2,1)}, bf16[2,2,4,16,1344]{4,3,2,1,0:T(8,128)(2,1)}, u32[]{:S(2)}, u32[]{:S(2)}) %collective-permute-start.22) | collective-permute-done | bytes 688160 | tf_op jit(solution)/shard_map/ppermute | solution.py:25
  138.0 26.2 %collective-permute-done.13 = bf16[2,2,4,16,1344]{4,3,2,1,0:T(8,128)(2,1)S(1)} collective-permute-done((bf16[2,2,4,16,1344]{4,3,2,1,0:T(8,128)(2,1)S(1)}, bf16[2,2,4,16,1344]{4,3,2,1,0:T(8,128)(2,1)S(1)}, u32[]{:S(2)}, u32[]{:S(2)}) %collective-permute-start.13) | collective-permute-done | bytes 688160 | tf_op jit(solution)/shard_map/ppermute | solution.py:25
  164.2 3.2 %collective-permute-start.24 = (bf16[2,2,16,1344]{3,2,1,0:T(8,128)(2,1)S(1)}, bf16[2,2,16,1344]{3,2,1,0:T(8,128)(2,1)S(1)}, u32[]{:S(2)}, u32[]{:S(2)}) collective-permute-start(bf16[2,2,16,1344]{3,2,1,0:T(8,128)(2,1)S(1)} %get-tuple-element.40), channel_id=1, source_target_pairs={{0,4},{4,8},{8,12},{12,0},{1,5},{5,9},{9,13},{13,1},{2,6},{6,10},{... | collective-permute-start | bytes 516104 | tf_op jit(solution)/shard_map/ppermute | solution.py:25
  167.9 7.4 %collective-permute-done.25 = bf16[2,2,16,1344]{3,2,1,0:T(8,128)(2,1)S(1)} collective-permute-done((bf16[2,2,16,1344]{3,2,1,0:T(8,128)(2,1)S(1)}, bf16[2,2,16,1344]{3,2,1,0:T(8,128)(2,1)S(1)}, u32[]{:S(2)}, u32[]{:S(2)}) %collective-permute-start.25) | collective-permute-done | bytes 172064 | tf_op jit(solution)/shard_map/ppermute | solution.py:25
  181.4 5.6 %collective-permute-done.15 = bf16[2,2,16,1344]{3,2,1,0:T(8,128)(2,1)S(1)} collective-permute-done((bf16[2,2,16,1344]{3,2,1,0:T(8,128)(2,1)S(1)}, bf16[2,2,16,1344]{3,2,1,0:T(8,128)(2,1)S(1)}, u32[]{:S(2)}, u32[]{:S(2)}) %collective-permute-start.15) | collective-permute-done | bytes 172064 | tf_op jit(solution)/shard_map/ppermute | solution.py:25
  187.0 3.5 %collective-permute-start.28 = (bf16[16,1344]{1,0:T(8,128)(2,1)S(1)}, bf16[16,1344]{1,0:T(8,128)(2,1)S(1)}, u32[]{:S(2)}, u32[]{:S(2)}) collective-permute-start(bf16[16,1344]{1,0:T(8,128)(2,1)S(1)} %get-tuple-element.69), channel_id=1, source_target_pairs={{0,3},{1,2},{2,1},{3,0},{64,67},{65,66},{66,65},{67,64},{4,7},{5,6... | collective-permute-start | bytes 129032 | tf_op jit(solution)/shard_map/ppermute | solution.py:112
  198.4 4.1 %collective-permute-done.17 = bf16[16,1344]{1,0:T(8,128)(2,1)S(1)} collective-permute-done((bf16[16,1344]{1,0:T(8,128)(2,1)S(1)}, bf16[16,1344]{1,0:T(8,128)(2,1)S(1)}, u32[]{:S(2)}, u32[]{:S(2)}) %collective-permute-start.17) | collective-permute-done | bytes 43040 | tf_op jit(solution)/shard_map/ppermute | solution.py:112
  210.6 3.6 %collective-permute-done.30 = bf16[16,5376]{1,0:T(8,128)(2,1)S(1)} collective-permute-done((bf16[16,5376]{1,0:T(8,128)(2,1)S(1)}, bf16[16,5376]{1,0:T(8,128)(2,1)S(1)}, u32[]{:S(2)}, u32[]{:S(2)}) %collective-permute-start.30) | collective-permute-done | bytes 172064 | tf_op jit(solution)/shard_map/ppermute | solution.py:29
  220.6 4.5 %collective-permute-done.39 = bf16[2,16,2688]{2,1,0:T(8,128)(2,1)S(1)} collective-permute-done((bf16[2,16,2688]{2,1,0:T(8,128)(2,1)S(1)}, bf16[2,16,2688]{2,1,0:T(8,128)(2,1)S(1)}, u32[]{:S(2)}, u32[]{:S(2)}) %collective-permute-start.39) | collective-permute-done | bytes 172064 | tf_op jit(solution)/shard_map/ppermute | solution.py:25
  229.7 17.2 %collective-permute-done.31 = bf16[2,16,2688]{2,1,0:T(8,128)(2,1)S(1)} collective-permute-done((bf16[2,16,2688]{2,1,0:T(8,128)(2,1)S(1)}, bf16[2,16,2688]{2,1,0:T(8,128)(2,1)S(1)}, u32[]{:S(2)}, u32[]{:S(2)}) %collective-permute-start.31) | collective-permute-done | bytes 172064 | tf_op jit(solution)/shard_map/ppermute | solution.py:25
  250.8 9.8 %collective-permute-done.40 = bf16[4,2,16,2688]{3,2,1,0:T(8,128)(2,1)S(1)} collective-permute-done((bf16[4,2,16,2688]{3,2,1,0:T(8,128)(2,1)S(1)}, bf16[4,2,16,2688]{3,2,1,0:T(8,128)(2,1)S(1)}, u32[]{:S(2)}, u32[]{:S(2)}) %collective-permute-start.40) | collective-permute-done | bytes 688160 | tf_op jit(solution)/shard_map/ppermute | solution.py:25
  261.2 5.7 %collective-permute-done.36 = bf16[4,2,16,2688]{3,2,1,0:T(8,128)(2,1)S(1)} collective-permute-done((bf16[4,2,16,2688]{3,2,1,0:T(8,128)(2,1)S(1)}, bf16[4,2,16,2688]{3,2,1,0:T(8,128)(2,1)S(1)}, u32[]{:S(2)}, u32[]{:S(2)}) %collective-permute-start.36) | collective-permute-done | bytes 688160 | tf_op jit(solution)/shard_map/ppermute | solution.py:25
  (157 shorter events, 85.0 us)
Async XLA Ops:
  14.4 49.0 %collective-permute-start = (bf16[512,1344]{0,1:T(8,128)(2,1)}, bf16[512,1344]{0,1:T(8,128)(2,1)}, u32[]{:S(2)}, u32[]{:S(2)}) collective-permute-start(bf16[512,1344]{0,1:T(8,128)(2,1)} %bitcast.140), channel_id=1, source_target_pairs={{0,1},{1,0},{2,3},{3,2},{4,5},{5,4},{6,7},{7,6},{8,9},{9,8},{10,11... | collective-permute-start | bytes 4128776 | tf_op jit(solution)/shard_map/ppermute | solution.py:29
  15.9 50.0 %collective-permute-start.2 = (bf16[512,1344]{0,1:T(8,128)(2,1)}, bf16[512,1344]{0,1:T(8,128)(2,1)S(1)}, u32[]{:S(2)}, u32[]{:S(2)}) collective-permute-start(bf16[512,1344]{0,1:T(8,128)(2,1)} %bitcast.141), channel_id=1, source_target_pairs={{0,2},{2,64},{64,66},{66,0},{1,3},{3,65},{65,67},{67,1},{4,6},{6,6... | collective-permute-start | bytes 4128776 | tf_op jit(solution)/shard_map/ppermute | solution.py:62
  19.5 47.6 %collective-permute-start.4 = (bf16[512,1344]{0,1:T(8,128)(2,1)}, bf16[512,1344]{0,1:T(8,128)(2,1)}, u32[]{:S(2)}, u32[]{:S(2)}) collective-permute-start(bf16[512,1344]{0,1:T(8,128)(2,1)} %bitcast.139), channel_id=1, source_target_pairs={{0,67},{1,66},{2,1},{3,0},{64,3},{65,2},{66,65},{67,64},{4,71},{5,... | collective-permute-start | bytes 4128776 | tf_op jit(solution)/shard_map/ppermute | solution.py:65
  21.7 41.7 %collective-permute-start.3 = (bf16[512,512]{1,0:T(8,128)(2,1)}, bf16[512,512]{1,0:T(8,128)(2,1)S(1)}, u32[]{:S(2)}, u32[]{:S(2)}) collective-permute-start(bf16[512,512]{1,0:T(8,128)(2,1)} %param.9), channel_id=1, source_target_pairs={{0,2},{2,0},{1,3},{3,1},{4,6},{6,4},{5,7},{7,5},{8,10},{10,8},{9,1... | collective-permute-start | bytes 1572872 | tf_op jit(solution)/shard_map/ppermute | solution.py:29
  21.7 41.7 %collective-permute-start.1 = (bf16[512,512]{1,0:T(8,128)(2,1)}, bf16[512,512]{1,0:T(8,128)(2,1)S(1)}, u32[]{:S(2)}, u32[]{:S(2)}) collective-permute-start(bf16[512,512]{1,0:T(8,128)(2,1)} %param.9), channel_id=1, source_target_pairs={{0,1},{1,0},{2,3},{3,2},{4,5},{5,4},{6,7},{7,6},{8,9},{9,8},{10,11... | collective-permute-start | bytes 1572872 | tf_op jit(solution)/shard_map/ppermute | solution.py:29
  82.9 133.9 %collective-permute-start.10 = (bf16[512,512]{1,0:T(8,128)(2,1)}, bf16[512,512]{1,0:T(8,128)(2,1)}, u32[]{:S(2)}, u32[]{:S(2)}) collective-permute-start(bf16[512,512]{1,0:T(8,128)(2,1)} %convolution_convert_fusion.2), channel_id=1, source_target_pairs={{0,3},{1,2},{2,1},{3,0},{4,7},{5,6},{6,5},{7,4},{8,11},{9,10},{10,... | collective-permute-start | bytes 1572872 | tf_op jit(solution)/shard_map/ppermute | solution.py:33
  84.7 132.9 %collective-permute-start.9 = (bf16[512,512]{1,0:T(8,128)(2,1)}, bf16[512,512]{1,0:T(8,128)(2,1)}, u32[]{:S(2)}, u32[]{:S(2)}) collective-permute-start(bf16[512,512]{1,0:T(8,128)(2,1)} %convolution_convert_fusion.3), channel_id=1, source_target_pairs={{0,2},{1,3},{2,0},{3,1},{4,6},{5,7},{6,4},{7,5},{8,10},{9,11},{10,... | collective-permute-start | bytes 1572872 | tf_op jit(solution)/shard_map/ppermute | solution.py:33
  94.1 35.1 %collective-permute-start.22 = (bf16[2,2,4,16,1344]{4,3,2,1,0:T(8,128)(2,1)}, bf16[2,2,4,16,1344]{4,3,2,1,0:T(8,128)(2,1)}, u32[]{:S(2)}, u32[]{:S(2)}) collective-permute-start(bf16[2,2,4,16,1344]{4,3,2,1,0:T(8,128)(2,1)} %get-tuple-element.23), channel_id=1, source_target_pairs={{0,48},{16,0},{32,16},{48,32},{1,49},{17,1},{33,17},{49,33},{2,50}... | collective-permute-start | bytes 2064392 | tf_op jit(solution)/shard_map/ppermute | solution.py:25
  97.1 35.8 %collective-permute-start.21 = (bf16[2,2,4,16,1344]{4,3,2,1,0:T(8,128)(2,1)}, bf16[2,2,4,16,1344]{4,3,2,1,0:T(8,128)(2,1)}, u32[]{:S(2)}, u32[]{:S(2)}) collective-permute-start(bf16[2,2,4,16,1344]{4,3,2,1,0:T(8,128)(2,1)} %get-tuple-element.24), channel_id=1, source_target_pairs={{0,16},{16,32},{32,48},{48,0},{1,17},{17,33},{33,49},{49,1},{2,18}... | collective-permute-start | bytes 2064392 | tf_op jit(solution)/shard_map/ppermute | solution.py:25
  97.1 36.3 %collective-permute-start.20 = (bf16[2,2,4,16,1344]{4,3,2,1,0:T(8,128)(2,1)}, bf16[2,2,4,16,1344]{4,3,2,1,0:T(8,128)(2,1)}, u32[]{:S(2)}, u32[]{:S(2)}) collective-permute-start(bf16[2,2,4,16,1344]{4,3,2,1,0:T(8,128)(2,1)} %get-tuple-element.22), channel_id=1, source_target_pairs={{0,32},{16,48},{32,0},{48,16},{1,33},{17,49},{33,1},{49,17},{2,34}... | collective-permute-start | bytes 2064392 | tf_op jit(solution)/shard_map/ppermute | solution.py:25
  129.1 35.1 %collective-permute-start.13 = (bf16[2,2,4,16,1344]{4,3,2,1,0:T(8,128)(2,1)S(1)}, bf16[2,2,4,16,1344]{4,3,2,1,0:T(8,128)(2,1)S(1)}, u32[]{:S(2)}, u32[]{:S(2)}) collective-permute-start(bf16[2,2,4,16,1344]{4,3,2,1,0:T(8,128)(2,1)S(1)} %get-tuple-element.20), channel_id=1, source_target_pairs={{0,12},{4,0},{8,4},{12,8},{1,13},{5,1},{9,5},{13,9},{2,14},{6,2},{... | collective-permute-start | bytes 2064392 | tf_op jit(solution)/shard_map/ppermute | solution.py:25
  132.9 31.3 %collective-permute-start.12 = (bf16[2,2,4,16,1344]{4,3,2,1,0:T(8,128)(2,1)S(1)}, bf16[2,2,4,16,1344]{4,3,2,1,0:T(8,128)(2,1)S(1)}, u32[]{:S(2)}, u32[]{:S(2)}) collective-permute-start(bf16[2,2,4,16,1344]{4,3,2,1,0:T(8,128)(2,1)S(1)} %get-tuple-element.21), channel_id=1, source_target_pairs={{0,4},{4,8},{8,12},{12,0},{1,5},{5,9},{9,13},{13,1},{2,6},{6,10},{... | collective-permute-start | bytes 2064392 | tf_op jit(solution)/shard_map/ppermute | solution.py:25
  133.4 34.1 %collective-permute-start.11 = (bf16[2,2,4,16,1344]{4,3,2,1,0:T(8,128)(2,1)S(1)}, bf16[2,2,4,16,1344]{4,3,2,1,0:T(8,128)(2,1)S(1)}, u32[]{:S(2)}, u32[]{:S(2)}) collective-permute-start(bf16[2,2,4,16,1344]{4,3,2,1,0:T(8,128)(2,1)S(1)} %get-tuple-element.19), channel_id=1, source_target_pairs={{0,8},{4,12},{8,0},{12,4},{1,9},{5,13},{9,1},{13,5},{2,10},{6,14},... | collective-permute-start | bytes 2064392 | tf_op jit(solution)/shard_map/ppermute | solution.py:25
  164.2 11.1 %collective-permute-start.25 = (bf16[2,2,16,1344]{3,2,1,0:T(8,128)(2,1)S(1)}, bf16[2,2,16,1344]{3,2,1,0:T(8,128)(2,1)S(1)}, u32[]{:S(2)}, u32[]{:S(2)}) collective-permute-start(bf16[2,2,16,1344]{3,2,1,0:T(8,128)(2,1)S(1)} %get-tuple-element.39), channel_id=1, source_target_pairs={{0,12},{4,0},{8,4},{12,8},{1,13},{5,1},{9,5},{13,9},{2,14},{6,2},{... | collective-permute-start | bytes 516104 | tf_op jit(solution)/shard_map/ppermute | solution.py:25
  164.2 14.2 %collective-permute-start.24 = (bf16[2,2,16,1344]{3,2,1,0:T(8,128)(2,1)S(1)}, bf16[2,2,16,1344]{3,2,1,0:T(8,128)(2,1)S(1)}, u32[]{:S(2)}, u32[]{:S(2)}) collective-permute-start(bf16[2,2,16,1344]{3,2,1,0:T(8,128)(2,1)S(1)} %get-tuple-element.40), channel_id=1, source_target_pairs={{0,4},{4,8},{8,12},{12,0},{1,5},{5,9},{9,13},{13,1},{2,6},{6,10},{... | collective-permute-start | bytes 516104 | tf_op jit(solution)/shard_map/ppermute | solution.py:25
  167.5 10.9 %collective-permute-start.23 = (bf16[2,2,16,1344]{3,2,1,0:T(8,128)(2,1)S(1)}, bf16[2,2,16,1344]{3,2,1,0:T(8,128)(2,1)S(1)}, u32[]{:S(2)}, u32[]{:S(2)}) collective-permute-start(bf16[2,2,16,1344]{3,2,1,0:T(8,128)(2,1)S(1)} %get-tuple-element.38), channel_id=1, source_target_pairs={{0,8},{4,12},{8,0},{12,4},{1,9},{5,13},{9,1},{13,5},{2,10},{6,14},... | collective-permute-start | bytes 516104 | tf_op jit(solution)/shard_map/ppermute | solution.py:25
  181.4 36.3 %collective-permute-start.8 = (bf16[512,512]{1,0:T(8,128)(2,1)}, bf16[512,512]{1,0:T(8,128)(2,1)S(1)}, u32[]{:S(2)}, u32[]{:S(2)}) collective-permute-start(bf16[512,512]{1,0:T(8,128)(2,1)} %convolution_convert_fusion.4), channel_id=1, source_target_pairs={{0,1},{1,0},{2,3},{3,2},{4,5},{5,4},{6,7},{7,6},{8,9},{9,8},{10,11... | collective-permute-start | bytes 1572872 | tf_op jit(solution)/shard_map/ppermute | solution.py:33
  225.2 21.8 %collective-permute-start.31 = (bf16[2,16,2688]{2,1,0:T(8,128)(2,1)S(1)}, bf16[2,16,2688]{2,1,0:T(8,128)(2,1)S(1)}, u32[]{:S(2)}, u32[]{:S(2)}) collective-permute-start(bf16[2,16,2688]{2,1,0:T(8,128)(2,1)S(1)} %get-tuple-element.60), channel_id=1, source_target_pairs={{0,16},{16,32},{32,48},{48,0},{1,17},{17,33},{33,49},{49,1},{2,18}... | collective-permute-start | bytes 516104 | tf_op jit(solution)/shard_map/ppermute | solution.py:25
  226.1 22.1 %collective-permute-start.42 = (bf16[4,2,16,2688]{3,2,1,0:T(8,128)(2,1)S(1)}, bf16[4,2,16,2688]{3,2,1,0:T(8,128)(2,1)S(1)}, u32[]{:S(2)}, u32[]{:S(2)}) collective-permute-start(bf16[4,2,16,2688]{3,2,1,0:T(8,128)(2,1)S(1)} %get-tuple-element.48), channel_id=1, source_target_pairs={{0,48},{16,0},{32,16},{48,32},{1,49},{17,1},{33,17},{49,33},{2,50}... | collective-permute-start | bytes 2064392 | tf_op jit(solution)/shard_map/ppermute | solution.py:25
  228.8 22.0 %collective-permute-start.41 = (bf16[4,2,16,2688]{3,2,1,0:T(8,128)(2,1)S(1)}, bf16[4,2,16,2688]{3,2,1,0:T(8,128)(2,1)S(1)}, u32[]{:S(2)}, u32[]{:S(2)}) collective-permute-start(bf16[4,2,16,2688]{3,2,1,0:T(8,128)(2,1)S(1)} %get-tuple-element.48), channel_id=1, source_target_pairs={{0,32},{16,48},{32,0},{48,16},{1,33},{17,49},{33,1},{49,17},{2,34}... | collective-permute-start | bytes 2064392 | tf_op jit(solution)/shard_map/ppermute | solution.py:25
  228.8 31.7 %collective-permute-start.40 = (bf16[4,2,16,2688]{3,2,1,0:T(8,128)(2,1)S(1)}, bf16[4,2,16,2688]{3,2,1,0:T(8,128)(2,1)S(1)}, u32[]{:S(2)}, u32[]{:S(2)}) collective-permute-start(bf16[4,2,16,2688]{3,2,1,0:T(8,128)(2,1)S(1)} %get-tuple-element.48), channel_id=1, source_target_pairs={{0,16},{16,32},{32,48},{48,0},{1,17},{17,33},{33,49},{49,1},{2,18}... | collective-permute-start | bytes 2064392 | tf_op jit(solution)/shard_map/ppermute | solution.py:25
  247.2 19.6 %collective-permute-start.36 = (bf16[4,2,16,2688]{3,2,1,0:T(8,128)(2,1)S(1)}, bf16[4,2,16,2688]{3,2,1,0:T(8,128)(2,1)S(1)}, u32[]{:S(2)}, u32[]{:S(2)}) collective-permute-start(bf16[4,2,16,2688]{3,2,1,0:T(8,128)(2,1)S(1)} %get-tuple-element.42), channel_id=1, source_target_pairs={{0,12},{4,0},{8,4},{12,8},{1,13},{5,1},{9,5},{13,9},{2,14},{6,2},{... | collective-permute-start | bytes 2064392 | tf_op jit(solution)/shard_map/ppermute | solution.py:25
  247.3 19.5 %collective-permute-start.35 = (bf16[4,2,16,2688]{3,2,1,0:T(8,128)(2,1)S(1)}, bf16[4,2,16,2688]{3,2,1,0:T(8,128)(2,1)S(1)}, u32[]{:S(2)}, u32[]{:S(2)}) collective-permute-start(bf16[4,2,16,2688]{3,2,1,0:T(8,128)(2,1)S(1)} %get-tuple-element.42), channel_id=1, source_target_pairs={{0,8},{4,12},{8,0},{12,4},{1,9},{5,13},{9,1},{13,5},{2,10},{6,14},... | collective-permute-start | bytes 2064392 | tf_op jit(solution)/shard_map/ppermute | solution.py:25
  248.2 19.5 %collective-permute-start.34 = (bf16[4,2,16,2688]{3,2,1,0:T(8,128)(2,1)S(1)}, bf16[4,2,16,2688]{3,2,1,0:T(8,128)(2,1)S(1)}, u32[]{:S(2)}, u32[]{:S(2)}) collective-permute-start(bf16[4,2,16,2688]{3,2,1,0:T(8,128)(2,1)S(1)} %get-tuple-element.42), channel_id=1, source_target_pairs={{0,4},{4,8},{8,12},{12,0},{1,5},{5,9},{9,13},{13,1},{2,6},{6,10},{... | collective-permute-start | bytes 2064392 | tf_op jit(solution)/shard_map/ppermute | solution.py:25
  (34 other events, 233.5 us)

commit v2 on v0

v2 whole, which is shorter than its diff:
```python
import jax
import jax.numpy as jnp
from jax import lax
from jax.experimental import pallas as pl
from jax.experimental.pallas import tpu as pltpu
from jax.sharding import Mesh, PartitionSpec as P

norm_eps = 1e-06
beta_one = 0.9
beta_two = 0.999
adam_eps = 1e-08
learn_rate = 0.01
weight_decay = 0.1
step_number = 100.0

axes = ("zh", "y", "x", "zl", "c")
sizes = (2, 4, 4, 2, 2)
bf16 = jnp.bfloat16
f32 = jnp.float32

places = [
    (zh, y, x, zl, c)
    for zh in range(2)
    for y in range(4)
    for x in range(4)
    for zl in range(2)
    for c in range(2)
]


def move(value, target):
    def flat(place):
        index = 0
        for size, at in zip(sizes, place):
            index = index * size + at % size
        return index

    return lax.ppermute(value, axes, [(flat(p), flat(target(*p))) for p in places])


def along_first(value, step):
    return move(
        value,
        lambda zh, y, x, zl, c: (zh, y, x + step, zl, c) if c == 0 else (zh, y + step, x, zl, c),
    )


def along_second(value, step):
    return move(
        value,
        lambda zh, y, x, zl, c: (zh, y + step, x, zl, c) if c == 0 else (zh, y, x + step, zl, c),
    )


def flip_core(value):
    return move(value, lambda zh, y, x, zl, c: (zh, y, x, zl, 1 - c))


def flip_z(value, low, high):
    return move(value, lambda zh, y, x, zl, c: (zh ^ high, y, x, zl ^ low, c))


def gradient_kernel(rows_ref, left_ref, own_ref, peer_ref, *rest):
    outs, (both, sent, sems) = rest[:4], rest[4:]
    step = pl.program_id(0)
    part = own_ref.shape[0]
    width = outs[0].shape[-1]

    @pl.when(step == 0)
    def _():
        core = rows_ref[64]
        first = pltpu.make_async_copy(
            own_ref, both.at[pl.ds(pl.multiple_of(core * part, 64), part)], sems.at[0]
        )
        second = pltpu.make_async_copy(
            peer_ref, both.at[pl.ds(pl.multiple_of((1 - core) * part, 64), part)], sems.at[1]
        )
        first.start()
        second.start()
        for k in range(64):
            row = pl.multiple_of(rows_ref[k], 16)
            sent[pl.ds(16 * k, 16), :] = left_ref[pl.ds(row, 16), :]
        first.wait()
        second.wait()

    block = both[pl.ds(pl.multiple_of(step * width, width), width), :]
    for s in range(4):
        term = lax.dot_general(
            sent[pl.ds(256 * s, 256), :],
            block,
            (((1,), (1,)), ((), ())),
            preferred_element_type=f32,
        )
        outs[s][...] = term.astype(bf16).reshape(16, 16, width)


def gradient_pieces(rows, left, own, peer):
    heads, tokens = left.shape
    part = own.shape[0]
    width = 384
    columns = 2 * part
    return pl.pallas_call(
        gradient_kernel,
        grid_spec=pltpu.PrefetchScalarGridSpec(
            num_scalar_prefetch=1,
            grid=(columns // width,),
            in_specs=[
                pl.BlockSpec((heads, tokens), lambda i, rows: (0, 0)),
                pl.BlockSpec(memory_space=pl.ANY),
                pl.BlockSpec(memory_space=pl.ANY),
            ],
            out_specs=[pl.BlockSpec((16, 16, width), lambda i, rows: (0, 0, i))] * 4,
            scratch_shapes=[
                pltpu.VMEM((columns, tokens), bf16),
                pltpu.VMEM((heads, tokens), bf16),
                pltpu.SemaphoreType.DMA((2,)),
            ],
        ),
        out_shape=[jax.ShapeDtypeStruct((16, 16, columns), bf16)] * 4,
        compiler_params=pltpu.CompilerParams(vmem_limit_bytes=32 * 1024 * 1024),
        cost_estimate=pl.CostEstimate(
            flops=2 * heads * tokens * columns, bytes_accessed=10_000_000, transcendentals=0
        ),
    )(rows, left, own, peer)


def join_kernel(*refs):
    *pieces, ready_ref, out_ref = refs
    size = pieces[0].shape[0]
    for t, piece in enumerate(pieces):
        out_ref[size * t : size * (t + 1)] = piece[...]


def join(pieces, ready):
    size, rows, width = pieces[0].shape
    vmem = pl.BlockSpec(memory_space=pltpu.VMEM)
    return pl.pallas_call(
        join_kernel,
        in_specs=[vmem] * (len(pieces) + 1),
        out_specs=vmem,
        out_shape=jax.ShapeDtypeStruct((len(pieces) * size, rows, width), bf16),
        compiler_params=pltpu.CompilerParams(vmem_limit_bytes=16 * 1024 * 1024),
        cost_estimate=pl.CostEstimate(flops=0, bytes_accessed=2_800_000, transcendentals=0),
    )(*pieces, ready)


def place_kernel(rows_ref, *refs):
    pieces, out_ref, sems = refs[:4], refs[4], refs[5]
    copies = [
        pltpu.make_async_copy(
            pieces[s].at[k],
            out_ref.at[pl.ds(pl.multiple_of(rows_ref[s * 8 + k], 16), 16)],
            sems.at[s * 8 + k],
        )
        for s in range(4)
        for k in range(8)
    ]
    for copy in copies:
        copy.start()
    for copy in copies:
        copy.wait()


def place_rows(rows, pieces):
    width = pieces[0].shape[-1]
    return pl.pallas_call(
        place_kernel,
        grid_spec=pltpu.PrefetchScalarGridSpec(
            num_scalar_prefetch=1,
            grid=(1,),
            in_specs=[pl.BlockSpec(memory_space=pltpu.VMEM)] * 4,
            out_specs=pl.BlockSpec(memory_space=pl.ANY),
            scratch_shapes=[pltpu.SemaphoreType.DMA((32,))],
        ),
        compiler_params=pltpu.CompilerParams(vmem_limit_bytes=24 * 1024 * 1024),
        out_shape=jax.ShapeDtypeStruct((512, width), bf16),
        cost_estimate=pl.CostEstimate(flops=0, bytes_accessed=11_000_000, transcendentals=0),
    )(rows, *pieces)


def local(attention, out_proj, post_gain, residual, cotangent, counted, master, moment, second):
    zh, y, x, zl, c = (lax.axis_index(a) for a in axes)
    replica = (zh * 4 + y) * 4 + x
    tokens, part = residual.shape
    heads = attention.shape[1]
    full_width = post_gain.shape[0]
    half = full_width // 2
    gain = lax.dynamic_slice_in_dim(post_gain, (zl * 2 + c) * part, part, 0)[:, None]
    counted_flag = jnp.sum((counted == replica).astype(f32))
    spot = jnp.where(c == 0, x, y)
    spot_second = jnp.where(c == 0, y, x)

    near = jnp.where(zl == 0, out_proj[:, :half], out_proj[:, half:])
    share, shared = 80, 320
    shares = lax.dynamic_slice_in_dim(out_proj, spot * share, share, 0)
    received = flip_z(jnp.where(zl == 0, shares[:, half:], shares[:, :half]), 1, 0)
    rest = out_proj[shared:]
    direct = flip_z(jnp.where(zl == 0, rest[:, half:], rest[:, :half]), 1, 1)
    far_attention = flip_z(attention, 1, 0)
    rel = jnp.stack([received] + [along_first(received, s) for s in (1, 2, 3)])
    far = jnp.concatenate(
        [lax.dynamic_index_in_dim(rel, (spot - j) % 4, 0, keepdims=False) for j in range(4)]
        + [direct]
    )

    left_rows = (((0,), (1,)), ((), ()))
    pre_pair = lax.dot_general(near, attention, left_rows, preferred_element_type=f32)
    pre_pair = pre_pair + lax.dot_general(far, far_attention, left_rows, preferred_element_type=f32)
    mine = lax.dynamic_slice_in_dim(pre_pair, c * part, part, 0)
    other = lax.dynamic_slice_in_dim(pre_pair, (1 - c) * part, part, 0)
    pre = mine + flip_core(other.astype(bf16)).astype(f32)

    scaled = cotangent.T.astype(f32) * gain
    stats = jnp.stack([jnp.sum(pre * pre, axis=0), jnp.sum(scaled * pre, axis=0)])
    stats = stats + flip_core(stats)
    stats = stats + flip_z(stats, 1, 0)
    inv_rms = lax.rsqrt(stats[0] / full_width + norm_eps)[None, :]
    proj = (stats[1] / full_width)[None, :]
    layer_out = (residual.T.astype(f32) + gain * (pre * inv_rms)).astype(bf16).T
    pre_grad = (inv_rms * scaled - pre * inv_rms**3 * proj).astype(bf16)
    peer_grad = flip_core(pre_grad)

    left = jnp.concatenate([attention, far_attention], axis=1)
    left = (left.astype(f32) * counted_flag).astype(bf16).T
    left = lax.optimization_barrier(left)
    s_, t_, slot_, dz_ = jnp.meshgrid(*(jnp.arange(n) for n in (4, 4, 2, 2)), indexing="ij")
    first_at = (spot + s_) % 4
    second_at = (spot_second + t_) % 4
    x_at = jnp.where(c == 0, first_at, second_at)
    y_at = jnp.where(c == 0, second_at, first_at)
    rows = slot_ * 512 + (((zh ^ dz_) * 4 + y_at) * 4 + x_at) * 16
    rows = jnp.concatenate([rows.reshape(64), c[None]]).astype(jnp.int32)
    pieces = gradient_pieces(rows, left, pre_grad, peer_grad)
    got = [along_first(pieces[s], s) for s in (2, 1, 3)]
    total = pieces[0].astype(f32)
    for one in got:
        total = total + one.astype(f32)
    total = total.astype(bf16).reshape(4, 4, 16, half)
    got = [along_second(total[t], t) for t in (2, 1, 3)]
    final = total[0].astype(f32)
    for one in got:
        final = final + one.astype(f32)
    final = final.astype(bf16).reshape(2, 2, 16, half)
    got = [flip_z(final[1, 1], 1, 1), flip_z(final[0, 1], 0, 1), flip_z(final[1, 0], 1, 0)]
    own_columns = final[0, 0].astype(f32) + got[1].astype(f32)
    far_columns = got[2].astype(f32) + got[0].astype(f32)
    owned_sum = jnp.where(
        zl == 0,
        jnp.concatenate([own_columns, far_columns], axis=1),
        jnp.concatenate([far_columns, own_columns], axis=1),
    )

    mean_grad = (owned_sum / counted.shape[0])[None, :, :]
    new_moment = beta_one * moment + (1.0 - beta_one) * mean_grad
    new_second = beta_two * second + (1.0 - beta_two) * mean_grad * mean_grad
    update = (
        new_moment
        / (1.0 - beta_one**step_number)
        / (jnp.sqrt(new_second / (1.0 - beta_two**step_number)) + adam_eps)
    )
    new_master = master - learn_rate * (update + weight_decay * master)

    own = new_master[0].astype(bf16)
    block = jnp.stack([own, flip_z(own, 0, 1)])
    got = [along_second(block, t) for t in (1, 2, 3)]
    block = join([block] + got, flip_core(jnp.concatenate([one[0, :, :128] for one in got])))
    spread = [block] + [along_first(block, s) for s in (1, 2, 3)]
    s_, t_, dz_ = jnp.meshgrid(*(jnp.arange(n) for n in (4, 4, 2)), indexing="ij")
    first_at = (spot - s_) % 4
    second_at = (spot_second - t_) % 4
    x_at = jnp.where(c == 0, first_at, second_at)
    y_at = jnp.where(c == 0, second_at, first_at)
    rows = ((((zh ^ dz_) * 4 + y_at) * 4 + x_at) * 16).reshape(32).astype(jnp.int32)
    new_proj = place_rows(rows, spread)

    pre_grad, peer_grad, _ = lax.optimization_barrier((pre_grad, peer_grad, pieces[0]))
    pair = jnp.stack([pre_grad, peer_grad])
    pair = jnp.concatenate(
        [lax.dynamic_index_in_dim(pair, c ^ j, 0, keepdims=False) for j in range(2)]
    )
    to_heads = (((0,), (1,)), ((), ()))
    attn_far = lax.dot_general(pair, far, to_heads, preferred_element_type=f32).astype(bf16)
    attn_near = lax.dot_general(pair, near, to_heads, preferred_element_type=f32)
    attn_grad = (attn_near + flip_z(attn_far, 1, 0).astype(f32)).astype(bf16)
    return (layer_out, attn_grad, new_proj, new_master, new_moment, new_second)


def solution(mesh):
    wide = Mesh(mesh.devices.reshape(sizes), axes)
    dp, mp = ("zh", "y", "x"), ("zl", "c")
    return jax.shard_map(
        local,
        mesh=wide,
        in_specs=(
            P(dp, mp),
            P(mp, None),
            P(),
            P(dp, mp),
            P(dp, mp),
            P(),
            P(mp, dp, None),
            P(mp, dp, None),
            P(mp, dp, None),
        ),
        out_specs=(
            P(dp, mp),
            P(dp, mp),
            P(mp, None),
            P(mp, dp, None),
            P(mp, dp, None),
            P(mp, dp, None),
        ),
        check_vma=False,
    )
```

time: 655 us -> 191 us (0.29)
  waiting for transfers between devices: 570 us -> 106 us
  starting transfers between devices: 0.34 us -> 32.5 us
  matrix products: 26.7 us -> 9.44 us
  between operations: 13.8 us -> 1.21 us
  Pallas kernels: 0 us -> 10.9 us
  other arithmetic: 25.8 us -> 18.2 us
    reduce_scatter x1 -> x0, waiting for transfers between devices: 248 us -> none  [local(): lax.psum_scatter(grad_term, 'dp', scatter_dimension=0, tiled=True)]
    psum x1 -> x0, waiting for transfers between devices: 197 us -> none  [local(): summed = lax.psum(partial_value, 'mp')]
    all_gather x2 -> x0, waiting for transfers between devices: 124 us -> none  [the longest x1 74.7 us: local(): lax.all_gather(new_master[0].astype(jnp.bfloat16), 'dp', axis=0, tiled=True)]
    ppermute x0 -> x28, waiting for transfers between devices: none -> 106 us  [move(): lax.ppermute(value, axes, [(flat(p), flat(target(*p))) for p in places])]
    ppermute x0 -> x28, starting transfers between devices: none -> 32.5 us  [move(): lax.ppermute(value, axes, [(flat(p), flat(target(*p))) for p in places])]
    dot_general x3 -> x4, matrix products: 26.7 us -> 9.44 us  [the longest x1 4.37 us: local(): lax.dot_general(near, attention, left_rows, preferred_element_type=f32)]
    pallas_call x0 -> x3, Pallas kernels: none -> 10.9 us  [the longest x1 6.66 us: gradient_pieces(): pl.pallas_call(gradient_kernel, grid_spec=pltpu.PrefetchScalarGridSpec(nu...]
    convert_element_type x3 -> x5, other arithmetic: 17.2 us -> 6.6 us  [the longest x1 3.62 us: local(): pre_grad = (inv_rms * scaled - pre * inv_rms ** 3 * proj).astype(bf16)]
  transfers between devices with their start and end apart: 4 -> 28, of which waited for: 4 -> 23; matrix products, arithmetic and copies ran while one was open for 5% -> 10% of each run, Pallas kernels for 0% -> 0%
where the time goes in v2:
time: 191 us; the launch traced here: 189 us
  waiting for transfers between devices  106 us (55%)
  starting transfers between devices  32.5 us (17%)
  other arithmetic  18.2 us (10%)
  Pallas kernels  10.9 us (6%)
  local copies, waits for them, and re-layouts  10.5 us (5%)
  matrix products  9.44 us (5%)
    ppermute x28, waiting for transfers between devices, move(): lax.ppermute(value, axes, [(flat(p), flat(target(*p))) for p in places])  106 us
    ppermute x28, starting transfers between devices, move(): lax.ppermute(value, axes, [(flat(p), flat(target(*p))) for p in places])  32.5 us
    pallas_call x1, Pallas kernels, gradient_pieces(): pl.pallas_call(gradient_kernel, grid_spec=pltpu.PrefetchScalarGridSpec(nu...  6.66 us
    unnamed x35, local copies, waits for them, and re-layouts  6.43 us
    dot_general x1, matrix products, local(): lax.dot_general(near, attention, left_rows, preferred_element_type=f32)  4.37 us
  transfers between devices with their start and end apart: 28, of which 23 were waited for; matrix products, arithmetic and copies ran while one was open for 10% of the time, Pallas kernels for 0%

profile of v2, /device:TPU:6, one launch (start us, length us, event | category | flops | bytes accessed | tf_op | source)
XLA Modules:
  0.0 188.6 jit_solution(13364522114021132395)
XLA Ops:
  7.7 4.1 %collective-permute-start.4 = (bf16[192,2688]{1,0:T(8,128)(2,1)S(1)}, bf16[192,2688]{1,0:T(8,128)(2,1)S(1)}, u32[]{:S(2)}, u32[]{:S(2)}) collective-permute-start(bf16[192,2688]{1,0:T(8,128)(2,1)S(1)} %slice_select_fusion.1), channel_id=1, source_target_pairs={{0,66},{1,67},{2,64},{3,65},{4,70},{5,71},{6,68},{7,69},{8,74},{9,... | collective-permute-start | bytes 3096584 | tf_op jit(solution)/shard_map/ppermute | solution.py:38
  11.8 4.0 %collective-permute-done = bf16[80,2688]{1,0:T(8,128)(2,1)} collective-permute-done((bf16[80,2688]{1,0:T(8,128)(2,1)}, bf16[80,2688]{1,0:T(8,128)(2,1)}, u32[]{:S(2)}, u32[]{:S(2)}) %collective-permute-start) | collective-permute-done | bytes 430112 | tf_op jit(solution)/shard_map/ppermute | solution.py:38
  19.8 4.4 %fusion.13 = f32[2688,512]{1,0:T(8,128)S(1)} fusion(bf16[512,512]{1,0:T(8,128)(2,1)} %param.9, bf16[512,5376]{1,0:T(8,128)(2,1)} %param.10, pred[]{:T(512)S(6)} %eq.31), kind=kOutput, calls=%fused_computation.38 | convolution fusion | flops 1410662400 | bytes 11534337 | tf_op jit(solution)/shard_map/dot_general | solution.py:207
  24.2 5.8 %collective-permute-done.3 = bf16[80,2688]{1,0:T(8,128)(2,1)S(1)} collective-permute-done((bf16[80,2688]{1,0:T(8,128)(2,1)}, bf16[80,2688]{1,0:T(8,128)(2,1)S(1)}, u32[]{:S(2)}, u32[]{:S(2)}) %collective-permute-start.3) | collective-permute-done | bytes 430112 | tf_op jit(solution)/shard_map/ppermute | solution.py:38
  35.9 2.4 %copy-done.2 = f32[2688,512]{1,0:T(8,128)} copy-done((f32[2688,512]{1,0:T(8,128)}, f32[2688,512]{1,0:T(8,128)S(1)}, u32[]{:S(2)}) %copy-start.2) | copy-done | bytes 5505048
  40.3 2.6 %collective-permute-done.6 = bf16[1344,512]{1,0:T(8,128)(2,1)S(1)} collective-permute-done((bf16[1344,512]{1,0:T(8,128)(2,1)}, bf16[1344,512]{1,0:T(8,128)(2,1)S(1)}, u32[]{:S(2)}, u32[]{:S(2)}) %collective-permute-start.6) | collective-permute-done | bytes 1376288 | tf_op jit(solution)/shard_map/ppermute | solution.py:38
  42.9 3.0 %multiply_reduce_fusion = (f32[512]{0:T(512)S(1)}, f32[512]{0:T(512)S(1)}) fusion(bf16[1344,512]{1,0:T(8,128)(2,1)S(1)} %collective-permute-done.6, f32[2688,512]{1,0:T(8,128)} %copy-done.2, s32[]{:T(128)S(6)} %select_n.169, f32[1344]{0:T(1024)S(1)} %dynamic_slice.32, bf16[512,1344]{0,1:T(8,128)(2,1)S(1)} %copy-done.6), kind=kLoop, calls=%fused_computation.15 | loop fusion | flops 5504000 | bytes 5514500 | tf_op jit(solution)/shard_map/reduce_sum | solution.py:214
  47.5 3.4 %collective-permute-done.8 = f32[2,512]{1,0:T(2,128)S(1)} collective-permute-done((f32[2,512]{1,0:T(2,128)S(1)}, f32[2,512]{1,0:T(2,128)S(1)}, u32[]{:S(2)}, u32[]{:S(2)}) %collective-permute-start.8) | collective-permute-done | bytes 4128 | tf_op jit(solution)/shard_map/ppermute | solution.py:38
  50.9 3.6 %fusion.2 = (bf16[1344,512]{1,0:T(8,128)(2,1)S(1)}, bf16[512,1344]{0,1:T(8,128)(2,1)}) fusion(bf16[512,1344]{0,1:T(8,128)(2,1)S(1)} %copy-done.6, f32[512]{0:T(512)S(1)} %bitcast.90, f32[512]{0:T(512)S(1)} %bitcast.88, f32[512]{0:T(512)S(1)} %bitcast.89, f32[1344]{0:T(1024)S(1)} %dynamic_slice.32, bf16[1344,512]{1,0:T(8,128)(2,1)} %copy-done.7, ...), kind=kLoop, calls=%fused_computation.10 | loop fusion | flops 9633792 | bytes 9656324 | tf_op jit(solution)/shard_map/convert_element_type | solution.py:220
  57.9 6.7 %shard_map.136 = (bf16[16,16,2688]{2,1,0:T(8,128)(2,1)S(1)}, bf16[16,16,2688]{2,1,0:T(8,128)(2,1)S(1)}, bf16[16,16,2688]{2,1,0:T(8,128)(2,1)S(1)}, bf16[16,16,2688]{2,1,0:T(8,128)(2,1)S(1)}) custom-call(s32[65]{0:T(128)S(1)} %pad_add_fusion.rows_ref, bf16[1024,512]{1,0:T(8,128)(2,1)S(1)} %fusion.12.left_ref, ...), custom_call_target="tpu_custom_call" | custom-call | flops 2818572288 | bytes 10000000 | tf_op jit(solution)/shard_map/pallas_call | solution.py:102
  68.1 16.4 %collective-permute-done.11 = bf16[16,16,2688]{2,1,0:T(8,128)(2,1)S(1)} collective-permute-done((bf16[16,16,2688]{2,1,0:T(8,128)(2,1)S(1)}, bf16[16,16,2688]{2,1,0:T(8,128)(2,1)S(1)}, u32[]{:S(2)}, u32[]{:S(2)}) %collective-permute-start.11) | collective-permute-done | bytes 1376288 | tf_op jit(solution)/shard_map/ppermute | solution.py:38
  84.6 12.9 %collective-permute-done.12 = bf16[16,16,2688]{2,1,0:T(8,128)(2,1)S(1)} collective-permute-done((bf16[16,16,2688]{2,1,0:T(8,128)(2,1)S(1)}, bf16[16,16,2688]{2,1,0:T(8,128)(2,1)S(1)}, u32[]{:S(2)}, u32[]{:S(2)}) %collective-permute-start.12) | collective-permute-done | bytes 1376288 | tf_op jit(solution)/shard_map/ppermute | solution.py:38
  100.0 3.3 %collective-permute-start.14 = (bf16[4,16,2688]{2,1,0:T(8,128)(2,1)S(1)}, bf16[4,16,2688]{2,1,0:T(8,128)(2,1)S(1)}, u32[]{:S(2)}, u32[]{:S(2)}) collective-permute-start(bf16[4,16,2688]{2,1,0:T(8,128)(2,1)S(1)} %get-tuple-element.30), channel_id=1, source_target_pairs={{0,32},{1,9},{2,34},{3,11},{4,36},{5,13},{6,38},{7,15},{8,40},{9,1... | collective-permute-start | bytes 1032200 | tf_op jit(solution)/shard_map/ppermute | solution.py:38
  105.3 3.5 %collective-permute-done.14 = bf16[4,16,2688]{2,1,0:T(8,128)(2,1)S(1)} collective-permute-done((bf16[4,16,2688]{2,1,0:T(8,128)(2,1)S(1)}, bf16[4,16,2688]{2,1,0:T(8,128)(2,1)S(1)}, u32[]{:S(2)}, u32[]{:S(2)}) %collective-permute-start.14) | collective-permute-done | bytes 344096 | tf_op jit(solution)/shard_map/ppermute | solution.py:38
  108.8 4.1 %collective-permute-done.16 = bf16[4,16,2688]{2,1,0:T(8,128)(2,1)S(1)} collective-permute-done((bf16[4,16,2688]{2,1,0:T(8,128)(2,1)S(1)}, bf16[4,16,2688]{2,1,0:T(8,128)(2,1)S(1)}, u32[]{:S(2)}, u32[]{:S(2)}) %collective-permute-start.16) | collective-permute-done | bytes 344096 | tf_op jit(solution)/shard_map/ppermute | solution.py:38
  113.1 2.5 %collective-permute-start.17 = (bf16[16,2688]{1,0:T(8,128)(2,1)S(1)}, bf16[16,2688]{1,0:T(8,128)(2,1)S(1)}, u32[]{:S(2)}, u32[]{:S(2)}) collective-permute-start(bf16[16,2688]{1,0:T(8,128)(2,1)S(1)} %get-tuple-element.35), channel_id=1, source_target_pairs={{0,64},{1,65},{2,66},{3,67},{4,68},{5,69},{6,70},{7,71},{8,72},{9,... | collective-permute-start | bytes 258056 | tf_op jit(solution)/shard_map/ppermute | solution.py:38
  123.9 6.9 %collective-permute-done.20 = bf16[16,5376]{1,0:T(8,128)(2,1)S(1)} collective-permute-done((bf16[16,5376]{1,0:T(8,128)(2,1)S(1)}, bf16[16,5376]{1,0:T(8,128)(2,1)S(1)}, u32[]{:S(2)}, u32[]{:S(2)}) %collective-permute-start.20) | collective-permute-done | bytes 172064 | tf_op jit(solution)/shard_map/ppermute | solution.py:38
  130.9 2.7 %collective-permute-start.23 = (bf16[2,16,5376]{2,1,0:T(8,128)(2,1)S(1)}, bf16[2,16,5376]{2,1,0:T(8,128)(2,1)S(1)}, u32[]{:S(2)}, u32[]{:S(2)}) collective-permute-start(bf16[2,16,5376]{2,1,0:T(8,128)(2,1)S(1)} %pad_maximum_fusion.6.refs_0_), channel_id=1, source_target_pairs={{0,48},{1,13},{2,50},{3,15},{4,52},{5,1},{6,54},{7,3},{8,56},{9,5}... | collective-permute-start | bytes 1032200 | tf_op jit(solution)/shard_map/ppermute | solution.py:38
  135.7 6.4 %collective-permute-done.23.refs_3_ = bf16[2,16,5376]{2,1,0:T(8,128)(2,1)S(1)} collective-permute-done((bf16[2,16,5376]{2,1,0:T(8,128)(2,1)S(1)}, bf16[2,16,5376]{2,1,0:T(8,128)(2,1)S(1)}, u32[]{:S(2)}, u32[]{:S(2)}) %collective-permute-start.23) | collective-permute-done | bytes 344096 | tf_op jit(solution)/shard_map/ppermute | solution.py:38
  143.2 2.8 %collective-permute-done.21.refs_1_ = bf16[2,16,5376]{2,1,0:T(8,128)(2,1)S(1)} collective-permute-done((bf16[2,16,5376]{2,1,0:T(8,128)(2,1)S(1)}, bf16[2,16,5376]{2,1,0:T(8,128)(2,1)S(1)}, u32[]{:S(2)}, u32[]{:S(2)}) %collective-permute-start.21) | collective-permute-done | bytes 344096 | tf_op jit(solution)/shard_map/ppermute | solution.py:38
  150.9 2.7 %collective-permute-start.26 = (bf16[8,16,5376]{2,1,0:T(8,128)(2,1)S(1)}, bf16[8,16,5376]{2,1,0:T(8,128)(2,1)S(1)}, u32[]{:S(2)}, u32[]{:S(2)}) collective-permute-start(bf16[8,16,5376]{2,1,0:T(8,128)(2,1)S(1)} %shard_map.137.refs_0_), channel_id=1, source_target_pairs={{0,8},{1,33},{2,10},{3,35},{4,12},{5,37},{6,14},{7,39},{8,0},{9,41... | collective-permute-start | bytes 4128776 | tf_op jit(solution)/shard_map/ppermute | solution.py:38
  159.5 9.6 %collective-permute-done.10 = bf16[512,512]{1,0:T(8,128)(2,1)S(1)} collective-permute-done((bf16[512,512]{1,0:T(8,128)(2,1)S(1)}, bf16[512,512]{1,0:T(8,128)(2,1)S(1)}, u32[]{:S(2)}, u32[]{:S(2)}) %collective-permute-start.10) | collective-permute-done | bytes 524320 | tf_op jit(solution)/shard_map/ppermute | solution.py:38
  170.0 14.5 %collective-permute-done.26.refs_2_ = bf16[8,16,5376]{2,1,0:T(8,128)(2,1)S(1)} collective-permute-done((bf16[8,16,5376]{2,1,0:T(8,128)(2,1)S(1)}, bf16[8,16,5376]{2,1,0:T(8,128)(2,1)S(1)}, u32[]{:S(2)}, u32[]{:S(2)}) %collective-permute-start.26) | collective-permute-done | bytes 1376288 | tf_op jit(solution)/shard_map/ppermute | solution.py:38
  185.2 3.2 %shard_map.138 = bf16[512,5376]{1,0:T(8,128)(2,1)} custom-call(s32[32]{0:T(128)S(1)} %fusion.28.rows_ref, bf16[8,16,5376]{2,1,0:T(8,128)(2,1)S(1)} %shard_map.137.refs_0_, bf16[8,16,5376]{2,1,0:T(8,128)(2,1)S(1)} %collective-permute-done.25.refs_1_, bf16[8,16,5376]{2,1,0:T(8,128)(2,1)S(1)} %collective-permute-done.26.refs_2_, ...), custom_call_target="tpu_custom_call" | custom-call | bytes 11000000 | tf_op jit(solution)/shard_map/pallas_call | solution.py:166
  (124 shorter events, 56.0 us)
Async XLA Ops:
  2.7 13.1 %collective-permute-start = (bf16[80,2688]{1,0:T(8,128)(2,1)}, bf16[80,2688]{1,0:T(8,128)(2,1)}, u32[]{:S(2)}, u32[]{:S(2)}) collective-permute-start(bf16[80,2688]{1,0:T(8,128)(2,1)} %dynamic-slice_select_fusion), channel_id=1, source_target_pairs={{0,2},{1,3},{2,0},{3,1},{4,6},{5,7},{6,4},{7,5},{8,10},{9,11},{10,... | collective-permute-start | bytes 1290248 | tf_op jit(solution)/shard_map/ppermute | solution.py:38
  5.8 28.3 %collective-permute-start.5 = (bf16[512,512]{0,1:T(8,128)(2,1)S(1)}, bf16[512,512]{0,1:T(8,128)(2,1)S(1)}, u32[]{:S(2)}, u32[]{:S(2)}) collective-permute-start(bf16[512,512]{0,1:T(8,128)(2,1)S(1)} %copy.17), channel_id=1, source_target_pairs={{0,2},{1,3},{2,0},{3,1},{4,6},{5,7},{6,4},{7,5},{8,10},{9,11},{10,... | collective-permute-start | bytes 1572872 | tf_op jit(solution)/shard_map/ppermute | solution.py:38
  7.7 26.4 %collective-permute-start.4 = (bf16[192,2688]{1,0:T(8,128)(2,1)S(1)}, bf16[192,2688]{1,0:T(8,128)(2,1)S(1)}, u32[]{:S(2)}, u32[]{:S(2)}) collective-permute-start(bf16[192,2688]{1,0:T(8,128)(2,1)S(1)} %slice_select_fusion.1), channel_id=1, source_target_pairs={{0,66},{1,67},{2,64},{3,65},{4,70},{5,71},{6,68},{7,69},{8,74},{9,... | collective-permute-start | bytes 3096584 | tf_op jit(solution)/shard_map/ppermute | solution.py:38
  15.7 14.2 %collective-permute-start.3 = (bf16[80,2688]{1,0:T(8,128)(2,1)}, bf16[80,2688]{1,0:T(8,128)(2,1)S(1)}, u32[]{:S(2)}, u32[]{:S(2)}) collective-permute-start(bf16[80,2688]{1,0:T(8,128)(2,1)} %collective-permute-done), channel_id=1, source_target_pairs={{0,12},{1,49},{2,14},{3,51},{4,0},{5,53},{6,2},{7,55},{8,4},{9,57}... | collective-permute-start | bytes 1290248 | tf_op jit(solution)/shard_map/ppermute | solution.py:38
  16.6 13.4 %collective-permute-start.2 = (bf16[80,2688]{1,0:T(8,128)(2,1)}, bf16[80,2688]{1,0:T(8,128)(2,1)S(1)}, u32[]{:S(2)}, u32[]{:S(2)}) collective-permute-start(bf16[80,2688]{1,0:T(8,128)(2,1)} %collective-permute-done), channel_id=1, source_target_pairs={{0,8},{1,33},{2,10},{3,35},{4,12},{5,37},{6,14},{7,39},{8,0},{9,41... | collective-permute-start | bytes 1290248 | tf_op jit(solution)/shard_map/ppermute | solution.py:38
  17.6 13.3 %collective-permute-start.1 = (bf16[80,2688]{1,0:T(8,128)(2,1)}, bf16[80,2688]{1,0:T(8,128)(2,1)S(1)}, u32[]{:S(2)}, u32[]{:S(2)}) collective-permute-start(bf16[80,2688]{1,0:T(8,128)(2,1)} %collective-permute-done), channel_id=1, source_target_pairs={{0,4},{1,17},{2,6},{3,19},{4,8},{5,21},{6,10},{7,23},{8,12},{9,25}... | collective-permute-start | bytes 1290248 | tf_op jit(solution)/shard_map/ppermute | solution.py:38
  47.2 3.7 %collective-permute-start.8 = (f32[2,512]{1,0:T(2,128)S(1)}, f32[2,512]{1,0:T(2,128)S(1)}, u32[]{:S(2)}, u32[]{:S(2)}) collective-permute-start(f32[2,512]{1,0:T(2,128)S(1)} %fusion.31), channel_id=1, source_target_pairs={{0,2},{1,3},{2,0},{3,1},{4,6},{5,7},{6,4},{7,5},{8,10},{9,11},{10,... | collective-permute-start | bytes 12296 | tf_op jit(solution)/shard_map/ppermute | solution.py:38
  64.6 20.0 %collective-permute-start.11 = (bf16[16,16,2688]{2,1,0:T(8,128)(2,1)S(1)}, bf16[16,16,2688]{2,1,0:T(8,128)(2,1)S(1)}, u32[]{:S(2)}, u32[]{:S(2)}) collective-permute-start(bf16[16,16,2688]{2,1,0:T(8,128)(2,1)S(1)} %get-tuple-element.15), channel_id=1, source_target_pairs={{0,8},{1,33},{2,10},{3,35},{4,12},{5,37},{6,14},{7,39},{8,0},{9,41... | collective-permute-start | bytes 4128776 | tf_op jit(solution)/shard_map/ppermute | solution.py:38
  66.0 31.5 %collective-permute-start.12 = (bf16[16,16,2688]{2,1,0:T(8,128)(2,1)S(1)}, bf16[16,16,2688]{2,1,0:T(8,128)(2,1)S(1)}, u32[]{:S(2)}, u32[]{:S(2)}) collective-permute-start(bf16[16,16,2688]{2,1,0:T(8,128)(2,1)S(1)} %get-tuple-element.16), channel_id=1, source_target_pairs={{0,4},{1,17},{2,6},{3,19},{4,8},{5,21},{6,10},{7,23},{8,12},{9,25}... | collective-permute-start | bytes 4128776 | tf_op jit(solution)/shard_map/ppermute | solution.py:38
  68.1 31.1 %collective-permute-start.13 = (bf16[16,16,2688]{2,1,0:T(8,128)(2,1)S(1)}, bf16[16,16,2688]{2,1,0:T(8,128)(2,1)S(1)}, u32[]{:S(2)}, u32[]{:S(2)}) collective-permute-start(bf16[16,16,2688]{2,1,0:T(8,128)(2,1)S(1)} %get-tuple-element.17), channel_id=1, source_target_pairs={{0,12},{1,49},{2,14},{3,51},{4,0},{5,53},{6,2},{7,55},{8,4},{9,57}... | collective-permute-start | bytes 4128776 | tf_op jit(solution)/shard_map/ppermute | solution.py:38
  100.0 8.8 %collective-permute-start.14 = (bf16[4,16,2688]{2,1,0:T(8,128)(2,1)S(1)}, bf16[4,16,2688]{2,1,0:T(8,128)(2,1)S(1)}, u32[]{:S(2)}, u32[]{:S(2)}) collective-permute-start(bf16[4,16,2688]{2,1,0:T(8,128)(2,1)S(1)} %get-tuple-element.30), channel_id=1, source_target_pairs={{0,32},{1,9},{2,34},{3,11},{4,36},{5,13},{6,38},{7,15},{8,40},{9,1... | collective-permute-start | bytes 1032200 | tf_op jit(solution)/shard_map/ppermute | solution.py:38
  103.3 9.6 %collective-permute-start.16 = (bf16[4,16,2688]{2,1,0:T(8,128)(2,1)S(1)}, bf16[4,16,2688]{2,1,0:T(8,128)(2,1)S(1)}, u32[]{:S(2)}, u32[]{:S(2)}) collective-permute-start(bf16[4,16,2688]{2,1,0:T(8,128)(2,1)S(1)} %get-tuple-element.31), channel_id=1, source_target_pairs={{0,48},{1,13},{2,50},{3,15},{4,52},{5,1},{6,54},{7,3},{8,56},{9,5}... | collective-permute-start | bytes 1032200 | tf_op jit(solution)/shard_map/ppermute | solution.py:38
  104.3 8.6 %collective-permute-start.15 = (bf16[4,16,2688]{2,1,0:T(8,128)(2,1)S(1)}, bf16[4,16,2688]{2,1,0:T(8,128)(2,1)S(1)}, u32[]{:S(2)}, u32[]{:S(2)}) collective-permute-start(bf16[4,16,2688]{2,1,0:T(8,128)(2,1)S(1)} %get-tuple-element.32), channel_id=1, source_target_pairs={{0,16},{1,5},{2,18},{3,7},{4,20},{5,9},{6,22},{7,11},{8,24},{9,13}... | collective-permute-start | bytes 1032200 | tf_op jit(solution)/shard_map/ppermute | solution.py:38
  113.1 6.1 %collective-permute-start.17 = (bf16[16,2688]{1,0:T(8,128)(2,1)S(1)}, bf16[16,2688]{1,0:T(8,128)(2,1)S(1)}, u32[]{:S(2)}, u32[]{:S(2)}) collective-permute-start(bf16[16,2688]{1,0:T(8,128)(2,1)S(1)} %get-tuple-element.35), channel_id=1, source_target_pairs={{0,64},{1,65},{2,66},{3,67},{4,68},{5,69},{6,70},{7,71},{8,72},{9,... | collective-permute-start | bytes 258056 | tf_op jit(solution)/shard_map/ppermute | solution.py:38
  115.6 4.8 %collective-permute-start.18 = (bf16[16,2688]{1,0:T(8,128)(2,1)S(1)}, bf16[16,2688]{1,0:T(8,128)(2,1)S(1)}, u32[]{:S(2)}, u32[]{:S(2)}) collective-permute-start(bf16[16,2688]{1,0:T(8,128)(2,1)S(1)} %get-tuple-element.33), channel_id=1, source_target_pairs={{0,2},{1,3},{2,0},{3,1},{4,6},{5,7},{6,4},{7,5},{8,10},{9,11},{10,... | collective-permute-start | bytes 258056 | tf_op jit(solution)/shard_map/ppermute | solution.py:38
  117.0 5.7 %collective-permute-start.19 = (bf16[16,2688]{1,0:T(8,128)(2,1)S(1)}, bf16[16,2688]{1,0:T(8,128)(2,1)S(1)}, u32[]{:S(2)}, u32[]{:S(2)}) collective-permute-start(bf16[16,2688]{1,0:T(8,128)(2,1)S(1)} %get-tuple-element.34), channel_id=1, source_target_pairs={{0,66},{1,67},{2,64},{3,65},{4,70},{5,71},{6,68},{7,69},{8,74},{9,... | collective-permute-start | bytes 258056 | tf_op jit(solution)/shard_map/ppermute | solution.py:38
  123.9 6.9 %collective-permute-start.20 = (bf16[16,5376]{1,0:T(8,128)(2,1)S(1)}, bf16[16,5376]{1,0:T(8,128)(2,1)S(1)}, u32[]{:S(2)}, u32[]{:S(2)}) collective-permute-start(bf16[16,5376]{1,0:T(8,128)(2,1)S(1)} %bitcast.77), channel_id=1, source_target_pairs={{0,64},{1,65},{2,66},{3,67},{4,68},{5,69},{6,70},{7,71},{8,72},{9,... | collective-permute-start | bytes 516104 | tf_op jit(solution)/shard_map/ppermute | solution.py:38
  130.9 11.2 %collective-permute-start.23 = (bf16[2,16,5376]{2,1,0:T(8,128)(2,1)S(1)}, bf16[2,16,5376]{2,1,0:T(8,128)(2,1)S(1)}, u32[]{:S(2)}, u32[]{:S(2)}) collective-permute-start(bf16[2,16,5376]{2,1,0:T(8,128)(2,1)S(1)} %pad_maximum_fusion.6.refs_0_), channel_id=1, source_target_pairs={{0,48},{1,13},{2,50},{3,15},{4,52},{5,1},{6,54},{7,3},{8,56},{9,5}... | collective-permute-start | bytes 1032200 | tf_op jit(solution)/shard_map/ppermute | solution.py:38
  133.6 9.0 %collective-permute-start.22 = (bf16[2,16,5376]{2,1,0:T(8,128)(2,1)S(1)}, bf16[2,16,5376]{2,1,0:T(8,128)(2,1)}, u32[]{:S(2)}, u32[]{:S(2)}) collective-permute-start(bf16[2,16,5376]{2,1,0:T(8,128)(2,1)S(1)} %pad_maximum_fusion.6.refs_0_), channel_id=1, source_target_pairs={{0,32},{1,9},{2,34},{3,11},{4,36},{5,13},{6,38},{7,15},{8,40},{9,1... | collective-permute-start | bytes 1032200 | tf_op jit(solution)/shard_map/ppermute | solution.py:38
  134.8 11.2 %collective-permute-start.21 = (bf16[2,16,5376]{2,1,0:T(8,128)(2,1)S(1)}, bf16[2,16,5376]{2,1,0:T(8,128)(2,1)S(1)}, u32[]{:S(2)}, u32[]{:S(2)}) collective-permute-start(bf16[2,16,5376]{2,1,0:T(8,128)(2,1)S(1)} %pad_maximum_fusion.6.refs_0_), channel_id=1, source_target_pairs={{0,16},{1,5},{2,18},{3,7},{4,20},{5,9},{6,22},{7,11},{8,24},{9,13}... | collective-permute-start | bytes 1032200 | tf_op jit(solution)/shard_map/ppermute | solution.py:38
  150.0 20.1 %collective-permute-start.27 = (bf16[8,16,5376]{2,1,0:T(8,128)(2,1)S(1)}, bf16[8,16,5376]{2,1,0:T(8,128)(2,1)S(1)}, u32[]{:S(2)}, u32[]{:S(2)}) collective-permute-start(bf16[8,16,5376]{2,1,0:T(8,128)(2,1)S(1)} %shard_map.137.refs_0_), channel_id=1, source_target_pairs={{0,12},{1,49},{2,14},{3,51},{4,0},{5,53},{6,2},{7,55},{8,4},{9,57}... | collective-permute-start | bytes 4128776 | tf_op jit(solution)/shard_map/ppermute | solution.py:38
  150.9 33.7 %collective-permute-start.26 = (bf16[8,16,5376]{2,1,0:T(8,128)(2,1)S(1)}, bf16[8,16,5376]{2,1,0:T(8,128)(2,1)S(1)}, u32[]{:S(2)}, u32[]{:S(2)}) collective-permute-start(bf16[8,16,5376]{2,1,0:T(8,128)(2,1)S(1)} %shard_map.137.refs_0_), channel_id=1, source_target_pairs={{0,8},{1,33},{2,10},{3,35},{4,12},{5,37},{6,14},{7,39},{8,0},{9,41... | collective-permute-start | bytes 4128776 | tf_op jit(solution)/shard_map/ppermute | solution.py:38
  153.6 31.7 %collective-permute-start.25 = (bf16[8,16,5376]{2,1,0:T(8,128)(2,1)S(1)}, bf16[8,16,5376]{2,1,0:T(8,128)(2,1)S(1)}, u32[]{:S(2)}, u32[]{:S(2)}) collective-permute-start(bf16[8,16,5376]{2,1,0:T(8,128)(2,1)S(1)} %shard_map.137.refs_0_), channel_id=1, source_target_pairs={{0,4},{1,17},{2,6},{3,19},{4,8},{5,21},{6,10},{7,23},{8,12},{9,25}... | collective-permute-start | bytes 4128776 | tf_op jit(solution)/shard_map/ppermute | solution.py:38
  157.7 11.4 %collective-permute-start.10 = (bf16[512,512]{1,0:T(8,128)(2,1)S(1)}, bf16[512,512]{1,0:T(8,128)(2,1)S(1)}, u32[]{:S(2)}, u32[]{:S(2)}) collective-permute-start(bf16[512,512]{1,0:T(8,128)(2,1)S(1)} %fusion.11), channel_id=1, source_target_pairs={{0,2},{1,3},{2,0},{3,1},{4,6},{5,7},{6,4},{7,5},{8,10},{9,11},{10,... | collective-permute-start | bytes 1572872 | tf_op jit(solution)/shard_map/ppermute | solution.py:38
  (19 other events, 115.0 us)

commit v3 on v2

v3 whole, which is shorter than its diff:
```python
import jax
import jax.numpy as jnp
from jax import lax
from jax.experimental import pallas as pl
from jax.experimental.pallas import tpu as pltpu
from jax.sharding import Mesh, PartitionSpec as P

norm_eps = 1e-06
beta_one = 0.9
beta_two = 0.999
adam_eps = 1e-08
learn_rate = 0.01
weight_decay = 0.1
step_number = 100.0

axes = ("zh", "y", "x", "zl", "c")
sizes = (2, 4, 4, 2, 2)
bf16 = jnp.bfloat16
f32 = jnp.float32

places = [
    (zh, y, x, zl, c)
    for zh in range(2)
    for y in range(4)
    for x in range(4)
    for zl in range(2)
    for c in range(2)
]


def move(value, target):
    def flat(place):
        index = 0
        for size, at in zip(sizes, place):
            index = index * size + at % size
        return index

    return lax.ppermute(value, axes, [(flat(p), flat(target(*p))) for p in places])


def along_first(value, step):
    return move(
        value,
        lambda zh, y, x, zl, c: (zh, y, x + step, zl, c) if c == 0 else (zh, y + step, x, zl, c),
    )


def along_second(value, step):
    return move(
        value,
        lambda zh, y, x, zl, c: (zh, y + step, x, zl, c) if c == 0 else (zh, y, x + step, zl, c),
    )


def flip_core(value):
    return move(value, lambda zh, y, x, zl, c: (zh, y, x, zl, 1 - c))


def flip_z(value, low, high):
    return move(value, lambda zh, y, x, zl, c: (zh ^ high, y, x, zl ^ low, c))


def gradient_kernel(rows_ref, left_ref, right_ref, *rest):
    outs, sent = rest[:4], rest[4]

    @pl.when(pl.program_id(0) == 0)
    def _():
        for k in range(32):
            row = pl.multiple_of(rows_ref[k], 16)
            sent[pl.ds(16 * k, 16), :] = left_ref[pl.ds(row, 16), :]

    term = lax.dot_general(
        sent[...], right_ref[...], (((1,), (1,)), ((), ())), preferred_element_type=f32
    )
    term = term.astype(bf16).reshape(4, 8, 16, right_ref.shape[0])
    for one in range(4):
        outs[one][...] = term[one]


def gradient_pieces(rows, left, right):
    heads, tokens = left.shape
    columns = right.shape[0]
    width = 384
    return pl.pallas_call(
        gradient_kernel,
        grid_spec=pltpu.PrefetchScalarGridSpec(
            num_scalar_prefetch=1,
            grid=(columns // width,),
            in_specs=[
                pl.BlockSpec((heads, tokens), lambda i, rows: (0, 0)),
                pl.BlockSpec((width, tokens), lambda i, rows: (i, 0)),
            ],
            out_specs=[pl.BlockSpec((8, 16, width), lambda i, rows: (0, 0, i))] * 4,
            scratch_shapes=[pltpu.VMEM((512, tokens), bf16)],
        ),
        out_shape=[jax.ShapeDtypeStruct((8, 16, columns), bf16)] * 4,
        compiler_params=pltpu.CompilerParams(vmem_limit_bytes=24 * 1024 * 1024),
        cost_estimate=pl.CostEstimate(
            flops=2 * 512 * tokens * columns, bytes_accessed=6_000_000, transcendentals=0
        ),
    )(rows, left, right)


def place_kernel(rows_ref, *refs):
    *pieces, out_ref, sems = refs
    copies = [
        pltpu.make_async_copy(
            piece.at[k],
            out_ref.at[pl.ds(pl.multiple_of(rows_ref[4 * i + k], 16), 16)],
            sems.at[4 * i + k],
        )
        for i, piece in enumerate(pieces)
        for k in range(4)
    ]
    for copy in copies:
        copy.start()
    for copy in copies:
        copy.wait()


def place_more_kernel(rows_ref, earlier_ref, *refs):
    place_kernel(rows_ref, *refs)


def place_rows(rows, pieces, earlier=None):
    count = len(pieces)
    anywhere = pl.BlockSpec(memory_space=pl.ANY)
    before = [] if earlier is None else [earlier]
    return pl.pallas_call(
        place_more_kernel if before else place_kernel,
        grid_spec=pltpu.PrefetchScalarGridSpec(
            num_scalar_prefetch=1,
            grid=(1,),
            in_specs=[anywhere] * len(before) + [pl.BlockSpec(memory_space=pltpu.VMEM)] * count,
            out_specs=anywhere,
            scratch_shapes=[pltpu.SemaphoreType.DMA((4 * count,))],
        ),
        out_shape=jax.ShapeDtypeStruct((512, pieces[0].shape[-1]), bf16),
        input_output_aliases={1: 0} if before else {},
        compiler_params=pltpu.CompilerParams(vmem_limit_bytes=24 * 1024 * 1024),
        cost_estimate=pl.CostEstimate(
            flops=0, bytes_accessed=1_400_000 * count, transcendentals=0
        ),
    )(rows, *before, *pieces)


def local(attention, out_proj, post_gain, residual, cotangent, counted, master, moment, second):
    zh, y, x, zl, c = (lax.axis_index(a) for a in axes)
    replica = (zh * 4 + y) * 4 + x
    tokens, part = residual.shape
    heads = attention.shape[1]
    full_width = post_gain.shape[0]
    half = full_width // 2
    gain = lax.dynamic_slice_in_dim(post_gain, (zl * 2 + c) * part, part, 0)[:, None]
    counted_flag = jnp.sum((counted == replica).astype(f32))
    spot = jnp.where(c == 0, x, y)
    spot_second = jnp.where(c == 0, y, x)

    near = jnp.where(zl == 0, out_proj[:, :half], out_proj[:, half:])
    share, shared = 80, 320
    shares = lax.dynamic_slice_in_dim(out_proj, spot * share, share, 0)
    received = flip_z(jnp.where(zl == 0, shares[:, half:], shares[:, :half]), 1, 0)
    rest = out_proj[shared:]
    direct = flip_z(jnp.where(zl == 0, rest[:, half:], rest[:, :half]), 1, 1)
    far_attention = flip_z(attention, 1, 0)
    rel = jnp.stack([received] + [along_first(received, s) for s in (1, 2, 3)])
    far = jnp.concatenate(
        [lax.dynamic_index_in_dim(rel, (spot - j) % 4, 0, keepdims=False) for j in range(4)]
        + [direct]
    )

    left_rows = (((0,), (1,)), ((), ()))
    pre_pair = lax.dot_general(near, attention, left_rows, preferred_element_type=f32)
    pre_pair = pre_pair + lax.dot_general(far, far_attention, left_rows, preferred_element_type=f32)
    mine = lax.dynamic_slice_in_dim(pre_pair, c * part, part, 0)
    other = lax.dynamic_slice_in_dim(pre_pair, (1 - c) * part, part, 0)
    pre = mine + flip_core(other.astype(bf16)).astype(f32)

    scaled = cotangent.T.astype(f32) * gain
    stats = jnp.stack([jnp.sum(pre * pre, axis=0), jnp.sum(scaled * pre, axis=0)])
    stats = stats + flip_core(stats)
    stats = stats + flip_z(stats, 1, 0)
    inv_rms = lax.rsqrt(stats[0] / full_width + norm_eps)[None, :]
    proj = (stats[1] / full_width)[None, :]
    layer_out = (residual.T.astype(f32) + gain * (pre * inv_rms)).astype(bf16).T
    pre_grad = (inv_rms * scaled - pre * inv_rms**3 * proj).astype(bf16)
    peer_grad = flip_core(pre_grad)

    pair = jnp.stack([pre_grad, peer_grad])
    pair = jnp.concatenate(
        [lax.dynamic_index_in_dim(pair, c ^ j, 0, keepdims=False) for j in range(2)]
    )

    left = jnp.concatenate([attention, far_attention], axis=1)
    left = (left.astype(f32) * counted_flag).astype(bf16).T
    left = lax.optimization_barrier(left)
    s_, dz_, t_, slot_ = jnp.meshgrid(*(jnp.arange(n) for n in (4, 2, 4, 2)), indexing="ij")
    first_at = (spot + s_) % 4
    second_at = (spot_second + t_) % 4
    x_at = jnp.where(c == 0, first_at, second_at)
    y_at = jnp.where(c == 0, second_at, first_at)
    rows = slot_ * 512 + (((zh ^ dz_) * 4 + y_at) * 4 + x_at) * 16
    rows = rows.reshape(4, 2, 8).astype(jnp.int32)
    early = jnp.concatenate([rows[2, 1], rows[3, 1], rows[2, 0], rows[1, 0]])
    later = jnp.concatenate([rows[1, 1], rows[0, 1], rows[3, 0], rows[0, 0]])
    two_far, three_far, two_near, one_near = gradient_pieces(early, left, pair)
    one_far, none_far, three_near, none_near = gradient_pieces(later, left, pair)

    passing_up, from_above = along_first(two_far, 1), along_first(three_far, -1)
    passing_down, from_below = along_first(two_near, -1), along_first(one_near, 1)
    summed_below = along_first((one_far.astype(f32) + passing_up.astype(f32)).astype(bf16), 1)
    summed_above = along_first((three_near.astype(f32) + passing_down.astype(f32)).astype(bf16), -1)

    def second_sum(total):
        total = total.astype(bf16).reshape(4, 2, 16, half)
        got = [along_second(total[t], t) for t in (2, 1, 3)]
        final = total[0].astype(f32)
        for one in got:
            final = final + one.astype(f32)
        return final.astype(bf16)

    far_rows = second_sum(none_far.astype(f32) + from_above.astype(f32) + summed_below.astype(f32))
    got = [flip_z(far_rows[0], 0, 1), flip_z(far_rows[1], 1, 1)]
    near_rows = second_sum(none_near.astype(f32) + from_below.astype(f32) + summed_above.astype(f32))
    own_columns = near_rows[0].astype(f32) + got[0].astype(f32)
    far_columns = flip_z(near_rows[1], 1, 0).astype(f32) + got[1].astype(f32)
    owned_sum = jnp.where(
        zl == 0,
        jnp.concatenate([own_columns, far_columns], axis=1),
        jnp.concatenate([far_columns, own_columns], axis=1),
    )

    mean_grad = (owned_sum / counted.shape[0])[None, :, :]
    new_moment = beta_one * moment + (1.0 - beta_one) * mean_grad
    new_second = beta_two * second + (1.0 - beta_two) * mean_grad * mean_grad
    update = (
        new_moment
        / (1.0 - beta_one**step_number)
        / (jnp.sqrt(new_second / (1.0 - beta_two**step_number)) + adam_eps)
    )
    new_master = master - learn_rate * (update + weight_decay * master)

    own = new_master.astype(bf16)
    other = flip_z(own, 0, 1)
    low = jnp.concatenate([own] + [along_second(own, t) for t in (1, 2, 3)])
    low_below, low_above = along_first(low, 1), along_first(low, -1)
    high = jnp.concatenate([other] + [along_second(other, t) for t in (1, 2, 3)])
    high_below, high_above = along_first(high, 1), along_first(high, -1)
    low_far, high_far = along_first(low_below, 1), along_first(high_above, -1)
    s_, dz_, t_ = jnp.meshgrid(*(jnp.arange(n) for n in (4, 2, 4)), indexing="ij")
    first_at = (spot - s_) % 4
    second_at = (spot_second - t_) % 4
    x_at = jnp.where(c == 0, first_at, second_at)
    y_at = jnp.where(c == 0, second_at, first_at)
    rows = ((((zh ^ dz_) * 4 + y_at) * 4 + x_at) * 16).reshape(4, 8).astype(jnp.int32)
    first_rows = jnp.concatenate([rows[0], rows[1], rows[3]])
    new_proj = place_rows(first_rows, [low, high, low_below, high_below, low_above, high_above])
    new_proj = place_rows(rows[2], [low_far, high_far], new_proj)

    pair, _ = lax.optimization_barrier((pair, none_near))
    to_heads = (((0,), (1,)), ((), ()))
    attn_far = lax.dot_general(pair, far, to_heads, preferred_element_type=f32).astype(bf16)
    attn_near = lax.dot_general(pair, near, to_heads, preferred_element_type=f32)
    attn_grad = (attn_near + flip_z(attn_far, 1, 0).astype(f32)).astype(bf16)
    return (layer_out, attn_grad, new_proj, new_master, new_moment, new_second)


def solution(mesh):
    wide = Mesh(mesh.devices.reshape(sizes), axes)
    dp, mp = ("zh", "y", "x"), ("zl", "c")
    return jax.shard_map(
        local,
        mesh=wide,
        in_specs=(
            P(dp, mp),
            P(mp, None),
            P(),
            P(dp, mp),
            P(dp, mp),
            P(),
            P(mp, dp, None),
            P(mp, dp, None),
            P(mp, dp, None),
        ),
        out_specs=(
            P(dp, mp),
            P(dp, mp),
            P(mp, None),
            P(mp, dp, None),
            P(mp, dp, None),
            P(mp, dp, None),
        ),
        check_vma=False,
    )
```

time: 191 us -> 168 us (0.88); the launches traced: 189 us -> 168 us
  waiting for transfers between devices: 106 us -> 62.7 us
  starting transfers between devices: 32.5 us -> 47 us
  matrix products: 9.44 us -> 13.8 us
  Pallas kernels: 10.9 us -> 14.3 us
    ppermute x28 -> x39, waiting for transfers between devices: 106 us -> 62.7 us  [move(): lax.ppermute(value, axes, [(flat(p), flat(target(*p))) for p in places])]
    ppermute x28 -> x39, starting transfers between devices: 32.5 us -> 47 us  [move(): lax.ppermute(value, axes, [(flat(p), flat(target(*p))) for p in places])]
    dot_general x1, matrix products: 1.73 us -> 4.32 us  [local(): lax.dot_general(pair, near, to_heads, preferred_element_type=f32)]
    pallas_call x1 -> x2, Pallas kernels: 6.66 us -> 8.38 us  [gradient_pieces(): pl.pallas_call(gradient_kernel, grid_spec=pltpu.PrefetchScalarGridSpec(nu...]
    unnamed x35 -> x26, local copies, waits for them, and re-layouts: 6.43 us -> 6.76 us
  transfers between devices with their start and end apart: 28 -> 39, of which waited for: 23 -> 25; matrix products, arithmetic and copies ran while one was open for 10% -> 15% of each run, Pallas kernels for 0% -> 5%
where the time goes in v3:
time: 168 us
  waiting for transfers between devices  62.7 us (37%)
  starting transfers between devices  47 us (28%)
  other arithmetic  18.5 us (11%)
  Pallas kernels  14.3 us (9%)
  matrix products  13.8 us (8%)
  local copies, waits for them, and re-layouts  10.3 us (6%)
    ppermute x39, waiting for transfers between devices, move(): lax.ppermute(value, axes, [(flat(p), flat(target(*p))) for p in places])  62.7 us
    ppermute x39, starting transfers between devices, move(): lax.ppermute(value, axes, [(flat(p), flat(target(*p))) for p in places])  47 us
    pallas_call x2, Pallas kernels, gradient_pieces(): pl.pallas_call(gradient_kernel, grid_spec=pltpu.PrefetchScalarGridSpec(nu...  8.38 us
    unnamed x26, local copies, waits for them, and re-layouts  6.76 us
    pallas_call x2, Pallas kernels, place_rows(): pl.pallas_call(place_more_kernel if before else place_kernel, grid_spec=p...  5.91 us
    dot_general x1, matrix products, local(): lax.dot_general(near, attention, left_rows, preferred_element_type=f32)  4.37 us
    dot_general x1, matrix products, local(): lax.dot_general(pair, near, to_heads, preferred_element_type=f32)  4.32 us
    convert_element_type x1, other arithmetic, local(): pre_grad = (inv_rms * scaled - pre * inv_rms ** 3 * proj).astype(bf16)  4.07 us
  transfers between devices with their start and end apart: 39, of which 25 were waited for; matrix products, arithmetic and copies ran while one was open for 15% of the time, Pallas kernels for 5%

profile of v3, /device:TPU:6, one launch (start us, length us, event | category | flops | bytes accessed | tf_op | source)
XLA Modules:
  0.0 167.8 jit_solution(13022362212343390397)
XLA Ops:
  7.7 4.1 %collective-permute-start.4 = (bf16[192,2688]{1,0:T(8,128)(2,1)S(1)}, bf16[192,2688]{1,0:T(8,128)(2,1)S(1)}, u32[]{:S(2)}, u32[]{:S(2)}) collective-permute-start(bf16[192,2688]{1,0:T(8,128)(2,1)S(1)} %slice_select_fusion.1), channel_id=1, source_target_pairs={{0,66},{1,67},{2,64},{3,65},{4,70},{5,71},{6,68},{7,69},{8,74},{9,... | collective-permute-start | bytes 3096584 | tf_op jit(solution)/shard_map/ppermute | solution.py:38
  11.8 3.9 %collective-permute-done = bf16[80,2688]{1,0:T(8,128)(2,1)S(1)} collective-permute-done((bf16[80,2688]{1,0:T(8,128)(2,1)}, bf16[80,2688]{1,0:T(8,128)(2,1)S(1)}, u32[]{:S(2)}, u32[]{:S(2)}) %collective-permute-start) | collective-permute-done | bytes 430112 | tf_op jit(solution)/shard_map/ppermute | solution.py:38
  19.7 4.4 %fusion.11 = f32[2688,512]{1,0:T(8,128)S(1)} fusion(bf16[512,512]{1,0:T(8,128)(2,1)} %param.9, bf16[512,5376]{1,0:T(8,128)(2,1)} %param.10, pred[]{:T(512)S(6)} %eq.31), kind=kOutput, calls=%fused_computation.40 | convolution fusion | flops 1410662400 | bytes 11534337 | tf_op jit(solution)/shard_map/dot_general | solution.py:173
  24.1 5.6 %collective-permute-done.3 = bf16[80,2688]{1,0:T(8,128)(2,1)S(1)} collective-permute-done((bf16[80,2688]{1,0:T(8,128)(2,1)S(1)}, bf16[80,2688]{1,0:T(8,128)(2,1)S(1)}, u32[]{:S(2)}, u32[]{:S(2)}) %collective-permute-start.3) | collective-permute-done | bytes 430112 | tf_op jit(solution)/shard_map/ppermute | solution.py:38
  31.0 3.0 %collective-permute-done.4 = bf16[192,2688]{1,0:T(8,128)(2,1)S(1)} collective-permute-done((bf16[192,2688]{1,0:T(8,128)(2,1)S(1)}, bf16[192,2688]{1,0:T(8,128)(2,1)S(1)}, u32[]{:S(2)}, u32[]{:S(2)}) %collective-permute-start.4) | collective-permute-done | bytes 1032224 | tf_op jit(solution)/shard_map/ppermute | solution.py:38
  36.7 2.4 %copy-done = f32[2688,512]{1,0:T(8,128)} copy-done((f32[2688,512]{1,0:T(8,128)}, f32[2688,512]{1,0:T(8,128)S(1)}, u32[]{:S(2)}) %copy-start) | copy-done | bytes 5505048
  41.2 2.5 %collective-permute-done.6 = bf16[1344,512]{1,0:T(8,128)(2,1)S(1)} collective-permute-done((bf16[1344,512]{1,0:T(8,128)(2,1)}, bf16[1344,512]{1,0:T(8,128)(2,1)S(1)}, u32[]{:S(2)}, u32[]{:S(2)}) %collective-permute-start.6) | collective-permute-done | bytes 1376288 | tf_op jit(solution)/shard_map/ppermute | solution.py:38
  43.7 3.0 %multiply_reduce_fusion = (f32[512]{0:T(512)S(1)}, f32[512]{0:T(512)S(1)}) fusion(bf16[1344,512]{1,0:T(8,128)(2,1)S(1)} %collective-permute-done.6, f32[2688,512]{1,0:T(8,128)} %copy-done, s32[]{:T(128)S(6)} %select_n.165, f32[1344]{0:T(1024)S(1)} %dynamic_slice.32, bf16[512,1344]{0,1:T(8,128)(2,1)S(1)} %copy-done.2), kind=kLoop, calls=%fused_computation.14 | loop fusion | flops 5504000 | bytes 5514500 | tf_op jit(solution)/shard_map/reduce_sum | solution.py:180
  48.1 3.6 %collective-permute-done.8 = f32[2,512]{1,0:T(2,128)S(1)} collective-permute-done((f32[2,512]{1,0:T(2,128)S(1)}, f32[2,512]{1,0:T(2,128)S(1)}, u32[]{:S(2)}, u32[]{:S(2)}) %collective-permute-start.8) | collective-permute-done | bytes 4128 | tf_op jit(solution)/shard_map/ppermute | solution.py:38
  51.7 4.1 %fusion.2 = (bf16[1344,512]{1,0:T(8,128)(2,1)S(1)}, bf16[512,1344]{0,1:T(8,128)(2,1)}) fusion(bf16[512,1344]{0,1:T(8,128)(2,1)S(1)} %copy-done.2, f32[512]{0:T(512)S(1)} %bitcast.93, f32[512]{0:T(512)S(1)} %bitcast.91, f32[512]{0:T(512)S(1)} %bitcast.92, f32[1344]{0:T(1024)S(1)} %dynamic_slice.32, bf16[1344,512]{1,0:T(8,128)(2,1)} %copy-done.3, ...), kind=kLoop, calls=%fused_computation.10 | loop fusion | flops 9633792 | bytes 9656324 | tf_op jit(solution)/shard_map/convert_element_type | solution.py:186
  60.1 4.2 %shard_map.137 = (bf16[8,16,2688]{2,1,0:T(8,128)(2,1)S(1)}, bf16[8,16,2688]{2,1,0:T(8,128)(2,1)S(1)}, bf16[8,16,2688]{2,1,0:T(8,128)(2,1)S(1)}, bf16[8,16,2688]{2,1,0:T(8,128)(2,1)S(1)}) custom-call(s32[32]{0:T(128)S(1)} %pad_add_fusion.2.rows_ref, bf16[1024,512]{1,0:T(8,128)(2,1)S(1)} %fusion.9.left_ref, bf16[2688,512]{1,0:T(8,128)(2,1)S(1)} %pad_maximum_fusion.right_ref), custom_call_target="tpu_custom_call" | custom-call | flops 1409286144 | bytes 6000000 | tf_op jit(solution)/shard_map/pallas_call | solution.py:84
  68.8 4.2 %shard_map.136 = (bf16[8,16,2688]{2,1,0:T(8,128)(2,1)S(1)}, bf16[8,16,2688]{2,1,0:T(8,128)(2,1)S(1)}, bf16[8,16,2688]{2,1,0:T(8,128)(2,1)S(1)}, bf16[8,16,2688]{2,1,0:T(8,128)(2,1)S(1)}) custom-call(s32[32]{0:T(128)S(1)} %pad_add_fusion.rows_ref, bf16[1024,512]{1,0:T(8,128)(2,1)S(1)} %fusion.9.left_ref, bf16[2688,512]{1,0:T(8,128)(2,1)S(1)} %pad_maximum_fusion.right_ref), custom_call_target="tpu_custom_call" | custom-call | flops 1409286144 | bytes 6000000 | tf_op jit(solution)/shard_map/pallas_call | solution.py:84
  79.1 7.1 %collective-permute-done.17 = bf16[8,16,2688]{2,1,0:T(8,128)(2,1)S(1)} collective-permute-done((bf16[8,16,2688]{2,1,0:T(8,128)(2,1)S(1)}, bf16[8,16,2688]{2,1,0:T(8,128)(2,1)S(1)}, u32[]{:S(2)}, u32[]{:S(2)}) %collective-permute-start.17) | collective-permute-done | bytes 688160 | tf_op jit(solution)/shard_map/ppermute | solution.py:38
  86.2 3.8 %collective-permute-done.19 = bf16[8,16,2688]{2,1,0:T(8,128)(2,1)S(1)} collective-permute-done((bf16[8,16,2688]{2,1,0:T(8,128)(2,1)S(1)}, bf16[8,16,2688]{2,1,0:T(8,128)(2,1)S(1)}, u32[]{:S(2)}, u32[]{:S(2)}) %collective-permute-start.19) | collective-permute-done | bytes 688160 | tf_op jit(solution)/shard_map/ppermute | solution.py:38
  90.4 3.3 %collective-permute-start.20 = (bf16[2,16,2688]{2,1,0:T(8,128)(2,1)S(1)}, bf16[2,16,2688]{2,1,0:T(8,128)(2,1)S(1)}, u32[]{:S(2)}, u32[]{:S(2)}) collective-permute-start(bf16[2,16,2688]{2,1,0:T(8,128)(2,1)S(1)} %get-tuple-element.41), channel_id=1, source_target_pairs={{0,32},{1,9},{2,34},{3,11},{4,36},{5,13},{6,38},{7,15},{8,40},{9,1... | collective-permute-start | bytes 516104 | tf_op jit(solution)/shard_map/ppermute | solution.py:38
  99.5 3.6 %collective-permute-done.21 = bf16[2,16,2688]{2,1,0:T(8,128)(2,1)S(1)} collective-permute-done((bf16[2,16,2688]{2,1,0:T(8,128)(2,1)S(1)}, bf16[2,16,2688]{2,1,0:T(8,128)(2,1)S(1)}, u32[]{:S(2)}, u32[]{:S(2)}) %collective-permute-start.21) | collective-permute-done | bytes 172064 | tf_op jit(solution)/shard_map/ppermute | solution.py:38
  103.3 2.5 %collective-permute-start.23 = (bf16[16,2688]{1,0:T(8,128)(2,1)S(1)}, bf16[16,2688]{1,0:T(8,128)(2,1)S(1)}, u32[]{:S(2)}, u32[]{:S(2)}) collective-permute-start(bf16[16,2688]{1,0:T(8,128)(2,1)S(1)} %get-tuple-element.45), channel_id=1, source_target_pairs={{0,64},{1,65},{2,66},{3,67},{4,68},{5,69},{6,70},{7,71},{8,72},{9,... | collective-permute-start | bytes 258056 | tf_op jit(solution)/shard_map/ppermute | solution.py:38
  123.6 3.3 %collective-permute-start.33 = (bf16[4,16,5376]{2,1,0:T(8,128)(2,1)S(1)}, bf16[4,16,5376]{2,1,0:T(8,128)(2,1)}, u32[]{:S(2)}, u32[]{:S(2)}) collective-permute-start(bf16[4,16,5376]{2,1,0:T(8,128)(2,1)S(1)} %pad_maximum_fusion.2.refs_0_), channel_id=1, source_target_pairs={{0,4},{1,17},{2,6},{3,19},{4,8},{5,21},{6,10},{7,23},{8,12},{9,25}... | collective-permute-start | bytes 2064392 | tf_op jit(solution)/shard_map/ppermute | solution.py:38
  130.3 6.5 %collective-permute-done.30 = bf16[1,16,5376]{2,1,0:T(8,128)(2,1)S(1)} collective-permute-done((bf16[1,16,5376]{2,1,0:T(8,128)(2,1)S(1)}, bf16[1,16,5376]{2,1,0:T(8,128)(2,1)S(1)}, u32[]{:S(2)}, u32[]{:S(2)}) %collective-permute-start.30) | collective-permute-done | bytes 172064 | tf_op jit(solution)/shard_map/ppermute | solution.py:38
  139.3 3.5 %convolution_convert_fusion = bf16[512,512]{1,0:T(8,128)(2,1)S(1)} fusion(bf16[2688,512]{1,0:T(8,128)(2,1)S(1)} %pad_maximum_fusion.right_ref, bf16[512,2688]{1,0:T(8,128)(2,1)} %copy-done.1), kind=kOutput, calls=%fused_computation.29 | convolution fusion | flops 1409548288 | bytes 6029312 | tf_op jit(solution)/shard_map/dot_general | solution.py:262
  148.4 2.9 %collective-permute-done.36.refs_5_ = bf16[4,16,5376]{2,1,0:T(8,128)(2,1)} collective-permute-done((bf16[4,16,5376]{2,1,0:T(8,128)(2,1)}, bf16[4,16,5376]{2,1,0:T(8,128)(2,1)}, u32[]{:S(2)}, u32[]{:S(2)}) %collective-permute-start.36) | collective-permute-done | bytes 688160 | tf_op jit(solution)/shard_map/ppermute | solution.py:38
  151.3 4.3 %fusion.10 = f32[512,512]{1,0:T(8,128)S(1)} fusion(bf16[2688,512]{1,0:T(8,128)(2,1)S(1)} %pad_maximum_fusion.right_ref, bf16[512,5376]{1,0:T(8,128)(2,1)} %param.10, pred[]{:T(512)S(6)} %eq.31), kind=kOutput, calls=%fused_computation.39 | convolution fusion | flops 1410662400 | bytes 9306113 | tf_op jit(solution)/shard_map/dot_general | solution.py:263
  158.6 4.2 %shard_map.138.earlier_ref = bf16[512,5376]{1,0:T(8,128)(2,1)} custom-call(s32[24]{0:T(128)S(1)} %pad_add_fusion.1.rows_ref, bf16[4,16,5376]{2,1,0:T(8,128)(2,1)S(1)} %pad_maximum_fusion.2.refs_0_, bf16[4,16,5376]{2,1,0:T(8,128)(2,1)} %constant_dynamic-update-slice_fusion.1.refs_1_, bf16[4,16,5376]{2,1,0:T(8,128)(2,1)} %collective-permute-done.33.refs_2_, ...), custom_call_target="tpu_custom_call" | custom-call | bytes 8400000 | tf_op jit(solution)/shard_map/pallas_call | solution.py:129
  162.8 3.1 %collective-permute-done.38.refs_1_ = bf16[4,16,5376]{2,1,0:T(8,128)(2,1)S(1)} collective-permute-done((bf16[4,16,5376]{2,1,0:T(8,128)(2,1)}, bf16[4,16,5376]{2,1,0:T(8,128)(2,1)S(1)}, u32[]{:S(2)}, u32[]{:S(2)}) %collective-permute-start.38) | collective-permute-done | bytes 688160 | tf_op jit(solution)/shard_map/ppermute | solution.py:38
  (145 shorter events, 73.4 us)
Async XLA Ops:
  2.7 13.0 %collective-permute-start = (bf16[80,2688]{1,0:T(8,128)(2,1)}, bf16[80,2688]{1,0:T(8,128)(2,1)S(1)}, u32[]{:S(2)}, u32[]{:S(2)}) collective-permute-start(bf16[80,2688]{1,0:T(8,128)(2,1)} %dynamic-slice_select_fusion), channel_id=1, source_target_pairs={{0,2},{1,3},{2,0},{3,1},{4,6},{5,7},{6,4},{7,5},{8,10},{9,11},{10,... | collective-permute-start | bytes 1290248 | tf_op jit(solution)/shard_map/ppermute | solution.py:38
  5.8 28.3 %collective-permute-start.5 = (bf16[512,512]{0,1:T(8,128)(2,1)S(1)}, bf16[512,512]{0,1:T(8,128)(2,1)S(1)}, u32[]{:S(2)}, u32[]{:S(2)}) collective-permute-start(bf16[512,512]{0,1:T(8,128)(2,1)S(1)} %copy.18), channel_id=1, source_target_pairs={{0,2},{1,3},{2,0},{3,1},{4,6},{5,7},{6,4},{7,5},{8,10},{9,11},{10,... | collective-permute-start | bytes 1572872 | tf_op jit(solution)/shard_map/ppermute | solution.py:38
  7.7 26.4 %collective-permute-start.4 = (bf16[192,2688]{1,0:T(8,128)(2,1)S(1)}, bf16[192,2688]{1,0:T(8,128)(2,1)S(1)}, u32[]{:S(2)}, u32[]{:S(2)}) collective-permute-start(bf16[192,2688]{1,0:T(8,128)(2,1)S(1)} %slice_select_fusion.1), channel_id=1, source_target_pairs={{0,66},{1,67},{2,64},{3,65},{4,70},{5,71},{6,68},{7,69},{8,74},{9,... | collective-permute-start | bytes 3096584 | tf_op jit(solution)/shard_map/ppermute | solution.py:38
  15.6 14.0 %collective-permute-start.3 = (bf16[80,2688]{1,0:T(8,128)(2,1)S(1)}, bf16[80,2688]{1,0:T(8,128)(2,1)S(1)}, u32[]{:S(2)}, u32[]{:S(2)}) collective-permute-start(bf16[80,2688]{1,0:T(8,128)(2,1)S(1)} %collective-permute-done), channel_id=1, source_target_pairs={{0,12},{1,49},{2,14},{3,51},{4,0},{5,53},{6,2},{7,55},{8,4},{9,57}... | collective-permute-start | bytes 1290248 | tf_op jit(solution)/shard_map/ppermute | solution.py:38
  16.5 13.2 %collective-permute-start.2 = (bf16[80,2688]{1,0:T(8,128)(2,1)S(1)}, bf16[80,2688]{1,0:T(8,128)(2,1)S(1)}, u32[]{:S(2)}, u32[]{:S(2)}) collective-permute-start(bf16[80,2688]{1,0:T(8,128)(2,1)S(1)} %collective-permute-done), channel_id=1, source_target_pairs={{0,8},{1,33},{2,10},{3,35},{4,12},{5,37},{6,14},{7,39},{8,0},{9,41... | collective-permute-start | bytes 1290248 | tf_op jit(solution)/shard_map/ppermute | solution.py:38
  17.5 13.0 %collective-permute-start.1 = (bf16[80,2688]{1,0:T(8,128)(2,1)S(1)}, bf16[80,2688]{1,0:T(8,128)(2,1)S(1)}, u32[]{:S(2)}, u32[]{:S(2)}) collective-permute-start(bf16[80,2688]{1,0:T(8,128)(2,1)S(1)} %collective-permute-done), channel_id=1, source_target_pairs={{0,4},{1,17},{2,6},{3,19},{4,8},{5,21},{6,10},{7,23},{8,12},{9,25}... | collective-permute-start | bytes 1290248 | tf_op jit(solution)/shard_map/ppermute | solution.py:38
  64.3 11.0 %collective-permute-start.18 = (bf16[8,16,2688]{2,1,0:T(8,128)(2,1)S(1)}, bf16[8,16,2688]{2,1,0:T(8,128)(2,1)S(1)}, u32[]{:S(2)}, u32[]{:S(2)}) collective-permute-start(bf16[8,16,2688]{2,1,0:T(8,128)(2,1)S(1)} %get-tuple-element.23), channel_id=1, source_target_pairs={{0,4},{1,17},{2,6},{3,19},{4,8},{5,21},{6,10},{7,23},{8,12},{9,25}... | collective-permute-start | bytes 2064392 | tf_op jit(solution)/shard_map/ppermute | solution.py:38
  65.0 30.7 %collective-permute-start.11 = (bf16[8,16,2688]{2,1,0:T(8,128)(2,1)S(1)}, bf16[8,16,2688]{2,1,0:T(8,128)(2,1)S(1)}, u32[]{:S(2)}, u32[]{:S(2)}) collective-permute-start(bf16[8,16,2688]{2,1,0:T(8,128)(2,1)S(1)} %get-tuple-element.17), channel_id=1, source_target_pairs={{0,4},{1,17},{2,6},{3,19},{4,8},{5,21},{6,10},{7,23},{8,12},{9,25}... | collective-permute-start | bytes 2064392 | tf_op jit(solution)/shard_map/ppermute | solution.py:38
  66.7 12.1 %collective-permute-start.12 = (bf16[8,16,2688]{2,1,0:T(8,128)(2,1)S(1)}, bf16[8,16,2688]{2,1,0:T(8,128)(2,1)S(1)}, u32[]{:S(2)}, u32[]{:S(2)}) collective-permute-start(bf16[8,16,2688]{2,1,0:T(8,128)(2,1)S(1)} %get-tuple-element.19), channel_id=1, source_target_pairs={{0,12},{1,49},{2,14},{3,51},{4,0},{5,53},{6,2},{7,55},{8,4},{9,57}... | collective-permute-start | bytes 2064392 | tf_op jit(solution)/shard_map/ppermute | solution.py:38
  67.2 19.0 %collective-permute-start.17 = (bf16[8,16,2688]{2,1,0:T(8,128)(2,1)S(1)}, bf16[8,16,2688]{2,1,0:T(8,128)(2,1)S(1)}, u32[]{:S(2)}, u32[]{:S(2)}) collective-permute-start(bf16[8,16,2688]{2,1,0:T(8,128)(2,1)S(1)} %get-tuple-element.21), channel_id=1, source_target_pairs={{0,12},{1,49},{2,14},{3,51},{4,0},{5,53},{6,2},{7,55},{8,4},{9,57}... | collective-permute-start | bytes 2064392 | tf_op jit(solution)/shard_map/ppermute | solution.py:38
  75.5 14.6 %collective-permute-start.19 = (bf16[8,16,2688]{2,1,0:T(8,128)(2,1)S(1)}, bf16[8,16,2688]{2,1,0:T(8,128)(2,1)S(1)}, u32[]{:S(2)}, u32[]{:S(2)}) collective-permute-start(bf16[8,16,2688]{2,1,0:T(8,128)(2,1)S(1)} %add_convert_fusion.1), channel_id=1, source_target_pairs={{0,4},{1,17},{2,6},{3,19},{4,8},{5,21},{6,10},{7,23},{8,12},{9,25}... | collective-permute-start | bytes 2064392 | tf_op jit(solution)/shard_map/ppermute | solution.py:38
  79.0 16.6 %collective-permute-start.13 = (bf16[8,16,2688]{2,1,0:T(8,128)(2,1)S(1)}, bf16[8,16,2688]{2,1,0:T(8,128)(2,1)S(1)}, u32[]{:S(2)}, u32[]{:S(2)}) collective-permute-start(bf16[8,16,2688]{2,1,0:T(8,128)(2,1)S(1)} %add_convert_fusion.3), channel_id=1, source_target_pairs={{0,12},{1,49},{2,14},{3,51},{4,0},{5,53},{6,2},{7,55},{8,4},{9,57}... | collective-permute-start | bytes 2064392 | tf_op jit(solution)/shard_map/ppermute | solution.py:38
  90.4 9.1 %collective-permute-start.20 = (bf16[2,16,2688]{2,1,0:T(8,128)(2,1)S(1)}, bf16[2,16,2688]{2,1,0:T(8,128)(2,1)S(1)}, u32[]{:S(2)}, u32[]{:S(2)}) collective-permute-start(bf16[2,16,2688]{2,1,0:T(8,128)(2,1)S(1)} %get-tuple-element.41), channel_id=1, source_target_pairs={{0,32},{1,9},{2,34},{3,11},{4,36},{5,13},{6,38},{7,15},{8,40},{9,1... | collective-permute-start | bytes 516104 | tf_op jit(solution)/shard_map/ppermute | solution.py:38
  96.0 9.7 %collective-permute-start.14 = (bf16[2,16,2688]{2,1,0:T(8,128)(2,1)S(1)}, bf16[2,16,2688]{2,1,0:T(8,128)(2,1)S(1)}, u32[]{:S(2)}, u32[]{:S(2)}) collective-permute-start(bf16[2,16,2688]{2,1,0:T(8,128)(2,1)S(1)} %get-tuple-element.38), channel_id=1, source_target_pairs={{0,32},{1,9},{2,34},{3,11},{4,36},{5,13},{6,38},{7,15},{8,40},{9,1... | collective-permute-start | bytes 516104 | tf_op jit(solution)/shard_map/ppermute | solution.py:38
  116.4 10.4 %collective-permute-start.29 = (bf16[1,16,5376]{2,1,0:T(8,128)(2,1)S(1)}, bf16[1,16,5376]{2,1,0:T(8,128)(2,1)S(1)}, u32[]{:S(2)}, u32[]{:S(2)}) collective-permute-start(bf16[1,16,5376]{2,1,0:T(8,128)(2,1)S(1)} %get-tuple-element.26), channel_id=1, source_target_pairs={{0,64},{1,65},{2,66},{3,67},{4,68},{5,69},{6,70},{7,71},{8,72},{9,... | collective-permute-start | bytes 516104 | tf_op jit(solution)/shard_map/ppermute | solution.py:38
  123.6 22.9 %collective-permute-start.33 = (bf16[4,16,5376]{2,1,0:T(8,128)(2,1)S(1)}, bf16[4,16,5376]{2,1,0:T(8,128)(2,1)}, u32[]{:S(2)}, u32[]{:S(2)}) collective-permute-start(bf16[4,16,5376]{2,1,0:T(8,128)(2,1)S(1)} %pad_maximum_fusion.2.refs_0_), channel_id=1, source_target_pairs={{0,4},{1,17},{2,6},{3,19},{4,8},{5,21},{6,10},{7,23},{8,12},{9,25}... | collective-permute-start | bytes 2064392 | tf_op jit(solution)/shard_map/ppermute | solution.py:38
  126.9 11.3 %collective-permute-start.32 = (bf16[1,16,5376]{2,1,0:T(8,128)(2,1)S(1)}, bf16[1,16,5376]{2,1,0:T(8,128)(2,1)S(1)}, u32[]{:S(2)}, u32[]{:S(2)}) collective-permute-start(bf16[1,16,5376]{2,1,0:T(8,128)(2,1)S(1)} %collective-permute-done.29), channel_id=1, source_target_pairs={{0,48},{1,13},{2,50},{3,15},{4,52},{5,1},{6,54},{7,3},{8,56},{9,5}... | collective-permute-start | bytes 516104 | tf_op jit(solution)/shard_map/ppermute | solution.py:38
  128.1 9.4 %collective-permute-start.31 = (bf16[1,16,5376]{2,1,0:T(8,128)(2,1)S(1)}, bf16[1,16,5376]{2,1,0:T(8,128)(2,1)S(1)}, u32[]{:S(2)}, u32[]{:S(2)}) collective-permute-start(bf16[1,16,5376]{2,1,0:T(8,128)(2,1)S(1)} %collective-permute-done.29), channel_id=1, source_target_pairs={{0,32},{1,9},{2,34},{3,11},{4,36},{5,13},{6,38},{7,15},{8,40},{9,1... | collective-permute-start | bytes 516104 | tf_op jit(solution)/shard_map/ppermute | solution.py:38
  138.9 12.5 %collective-permute-start.36 = (bf16[4,16,5376]{2,1,0:T(8,128)(2,1)}, bf16[4,16,5376]{2,1,0:T(8,128)(2,1)}, u32[]{:S(2)}, u32[]{:S(2)}) collective-permute-start(bf16[4,16,5376]{2,1,0:T(8,128)(2,1)} %constant_dynamic-update-slice_fusion.1.refs_1_), channel_id=1, source_target_pairs={{0,12},{1,49},{2,14},{3,51},{4,0},{5,53},{6,2},{7,55},{8,4},{9,57}... | collective-permute-start | bytes 2064392 | tf_op jit(solution)/shard_map/ppermute | solution.py:38
  142.8 12.8 %collective-permute-start.10 = (bf16[512,512]{1,0:T(8,128)(2,1)S(1)}, bf16[512,512]{1,0:T(8,128)(2,1)S(1)}, u32[]{:S(2)}, u32[]{:S(2)}) collective-permute-start(bf16[512,512]{1,0:T(8,128)(2,1)S(1)} %convolution_convert_fusion), channel_id=1, source_target_pairs={{0,2},{1,3},{2,0},{3,1},{4,6},{5,7},{6,4},{7,5},{8,10},{9,11},{10,... | collective-permute-start | bytes 1572872 | tf_op jit(solution)/shard_map/ppermute | solution.py:38
  142.9 15.7 %collective-permute-start.35 = (bf16[4,16,5376]{2,1,0:T(8,128)(2,1)S(1)}, bf16[4,16,5376]{2,1,0:T(8,128)(2,1)S(1)}, u32[]{:S(2)}, u32[]{:S(2)}) collective-permute-start(bf16[4,16,5376]{2,1,0:T(8,128)(2,1)S(1)} %pad_maximum_fusion.2.refs_0_), channel_id=1, source_target_pairs={{0,12},{1,49},{2,14},{3,51},{4,0},{5,53},{6,2},{7,55},{8,4},{9,57}... | collective-permute-start | bytes 2064392 | tf_op jit(solution)/shard_map/ppermute | solution.py:38
  144.3 14.3 %collective-permute-start.34 = (bf16[4,16,5376]{2,1,0:T(8,128)(2,1)}, bf16[4,16,5376]{2,1,0:T(8,128)(2,1)S(1)}, u32[]{:S(2)}, u32[]{:S(2)}) collective-permute-start(bf16[4,16,5376]{2,1,0:T(8,128)(2,1)} %constant_dynamic-update-slice_fusion.1.refs_1_), channel_id=1, source_target_pairs={{0,4},{1,17},{2,6},{3,19},{4,8},{5,21},{6,10},{7,23},{8,12},{9,25}... | collective-permute-start | bytes 2064392 | tf_op jit(solution)/shard_map/ppermute | solution.py:38
  146.5 16.4 %collective-permute-start.37 = (bf16[4,16,5376]{2,1,0:T(8,128)(2,1)}, bf16[4,16,5376]{2,1,0:T(8,128)(2,1)S(1)}, u32[]{:S(2)}, u32[]{:S(2)}) collective-permute-start(bf16[4,16,5376]{2,1,0:T(8,128)(2,1)} %collective-permute-done.33.refs_2_), channel_id=1, source_target_pairs={{0,4},{1,17},{2,6},{3,19},{4,8},{5,21},{6,10},{7,23},{8,12},{9,25}... | collective-permute-start | bytes 2064392 | tf_op jit(solution)/shard_map/ppermute | solution.py:38
  151.3 14.6 %collective-permute-start.38 = (bf16[4,16,5376]{2,1,0:T(8,128)(2,1)}, bf16[4,16,5376]{2,1,0:T(8,128)(2,1)S(1)}, u32[]{:S(2)}, u32[]{:S(2)}) collective-permute-start(bf16[4,16,5376]{2,1,0:T(8,128)(2,1)} %collective-permute-done.36.refs_5_), channel_id=1, source_target_pairs={{0,12},{1,49},{2,14},{3,51},{4,0},{5,53},{6,2},{7,55},{8,4},{9,57}... | collective-permute-start | bytes 2064392 | tf_op jit(solution)/shard_map/ppermute | solution.py:38
  (24 other events, 158.0 us)

commit v4 on v3

--- a/solution.py
+++ b/solution.py
@@ -80,7 +80,7 @@
 def gradient_pieces(rows, left, right):
     heads, tokens = left.shape
     columns = right.shape[0]
-    width = 384
+    width = 896
     return pl.pallas_call(
         gradient_kernel,
         grid_spec=pltpu.PrefetchScalarGridSpec(
@@ -99,6 +99,33 @@
             flops=2 * 512 * tokens * columns, bytes_accessed=6_000_000, transcendentals=0
         ),
     )(rows, left, right)
+
+
+def whole(kernel, operands, outs, limit, flops=0, loose=(), scalars=()):
+    vmem = pl.BlockSpec(memory_space=pltpu.VMEM)
+
+    def body(*refs):
+        count = len(scalars) + len(operands)
+        kernel(*refs[:count], *refs[count + len(loose) :])
+
+    moved = sum(2 * v.size for v in operands)
+    return pl.pallas_call(
+        body,
+        in_specs=[pl.BlockSpec(memory_space=pltpu.SMEM)] * len(scalars)
+        + [vmem] * len(operands)
+        + [pl.BlockSpec(memory_space=pl.ANY)] * len(loose),
+        out_specs=[vmem] * len(outs),
+        out_shape=[jax.ShapeDtypeStruct(shape, dtype) for shape, dtype in outs],
+        compiler_params=pltpu.CompilerParams(vmem_limit_bytes=limit * 1024 * 1024),
+        cost_estimate=pl.CostEstimate(flops=flops, bytes_accessed=moved, transcendentals=0),
+    )(*scalars, *operands, *loose)
+
+
+def join_kernel(*refs):
+    *pieces, low_ref, high_ref = refs
+    for t in range(4):
+        low_ref[t : t + 1] = pieces[t][...]
+        high_ref[t : t + 1] = pieces[4 + t][...]
 
 
 def place_kernel(rows_ref, *refs):
@@ -172,8 +199,10 @@
     left_rows = (((0,), (1,)), ((), ()))
     pre_pair = lax.dot_general(near, attention, left_rows, preferred_element_type=f32)
     pre_pair = pre_pair + lax.dot_general(far, far_attention, left_rows, preferred_element_type=f32)
-    mine = lax.dynamic_slice_in_dim(pre_pair, c * part, part, 0)
-    other = lax.dynamic_slice_in_dim(pre_pair, (1 - c) * part, part, 0)
+    lower, upper = pre_pair[:part], pre_pair[part:]
+    mine = jnp.where(c == 0, lower, upper)
+    other = jnp.where(c == 0, upper, lower)
+    mine, other = lax.optimization_barrier((mine, other.astype(bf16)))
     pre = mine + flip_core(other.astype(bf16)).astype(f32)
 
     scaled = cotangent.T.astype(f32) * gain
@@ -242,9 +271,16 @@
 
     own = new_master.astype(bf16)
     other = flip_z(own, 0, 1)
-    low = jnp.concatenate([own] + [along_second(own, t) for t in (1, 2, 3)])
+    near_blocks = [along_second(own, t) for t in (1, 2, 3)]
+    peer_blocks = [along_second(other, t) for t in (1, 2, 3)]
+    low, high = whole(
+        join_kernel,
+        [own] + near_blocks + [other] + peer_blocks,
+        [((4,) + own.shape[1:], bf16)] * 2,
+        16,
+        loose=[],
+    )
     low_below, low_above = along_first(low, 1), along_first(low, -1)
-    high = jnp.concatenate([other] + [along_second(other, t) for t in (1, 2, 3)])
     high_below, high_above = along_first(high, 1), along_first(high, -1)
     low_far, high_far = along_first(low_below, 1), along_first(high_above, -1)
     s_, dz_, t_ = jnp.meshgrid(*(jnp.arange(n) for n in (4, 2, 4)), indexing="ij")

time: 168 us -> 162 us (0.964)
  local copies, waits for them, and re-layouts: 10.3 us -> 3.07 us
  other arithmetic: 18.5 us -> 21 us
  waiting for transfers between devices: 62.7 us -> 60.6 us
    unnamed x26 -> x17, local copies, waits for them, and re-layouts: 6.76 us -> 1.48 us
    pallas_call x2, Pallas kernels: 8.38 us -> 6.16 us  [gradient_pieces(): pl.pallas_call(gradient_kernel, grid_spec=pltpu.PrefetchScalarGridSpec(nu...]
    ppermute x39, waiting for transfers between devices: 62.7 us -> 60.6 us  [move(): lax.ppermute(value, axes, [(flat(p), flat(target(*p))) for p in places])]
  transfers between devices with their start and end apart: 39 -> 39, of which waited for: 25 -> 28; matrix products, arithmetic and copies ran while one was open for 15% -> 14% of each run, Pallas kernels for 5% -> 5%
where the time goes in v4:
time: 162 us
  waiting for transfers between devices  60.6 us (37%)
  starting transfers between devices  48.6 us (30%)
  other arithmetic  21 us (13%)
  matrix products  13.8 us (9%)
  Pallas kernels  13 us (8%)
  local copies, waits for them, and re-layouts  3.07 us (2%)
    ppermute x39, waiting for transfers between devices, move(): lax.ppermute(value, axes, [(flat(p), flat(target(*p))) for p in places])  60.6 us
    ppermute x39, starting transfers between devices, move(): lax.ppermute(value, axes, [(flat(p), flat(target(*p))) for p in places])  48.6 us
    pallas_call x2, Pallas kernels, gradient_pieces(): pl.pallas_call(gradient_kernel, grid_spec=pltpu.PrefetchScalarGridSpec(nu...  6.16 us
    pallas_call x2, Pallas kernels, place_rows(): pl.pallas_call(place_more_kernel if before else place_kernel, grid_spec=p...  5.91 us
    dot_general x1, matrix products, local(): lax.dot_general(near, attention, left_rows, preferred_element_type=f32)  4.37 us
    dot_general x1, matrix products, local(): lax.dot_general(pair, near, to_heads, preferred_element_type=f32)  4.33 us
    convert_element_type x1, other arithmetic, local(): pre_grad = (inv_rms * scaled - pre * inv_rms ** 3 * proj).astype(bf16)  3.95 us
    dot_general x1, matrix products, local(): lax.dot_general(pair, far, to_heads, preferred_element_type=f32)  3.48 us
  transfers between devices with their start and end apart: 39, of which 28 were waited for; matrix products, arithmetic and copies ran while one was open for 14% of the time, Pallas kernels for 5%

profile of v4, /device:TPU:6, one launch (start us, length us, event | category | flops | bytes accessed | tf_op | source)
XLA Modules:
  0.0 161.5 jit_solution(6374307974733045220)
XLA Ops:
  7.7 4.1 %collective-permute-start.4 = (bf16[192,2688]{1,0:T(8,128)(2,1)S(1)}, bf16[192,2688]{1,0:T(8,128)(2,1)S(1)}, u32[]{:S(2)}, u32[]{:S(2)}) collective-permute-start(bf16[192,2688]{1,0:T(8,128)(2,1)S(1)} %slice_select_fusion.2), channel_id=1, source_target_pairs={{0,66},{1,67},{2,64},{3,65},{4,70},{5,71},{6,68},{7,69},{8,74},{9,... | collective-permute-start | bytes 3096584 | tf_op jit(solution)/shard_map/ppermute | solution.py:38
  11.8 3.9 %collective-permute-done = bf16[80,2688]{1,0:T(8,128)(2,1)S(1)} collective-permute-done((bf16[80,2688]{1,0:T(8,128)(2,1)}, bf16[80,2688]{1,0:T(8,128)(2,1)S(1)}, u32[]{:S(2)}, u32[]{:S(2)}) %collective-permute-start) | collective-permute-done | bytes 430112 | tf_op jit(solution)/shard_map/ppermute | solution.py:38
  19.7 4.4 %fusion.11 = f32[2688,512]{1,0:T(8,128)S(1)} fusion(bf16[512,512]{1,0:T(8,128)(2,1)} %param.9, bf16[512,5376]{1,0:T(8,128)(2,1)} %param.10, pred[]{:T(512)S(6)} %eq.34), kind=kOutput, calls=%fused_computation.40 | convolution fusion | flops 1410662400 | bytes 11534337 | tf_op jit(solution)/shard_map/dot_general | solution.py:200
  24.1 5.6 %collective-permute-done.3 = bf16[80,2688]{1,0:T(8,128)(2,1)S(1)} collective-permute-done((bf16[80,2688]{1,0:T(8,128)(2,1)S(1)}, bf16[80,2688]{1,0:T(8,128)(2,1)S(1)}, u32[]{:S(2)}, u32[]{:S(2)}) %collective-permute-start.3) | collective-permute-done | bytes 430112 | tf_op jit(solution)/shard_map/ppermute | solution.py:38
  31.0 3.0 %collective-permute-done.4 = bf16[192,2688]{1,0:T(8,128)(2,1)S(1)} collective-permute-done((bf16[192,2688]{1,0:T(8,128)(2,1)S(1)}, bf16[192,2688]{1,0:T(8,128)(2,1)S(1)}, u32[]{:S(2)}, u32[]{:S(2)}) %collective-permute-start.4) | collective-permute-done | bytes 1032224 | tf_op jit(solution)/shard_map/ppermute | solution.py:38
  38.8 2.6 %collective-permute-done.6 = bf16[1344,512]{1,0:T(8,128)(2,1)} collective-permute-done((bf16[1344,512]{1,0:T(8,128)(2,1)}, bf16[1344,512]{1,0:T(8,128)(2,1)}, u32[]{:S(2)}, u32[]{:S(2)}) %collective-permute-start.6) | collective-permute-done | bytes 1376288 | tf_op jit(solution)/shard_map/ppermute | solution.py:38
  45.3 3.6 %collective-permute-done.8 = f32[2,512]{1,0:T(2,128)S(1)} collective-permute-done((f32[2,512]{1,0:T(2,128)S(1)}, f32[2,512]{1,0:T(2,128)S(1)}, u32[]{:S(2)}, u32[]{:S(2)}) %collective-permute-start.8) | collective-permute-done | bytes 4128 | tf_op jit(solution)/shard_map/ppermute | solution.py:38
  48.9 4.0 %fusion.2 = (bf16[1344,512]{1,0:T(8,128)(2,1)}, bf16[512,1344]{0,1:T(8,128)(2,1)}) fusion(bf16[512,1344]{0,1:T(8,128)(2,1)} %param.13, f32[512]{0:T(512)S(1)} %bitcast.92, f32[512]{0:T(512)S(1)} %bitcast.90, f32[512]{0:T(512)S(1)} %bitcast.91, f32[1344]{0:T(1024)S(1)} %dynamic_slice.26, f32[1344,512]{1,0:T(8,128)S(1)} %slice_select_fusion.1, ...), kind=kLoop, calls=%fused_computation.10 | loop fusion | flops 9633792 | bytes 9645312 | tf_op jit(solution)/shard_map/convert_element_type | solution.py:215
  58.7 3.1 %shard_map.137 = (bf16[8,16,2688]{2,1,0:T(8,128)(2,1)S(1)}, bf16[8,16,2688]{2,1,0:T(8,128)(2,1)S(1)}, bf16[8,16,2688]{2,1,0:T(8,128)(2,1)S(1)}, bf16[8,16,2688]{2,1,0:T(8,128)(2,1)S(1)}) custom-call(s32[32]{0:T(128)S(1)} %pad_add_fusion.2.rows_ref, bf16[1024,512]{1,0:T(8,128)(2,1)S(1)} %fusion.9.left_ref, bf16[2688,512]{1,0:T(8,128)(2,1)S(1)} %pad_maximum_fusion.right_ref), custom_call_target="tpu_custom_call" | custom-call | flops 1409286144 | bytes 6000000 | tf_op jit(solution)/shard_map/pallas_call | solution.py:84
  66.0 3.1 %shard_map.136 = (bf16[8,16,2688]{2,1,0:T(8,128)(2,1)S(1)}, bf16[8,16,2688]{2,1,0:T(8,128)(2,1)S(1)}, bf16[8,16,2688]{2,1,0:T(8,128)(2,1)S(1)}, bf16[8,16,2688]{2,1,0:T(8,128)(2,1)S(1)}) custom-call(s32[32]{0:T(128)S(1)} %pad_add_fusion.rows_ref, bf16[1024,512]{1,0:T(8,128)(2,1)S(1)} %fusion.9.left_ref, bf16[2688,512]{1,0:T(8,128)(2,1)S(1)} %pad_maximum_fusion.right_ref), custom_call_target="tpu_custom_call" | custom-call | flops 1409286144 | bytes 6000000 | tf_op jit(solution)/shard_map/pallas_call | solution.py:84
  69.1 3.7 %collective-permute-done.18 = bf16[8,16,2688]{2,1,0:T(8,128)(2,1)S(1)} collective-permute-done((bf16[8,16,2688]{2,1,0:T(8,128)(2,1)S(1)}, bf16[8,16,2688]{2,1,0:T(8,128)(2,1)S(1)}, u32[]{:S(2)}, u32[]{:S(2)}) %collective-permute-start.18) | collective-permute-done | bytes 688160 | tf_op jit(solution)/shard_map/ppermute | solution.py:38
  76.3 7.1 %collective-permute-done.17 = bf16[8,16,2688]{2,1,0:T(8,128)(2,1)S(1)} collective-permute-done((bf16[8,16,2688]{2,1,0:T(8,128)(2,1)S(1)}, bf16[8,16,2688]{2,1,0:T(8,128)(2,1)S(1)}, u32[]{:S(2)}, u32[]{:S(2)}) %collective-permute-start.17) | collective-permute-done | bytes 688160 | tf_op jit(solution)/shard_map/ppermute | solution.py:38
  83.4 4.1 %collective-permute-done.19 = bf16[8,16,2688]{2,1,0:T(8,128)(2,1)S(1)} collective-permute-done((bf16[8,16,2688]{2,1,0:T(8,128)(2,1)S(1)}, bf16[8,16,2688]{2,1,0:T(8,128)(2,1)S(1)}, u32[]{:S(2)}, u32[]{:S(2)}) %collective-permute-start.19) | collective-permute-done | bytes 688160 | tf_op jit(solution)/shard_map/ppermute | solution.py:38
  87.8 3.3 %collective-permute-start.20 = (bf16[2,16,2688]{2,1,0:T(8,128)(2,1)S(1)}, bf16[2,16,2688]{2,1,0:T(8,128)(2,1)S(1)}, u32[]{:S(2)}, u32[]{:S(2)}) collective-permute-start(bf16[2,16,2688]{2,1,0:T(8,128)(2,1)S(1)} %get-tuple-element.49), channel_id=1, source_target_pairs={{0,32},{1,9},{2,34},{3,11},{4,36},{5,13},{6,38},{7,15},{8,40},{9,1... | collective-permute-start | bytes 516104 | tf_op jit(solution)/shard_map/ppermute | solution.py:38
  94.4 2.5 %collective-permute-start.16 = (bf16[2,16,2688]{2,1,0:T(8,128)(2,1)S(1)}, bf16[2,16,2688]{2,1,0:T(8,128)(2,1)S(1)}, u32[]{:S(2)}, u32[]{:S(2)}) collective-permute-start(bf16[2,16,2688]{2,1,0:T(8,128)(2,1)S(1)} %get-tuple-element.47), channel_id=1, source_target_pairs={{0,48},{1,13},{2,50},{3,15},{4,52},{5,1},{6,54},{7,3},{8,56},{9,5}... | collective-permute-start | bytes 516104 | tf_op jit(solution)/shard_map/ppermute | solution.py:38
  97.0 3.6 %collective-permute-done.21 = bf16[2,16,2688]{2,1,0:T(8,128)(2,1)S(1)} collective-permute-done((bf16[2,16,2688]{2,1,0:T(8,128)(2,1)S(1)}, bf16[2,16,2688]{2,1,0:T(8,128)(2,1)S(1)}, u32[]{:S(2)}, u32[]{:S(2)}) %collective-permute-start.21) | collective-permute-done | bytes 172064 | tf_op jit(solution)/shard_map/ppermute | solution.py:38
  116.1 2.6 %collective-permute-done.29.refs_4_ = bf16[1,16,5376]{2,1,0:T(8,128)(2,1)S(1)} collective-permute-done((bf16[1,16,5376]{2,1,0:T(8,128)(2,1)S(1)}, bf16[1,16,5376]{2,1,0:T(8,128)(2,1)S(1)}, u32[]{:S(2)}, u32[]{:S(2)}) %collective-permute-start.29) | collective-permute-done | bytes 172064 | tf_op jit(solution)/shard_map/ppermute | solution.py:38
  125.7 2.7 %collective-permute-done.30.refs_5_ = bf16[1,16,5376]{2,1,0:T(8,128)(2,1)S(1)} collective-permute-done((bf16[1,16,5376]{2,1,0:T(8,128)(2,1)S(1)}, bf16[1,16,5376]{2,1,0:T(8,128)(2,1)S(1)}, u32[]{:S(2)}, u32[]{:S(2)}) %collective-permute-start.30) | collective-permute-done | bytes 172064 | tf_op jit(solution)/shard_map/ppermute | solution.py:38
  129.4 3.2 %collective-permute-start.33 = (bf16[4,16,5376]{2,1,0:T(8,128)(2,1)S(1)}, bf16[4,16,5376]{2,1,0:T(8,128)(2,1)}, u32[]{:S(2)}, u32[]{:S(2)}) collective-permute-start(bf16[4,16,5376]{2,1,0:T(8,128)(2,1)S(1)} %get-tuple-element.30.refs_0_), channel_id=1, source_target_pairs={{0,4},{1,17},{2,6},{3,19},{4,8},{5,21},{6,10},{7,23},{8,12},{9,25}... | collective-permute-start | bytes 2064392 | tf_op jit(solution)/shard_map/ppermute | solution.py:38
  133.0 3.5 %convolution_convert_fusion = bf16[512,512]{1,0:T(8,128)(2,1)S(1)} fusion(bf16[2688,512]{1,0:T(8,128)(2,1)S(1)} %pad_maximum_fusion.right_ref, bf16[512,2688]{1,0:T(8,128)(2,1)} %copy-done), kind=kOutput, calls=%fused_computation.30 | convolution fusion | flops 1409548288 | bytes 6029312 | tf_op jit(solution)/shard_map/dot_general | solution.py:298
  141.0 3.8 %collective-permute-start.37 = (bf16[4,16,5376]{2,1,0:T(8,128)(2,1)}, bf16[4,16,5376]{2,1,0:T(8,128)(2,1)S(1)}, u32[]{:S(2)}, u32[]{:S(2)}) collective-permute-start(bf16[4,16,5376]{2,1,0:T(8,128)(2,1)} %collective-permute-done.33.refs_2_), channel_id=1, source_target_pairs={{0,4},{1,17},{2,6},{3,19},{4,8},{5,21},{6,10},{7,23},{8,12},{9,25}... | collective-permute-start | bytes 2064392 | tf_op jit(solution)/shard_map/ppermute | solution.py:38
  145.0 4.3 %fusion.10 = f32[512,512]{1,0:T(8,128)S(1)} fusion(bf16[2688,512]{1,0:T(8,128)(2,1)S(1)} %pad_maximum_fusion.right_ref, bf16[512,5376]{1,0:T(8,128)(2,1)} %param.10, pred[]{:T(512)S(6)} %eq.34), kind=kOutput, calls=%fused_computation.39 | convolution fusion | flops 1410662400 | bytes 9306113 | tf_op jit(solution)/shard_map/dot_general | solution.py:299
  152.3 4.2 %shard_map.139.earlier_ref = bf16[512,5376]{1,0:T(8,128)(2,1)} custom-call(s32[24]{0:T(128)S(1)} %pad_add_fusion.1.rows_ref, bf16[4,16,5376]{2,1,0:T(8,128)(2,1)S(1)} %get-tuple-element.30.refs_0_, bf16[4,16,5376]{2,1,0:T(8,128)(2,1)} %get-tuple-element.31.refs_1_, bf16[4,16,5376]{2,1,0:T(8,128)(2,1)} %collective-permute-done.33.refs_2_, ...), custom_call_target="tpu_custom_call" | custom-call | bytes 8400000 | tf_op jit(solution)/shard_map/pallas_call | solution.py:156
  156.5 3.1 %collective-permute-done.38.refs_1_ = bf16[4,16,5376]{2,1,0:T(8,128)(2,1)S(1)} collective-permute-done((bf16[4,16,5376]{2,1,0:T(8,128)(2,1)}, bf16[4,16,5376]{2,1,0:T(8,128)(2,1)S(1)}, u32[]{:S(2)}, u32[]{:S(2)}) %collective-permute-start.38) | collective-permute-done | bytes 688160 | tf_op jit(solution)/shard_map/ppermute | solution.py:38
  (136 shorter events, 71.1 us)
Async XLA Ops:
  2.7 13.0 %collective-permute-start = (bf16[80,2688]{1,0:T(8,128)(2,1)}, bf16[80,2688]{1,0:T(8,128)(2,1)S(1)}, u32[]{:S(2)}, u32[]{:S(2)}) collective-permute-start(bf16[80,2688]{1,0:T(8,128)(2,1)} %dynamic-slice_select_fusion), channel_id=1, source_target_pairs={{0,2},{1,3},{2,0},{3,1},{4,6},{5,7},{6,4},{7,5},{8,10},{9,11},{10,... | collective-permute-start | bytes 1290248 | tf_op jit(solution)/shard_map/ppermute | solution.py:38
  5.8 28.3 %collective-permute-start.5 = (bf16[512,512]{0,1:T(8,128)(2,1)S(1)}, bf16[512,512]{0,1:T(8,128)(2,1)S(1)}, u32[]{:S(2)}, u32[]{:S(2)}) collective-permute-start(bf16[512,512]{0,1:T(8,128)(2,1)S(1)} %copy.18), channel_id=1, source_target_pairs={{0,2},{1,3},{2,0},{3,1},{4,6},{5,7},{6,4},{7,5},{8,10},{9,11},{10,... | collective-permute-start | bytes 1572872 | tf_op jit(solution)/shard_map/ppermute | solution.py:38
  7.7 26.4 %collective-permute-start.4 = (bf16[192,2688]{1,0:T(8,128)(2,1)S(1)}, bf16[192,2688]{1,0:T(8,128)(2,1)S(1)}, u32[]{:S(2)}, u32[]{:S(2)}) collective-permute-start(bf16[192,2688]{1,0:T(8,128)(2,1)S(1)} %slice_select_fusion.2), channel_id=1, source_target_pairs={{0,66},{1,67},{2,64},{3,65},{4,70},{5,71},{6,68},{7,69},{8,74},{9,... | collective-permute-start | bytes 3096584 | tf_op jit(solution)/shard_map/ppermute | solution.py:38
  15.6 14.0 %collective-permute-start.3 = (bf16[80,2688]{1,0:T(8,128)(2,1)S(1)}, bf16[80,2688]{1,0:T(8,128)(2,1)S(1)}, u32[]{:S(2)}, u32[]{:S(2)}) collective-permute-start(bf16[80,2688]{1,0:T(8,128)(2,1)S(1)} %collective-permute-done), channel_id=1, source_target_pairs={{0,12},{1,49},{2,14},{3,51},{4,0},{5,53},{6,2},{7,55},{8,4},{9,57}... | collective-permute-start | bytes 1290248 | tf_op jit(solution)/shard_map/ppermute | solution.py:38
  16.5 13.2 %collective-permute-start.2 = (bf16[80,2688]{1,0:T(8,128)(2,1)S(1)}, bf16[80,2688]{1,0:T(8,128)(2,1)S(1)}, u32[]{:S(2)}, u32[]{:S(2)}) collective-permute-start(bf16[80,2688]{1,0:T(8,128)(2,1)S(1)} %collective-permute-done), channel_id=1, source_target_pairs={{0,8},{1,33},{2,10},{3,35},{4,12},{5,37},{6,14},{7,39},{8,0},{9,41... | collective-permute-start | bytes 1290248 | tf_op jit(solution)/shard_map/ppermute | solution.py:38
  17.5 13.0 %collective-permute-start.1 = (bf16[80,2688]{1,0:T(8,128)(2,1)S(1)}, bf16[80,2688]{1,0:T(8,128)(2,1)S(1)}, u32[]{:S(2)}, u32[]{:S(2)}) collective-permute-start(bf16[80,2688]{1,0:T(8,128)(2,1)S(1)} %collective-permute-done), channel_id=1, source_target_pairs={{0,4},{1,17},{2,6},{3,19},{4,8},{5,21},{6,10},{7,23},{8,12},{9,25}... | collective-permute-start | bytes 1290248 | tf_op jit(solution)/shard_map/ppermute | solution.py:38
  61.8 11.0 %collective-permute-start.18 = (bf16[8,16,2688]{2,1,0:T(8,128)(2,1)S(1)}, bf16[8,16,2688]{2,1,0:T(8,128)(2,1)S(1)}, u32[]{:S(2)}, u32[]{:S(2)}) collective-permute-start(bf16[8,16,2688]{2,1,0:T(8,128)(2,1)S(1)} %get-tuple-element.29), channel_id=1, source_target_pairs={{0,4},{1,17},{2,6},{3,19},{4,8},{5,21},{6,10},{7,23},{8,12},{9,25}... | collective-permute-start | bytes 2064392 | tf_op jit(solution)/shard_map/ppermute | solution.py:38
  62.4 30.7 %collective-permute-start.11 = (bf16[8,16,2688]{2,1,0:T(8,128)(2,1)S(1)}, bf16[8,16,2688]{2,1,0:T(8,128)(2,1)S(1)}, u32[]{:S(2)}, u32[]{:S(2)}) collective-permute-start(bf16[8,16,2688]{2,1,0:T(8,128)(2,1)S(1)} %get-tuple-element.23), channel_id=1, source_target_pairs={{0,4},{1,17},{2,6},{3,19},{4,8},{5,21},{6,10},{7,23},{8,12},{9,25}... | collective-permute-start | bytes 2064392 | tf_op jit(solution)/shard_map/ppermute | solution.py:38
  63.9 12.1 %collective-permute-start.12 = (bf16[8,16,2688]{2,1,0:T(8,128)(2,1)S(1)}, bf16[8,16,2688]{2,1,0:T(8,128)(2,1)S(1)}, u32[]{:S(2)}, u32[]{:S(2)}) collective-permute-start(bf16[8,16,2688]{2,1,0:T(8,128)(2,1)S(1)} %get-tuple-element.25), channel_id=1, source_target_pairs={{0,12},{1,49},{2,14},{3,51},{4,0},{5,53},{6,2},{7,55},{8,4},{9,57}... | collective-permute-start | bytes 2064392 | tf_op jit(solution)/shard_map/ppermute | solution.py:38
  64.4 19.0 %collective-permute-start.17 = (bf16[8,16,2688]{2,1,0:T(8,128)(2,1)S(1)}, bf16[8,16,2688]{2,1,0:T(8,128)(2,1)S(1)}, u32[]{:S(2)}, u32[]{:S(2)}) collective-permute-start(bf16[8,16,2688]{2,1,0:T(8,128)(2,1)S(1)} %get-tuple-element.27), channel_id=1, source_target_pairs={{0,12},{1,49},{2,14},{3,51},{4,0},{5,53},{6,2},{7,55},{8,4},{9,57}... | collective-permute-start | bytes 2064392 | tf_op jit(solution)/shard_map/ppermute | solution.py:38
  72.9 14.6 %collective-permute-start.19 = (bf16[8,16,2688]{2,1,0:T(8,128)(2,1)S(1)}, bf16[8,16,2688]{2,1,0:T(8,128)(2,1)S(1)}, u32[]{:S(2)}, u32[]{:S(2)}) collective-permute-start(bf16[8,16,2688]{2,1,0:T(8,128)(2,1)S(1)} %add_convert_fusion.1), channel_id=1, source_target_pairs={{0,4},{1,17},{2,6},{3,19},{4,8},{5,21},{6,10},{7,23},{8,12},{9,25}... | collective-permute-start | bytes 2064392 | tf_op jit(solution)/shard_map/ppermute | solution.py:38
  76.2 16.9 %collective-permute-start.13 = (bf16[8,16,2688]{2,1,0:T(8,128)(2,1)S(1)}, bf16[8,16,2688]{2,1,0:T(8,128)(2,1)S(1)}, u32[]{:S(2)}, u32[]{:S(2)}) collective-permute-start(bf16[8,16,2688]{2,1,0:T(8,128)(2,1)S(1)} %add_convert_fusion.3), channel_id=1, source_target_pairs={{0,12},{1,49},{2,14},{3,51},{4,0},{5,53},{6,2},{7,55},{8,4},{9,57}... | collective-permute-start | bytes 2064392 | tf_op jit(solution)/shard_map/ppermute | solution.py:38
  87.8 9.1 %collective-permute-start.20 = (bf16[2,16,2688]{2,1,0:T(8,128)(2,1)S(1)}, bf16[2,16,2688]{2,1,0:T(8,128)(2,1)S(1)}, u32[]{:S(2)}, u32[]{:S(2)}) collective-permute-start(bf16[2,16,2688]{2,1,0:T(8,128)(2,1)S(1)} %get-tuple-element.49), channel_id=1, source_target_pairs={{0,32},{1,9},{2,34},{3,11},{4,36},{5,13},{6,38},{7,15},{8,40},{9,1... | collective-permute-start | bytes 516104 | tf_op jit(solution)/shard_map/ppermute | solution.py:38
  92.2 8.5 %collective-permute-start.21 = (bf16[2,16,2688]{2,1,0:T(8,128)(2,1)S(1)}, bf16[2,16,2688]{2,1,0:T(8,128)(2,1)S(1)}, u32[]{:S(2)}, u32[]{:S(2)}) collective-permute-start(bf16[2,16,2688]{2,1,0:T(8,128)(2,1)S(1)} %get-tuple-element.51), channel_id=1, source_target_pairs={{0,16},{1,5},{2,18},{3,7},{4,20},{5,9},{6,22},{7,11},{8,24},{9,13}... | collective-permute-start | bytes 516104 | tf_op jit(solution)/shard_map/ppermute | solution.py:38
  93.5 9.7 %collective-permute-start.14 = (bf16[2,16,2688]{2,1,0:T(8,128)(2,1)S(1)}, bf16[2,16,2688]{2,1,0:T(8,128)(2,1)S(1)}, u32[]{:S(2)}, u32[]{:S(2)}) collective-permute-start(bf16[2,16,2688]{2,1,0:T(8,128)(2,1)S(1)} %get-tuple-element.46), channel_id=1, source_target_pairs={{0,32},{1,9},{2,34},{3,11},{4,36},{5,13},{6,38},{7,15},{8,40},{9,1... | collective-permute-start | bytes 516104 | tf_op jit(solution)/shard_map/ppermute | solution.py:38
  94.4 8.8 %collective-permute-start.16 = (bf16[2,16,2688]{2,1,0:T(8,128)(2,1)S(1)}, bf16[2,16,2688]{2,1,0:T(8,128)(2,1)S(1)}, u32[]{:S(2)}, u32[]{:S(2)}) collective-permute-start(bf16[2,16,2688]{2,1,0:T(8,128)(2,1)S(1)} %get-tuple-element.47), channel_id=1, source_target_pairs={{0,48},{1,13},{2,50},{3,15},{4,52},{5,1},{6,54},{7,3},{8,56},{9,5}... | collective-permute-start | bytes 516104 | tf_op jit(solution)/shard_map/ppermute | solution.py:38
  115.5 8.3 %collective-permute-start.26 = (bf16[1,16,5376]{2,1,0:T(8,128)(2,1)S(1)}, bf16[1,16,5376]{2,1,0:T(8,128)(2,1)S(1)}, u32[]{:S(2)}, u32[]{:S(2)}) collective-permute-start(bf16[1,16,5376]{2,1,0:T(8,128)(2,1)S(1)} %get-tuple-element.34.refs_0_), channel_id=1, source_target_pairs={{0,16},{1,5},{2,18},{3,7},{4,20},{5,9},{6,22},{7,11},{8,24},{9,13}... | collective-permute-start | bytes 516104 | tf_op jit(solution)/shard_map/ppermute | solution.py:38
  129.4 11.6 %collective-permute-start.33 = (bf16[4,16,5376]{2,1,0:T(8,128)(2,1)S(1)}, bf16[4,16,5376]{2,1,0:T(8,128)(2,1)}, u32[]{:S(2)}, u32[]{:S(2)}) collective-permute-start(bf16[4,16,5376]{2,1,0:T(8,128)(2,1)S(1)} %get-tuple-element.30.refs_0_), channel_id=1, source_target_pairs={{0,4},{1,17},{2,6},{3,19},{4,8},{5,21},{6,10},{7,23},{8,12},{9,25}... | collective-permute-start | bytes 2064392 | tf_op jit(solution)/shard_map/ppermute | solution.py:38
  132.6 12.5 %collective-permute-start.36 = (bf16[4,16,5376]{2,1,0:T(8,128)(2,1)}, bf16[4,16,5376]{2,1,0:T(8,128)(2,1)}, u32[]{:S(2)}, u32[]{:S(2)}) collective-permute-start(bf16[4,16,5376]{2,1,0:T(8,128)(2,1)} %get-tuple-element.31.refs_1_), channel_id=1, source_target_pairs={{0,12},{1,49},{2,14},{3,51},{4,0},{5,53},{6,2},{7,55},{8,4},{9,57}... | collective-permute-start | bytes 2064392 | tf_op jit(solution)/shard_map/ppermute | solution.py:38
  136.4 12.9 %collective-permute-start.10 = (bf16[512,512]{1,0:T(8,128)(2,1)S(1)}, bf16[512,512]{1,0:T(8,128)(2,1)S(1)}, u32[]{:S(2)}, u32[]{:S(2)}) collective-permute-start(bf16[512,512]{1,0:T(8,128)(2,1)S(1)} %convolution_convert_fusion), channel_id=1, source_target_pairs={{0,2},{1,3},{2,0},{3,1},{4,6},{5,7},{6,4},{7,5},{8,10},{9,11},{10,... | collective-permute-start | bytes 1572872 | tf_op jit(solution)/shard_map/ppermute | solution.py:38
  136.8 15.5 %collective-permute-start.35 = (bf16[4,16,5376]{2,1,0:T(8,128)(2,1)S(1)}, bf16[4,16,5376]{2,1,0:T(8,128)(2,1)S(1)}, u32[]{:S(2)}, u32[]{:S(2)}) collective-permute-start(bf16[4,16,5376]{2,1,0:T(8,128)(2,1)S(1)} %get-tuple-element.30.refs_0_), channel_id=1, source_target_pairs={{0,12},{1,49},{2,14},{3,51},{4,0},{5,53},{6,2},{7,55},{8,4},{9,57}... | collective-permute-start | bytes 2064392 | tf_op jit(solution)/shard_map/ppermute | solution.py:38
  138.0 14.3 %collective-permute-start.34 = (bf16[4,16,5376]{2,1,0:T(8,128)(2,1)}, bf16[4,16,5376]{2,1,0:T(8,128)(2,1)S(1)}, u32[]{:S(2)}, u32[]{:S(2)}) collective-permute-start(bf16[4,16,5376]{2,1,0:T(8,128)(2,1)} %get-tuple-element.31.refs_1_), channel_id=1, source_target_pairs={{0,4},{1,17},{2,6},{3,19},{4,8},{5,21},{6,10},{7,23},{8,12},{9,25}... | collective-permute-start | bytes 2064392 | tf_op jit(solution)/shard_map/ppermute | solution.py:38
  141.0 15.5 %collective-permute-start.37 = (bf16[4,16,5376]{2,1,0:T(8,128)(2,1)}, bf16[4,16,5376]{2,1,0:T(8,128)(2,1)S(1)}, u32[]{:S(2)}, u32[]{:S(2)}) collective-permute-start(bf16[4,16,5376]{2,1,0:T(8,128)(2,1)} %collective-permute-done.33.refs_2_), channel_id=1, source_target_pairs={{0,4},{1,17},{2,6},{3,19},{4,8},{5,21},{6,10},{7,23},{8,12},{9,25}... | collective-permute-start | bytes 2064392 | tf_op jit(solution)/shard_map/ppermute | solution.py:38
  145.0 14.6 %collective-permute-start.38 = (bf16[4,16,5376]{2,1,0:T(8,128)(2,1)}, bf16[4,16,5376]{2,1,0:T(8,128)(2,1)S(1)}, u32[]{:S(2)}, u32[]{:S(2)}) collective-permute-start(bf16[4,16,5376]{2,1,0:T(8,128)(2,1)} %collective-permute-done.36.refs_5_), channel_id=1, source_target_pairs={{0,12},{1,49},{2,14},{3,51},{4,0},{5,53},{6,2},{7,55},{8,4},{9,57}... | collective-permute-start | bytes 2064392 | tf_op jit(solution)/shard_map/ppermute | solution.py:38
  (21 other events, 142.3 us)

commit v5 on v4

--- a/solution.py
+++ b/solution.py
@@ -80,7 +80,7 @@
 def gradient_pieces(rows, left, right):
     heads, tokens = left.shape
     columns = right.shape[0]
-    width = 896
+    width = 2688
     return pl.pallas_call(
         gradient_kernel,
         grid_spec=pltpu.PrefetchScalarGridSpec(

time: 162 us -> 161 us (level)
  transfers between devices with their start and end apart: 39 -> 39, of which waited for: 28 -> 28; matrix products, arithmetic and copies ran while one was open for 14% -> 14% of each run, Pallas kernels for 5% -> 4%
where the time goes in v5:
time: 161 us
  waiting for transfers between devices  61.3 us (38%)
  starting transfers between devices  48.9 us (30%)
  other arithmetic  21 us (13%)
  matrix products  13.8 us (9%)
  Pallas kernels  11.4 us (7%)
  local copies, waits for them, and re-layouts  3.07 us (2%)
    ppermute x39, waiting for transfers between devices, move(): lax.ppermute(value, axes, [(flat(p), flat(target(*p))) for p in places])  61.3 us
    ppermute x39, starting transfers between devices, move(): lax.ppermute(value, axes, [(flat(p), flat(target(*p))) for p in places])  48.9 us
    pallas_call x2, Pallas kernels, place_rows(): pl.pallas_call(place_more_kernel if before else place_kernel, grid_spec=p...  5.91 us
    pallas_call x2, Pallas kernels, gradient_pieces(): pl.pallas_call(gradient_kernel, grid_spec=pltpu.PrefetchScalarGridSpec(nu...  4.55 us
    dot_general x1, matrix products, local(): lax.dot_general(near, attention, left_rows, preferred_element_type=f32)  4.37 us
    dot_general x1, matrix products, local(): lax.dot_general(pair, near, to_heads, preferred_element_type=f32)  4.32 us
    convert_element_type x1, other arithmetic, local(): pre_grad = (inv_rms * scaled - pre * inv_rms ** 3 * proj).astype(bf16)  3.95 us
    dot_general x1, matrix products, local(): lax.dot_general(pair, far, to_heads, preferred_element_type=f32)  3.48 us
  transfers between devices with their start and end apart: 39, of which 28 were waited for; matrix products, arithmetic and copies ran while one was open for 14% of the time, Pallas kernels for 4%

profile of v5, /device:TPU:6, one launch (start us, length us, event | category | flops | bytes accessed | tf_op | source)
XLA Modules:
  0.0 160.8 jit_solution(17413585966568402583)
XLA Ops:
  7.7 4.1 %collective-permute-start.4 = (bf16[192,2688]{1,0:T(8,128)(2,1)S(1)}, bf16[192,2688]{1,0:T(8,128)(2,1)S(1)}, u32[]{:S(2)}, u32[]{:S(2)}) collective-permute-start(bf16[192,2688]{1,0:T(8,128)(2,1)S(1)} %slice_select_fusion.2), channel_id=1, source_target_pairs={{0,66},{1,67},{2,64},{3,65},{4,70},{5,71},{6,68},{7,69},{8,74},{9,... | collective-permute-start | bytes 3096584 | tf_op jit(solution)/shard_map/ppermute | solution.py:38
  11.8 3.9 %collective-permute-done = bf16[80,2688]{1,0:T(8,128)(2,1)S(1)} collective-permute-done((bf16[80,2688]{1,0:T(8,128)(2,1)}, bf16[80,2688]{1,0:T(8,128)(2,1)S(1)}, u32[]{:S(2)}, u32[]{:S(2)}) %collective-permute-start) | collective-permute-done | bytes 430112 | tf_op jit(solution)/shard_map/ppermute | solution.py:38
  19.7 4.4 %fusion.11 = f32[2688,512]{1,0:T(8,128)S(1)} fusion(bf16[512,512]{1,0:T(8,128)(2,1)} %param.9, bf16[512,5376]{1,0:T(8,128)(2,1)} %param.10, pred[]{:T(512)S(6)} %eq.34), kind=kOutput, calls=%fused_computation.40 | convolution fusion | flops 1410662400 | bytes 11534337 | tf_op jit(solution)/shard_map/dot_general | solution.py:200
  24.1 5.6 %collective-permute-done.3 = bf16[80,2688]{1,0:T(8,128)(2,1)S(1)} collective-permute-done((bf16[80,2688]{1,0:T(8,128)(2,1)S(1)}, bf16[80,2688]{1,0:T(8,128)(2,1)S(1)}, u32[]{:S(2)}, u32[]{:S(2)}) %collective-permute-start.3) | collective-permute-done | bytes 430112 | tf_op jit(solution)/shard_map/ppermute | solution.py:38
  31.0 3.0 %collective-permute-done.4 = bf16[192,2688]{1,0:T(8,128)(2,1)S(1)} collective-permute-done((bf16[192,2688]{1,0:T(8,128)(2,1)S(1)}, bf16[192,2688]{1,0:T(8,128)(2,1)S(1)}, u32[]{:S(2)}, u32[]{:S(2)}) %collective-permute-start.4) | collective-permute-done | bytes 1032224 | tf_op jit(solution)/shard_map/ppermute | solution.py:38
  38.8 2.6 %collective-permute-done.6 = bf16[1344,512]{1,0:T(8,128)(2,1)} collective-permute-done((bf16[1344,512]{1,0:T(8,128)(2,1)}, bf16[1344,512]{1,0:T(8,128)(2,1)}, u32[]{:S(2)}, u32[]{:S(2)}) %collective-permute-start.6) | collective-permute-done | bytes 1376288 | tf_op jit(solution)/shard_map/ppermute | solution.py:38
  41.4 2.5 %multiply_reduce_fusion = (f32[512]{0:T(512)S(1)}, f32[512]{0:T(512)S(1)}) fusion(f32[1344,512]{1,0:T(8,128)S(1)} %slice_select_fusion.1, bf16[1344,512]{1,0:T(8,128)(2,1)} %collective-permute-done.6, f32[1344]{0:T(1024)S(1)} %dynamic_slice.26, bf16[512,1344]{0,1:T(8,128)(2,1)} %param.13), kind=kLoop, calls=%fused_computation.14 | loop fusion | flops 5504000 | bytes 5514496 | tf_op jit(solution)/shard_map/reduce_sum | solution.py:209
  45.3 3.6 %collective-permute-done.8 = f32[2,512]{1,0:T(2,128)S(1)} collective-permute-done((f32[2,512]{1,0:T(2,128)S(1)}, f32[2,512]{1,0:T(2,128)S(1)}, u32[]{:S(2)}, u32[]{:S(2)}) %collective-permute-start.8) | collective-permute-done | bytes 4128 | tf_op jit(solution)/shard_map/ppermute | solution.py:38
  48.9 4.0 %fusion.2 = (bf16[1344,512]{1,0:T(8,128)(2,1)}, bf16[512,1344]{0,1:T(8,128)(2,1)}) fusion(bf16[512,1344]{0,1:T(8,128)(2,1)} %param.13, f32[512]{0:T(512)S(1)} %bitcast.92, f32[512]{0:T(512)S(1)} %bitcast.90, f32[512]{0:T(512)S(1)} %bitcast.91, f32[1344]{0:T(1024)S(1)} %dynamic_slice.26, f32[1344,512]{1,0:T(8,128)S(1)} %slice_select_fusion.1, ...), kind=kLoop, calls=%fused_computation.10 | loop fusion | flops 9633792 | bytes 9645312 | tf_op jit(solution)/shard_map/convert_element_type | solution.py:215
  67.5 4.5 %collective-permute-done.18 = bf16[8,16,2688]{2,1,0:T(8,128)(2,1)S(1)} collective-permute-done((bf16[8,16,2688]{2,1,0:T(8,128)(2,1)S(1)}, bf16[8,16,2688]{2,1,0:T(8,128)(2,1)S(1)}, u32[]{:S(2)}, u32[]{:S(2)}) %collective-permute-start.18) | collective-permute-done | bytes 688160 | tf_op jit(solution)/shard_map/ppermute | solution.py:38
  75.5 7.1 %collective-permute-done.17 = bf16[8,16,2688]{2,1,0:T(8,128)(2,1)S(1)} collective-permute-done((bf16[8,16,2688]{2,1,0:T(8,128)(2,1)S(1)}, bf16[8,16,2688]{2,1,0:T(8,128)(2,1)S(1)}, u32[]{:S(2)}, u32[]{:S(2)}) %collective-permute-start.17) | collective-permute-done | bytes 688160 | tf_op jit(solution)/shard_map/ppermute | solution.py:38
  82.6 4.1 %collective-permute-done.19 = bf16[8,16,2688]{2,1,0:T(8,128)(2,1)S(1)} collective-permute-done((bf16[8,16,2688]{2,1,0:T(8,128)(2,1)S(1)}, bf16[8,16,2688]{2,1,0:T(8,128)(2,1)S(1)}, u32[]{:S(2)}, u32[]{:S(2)}) %collective-permute-start.19) | collective-permute-done | bytes 688160 | tf_op jit(solution)/shard_map/ppermute | solution.py:38
  87.0 3.3 %collective-permute-start.20 = (bf16[2,16,2688]{2,1,0:T(8,128)(2,1)S(1)}, bf16[2,16,2688]{2,1,0:T(8,128)(2,1)S(1)}, u32[]{:S(2)}, u32[]{:S(2)}) collective-permute-start(bf16[2,16,2688]{2,1,0:T(8,128)(2,1)S(1)} %get-tuple-element.49), channel_id=1, source_target_pairs={{0,32},{1,9},{2,34},{3,11},{4,36},{5,13},{6,38},{7,15},{8,40},{9,1... | collective-permute-start | bytes 516104 | tf_op jit(solution)/shard_map/ppermute | solution.py:38
  93.6 2.5 %collective-permute-start.16 = (bf16[2,16,2688]{2,1,0:T(8,128)(2,1)S(1)}, bf16[2,16,2688]{2,1,0:T(8,128)(2,1)S(1)}, u32[]{:S(2)}, u32[]{:S(2)}) collective-permute-start(bf16[2,16,2688]{2,1,0:T(8,128)(2,1)S(1)} %get-tuple-element.47), channel_id=1, source_target_pairs={{0,48},{1,13},{2,50},{3,15},{4,52},{5,1},{6,54},{7,3},{8,56},{9,5}... | collective-permute-start | bytes 516104 | tf_op jit(solution)/shard_map/ppermute | solution.py:38
  96.2 3.6 %collective-permute-done.21 = bf16[2,16,2688]{2,1,0:T(8,128)(2,1)S(1)} collective-permute-done((bf16[2,16,2688]{2,1,0:T(8,128)(2,1)S(1)}, bf16[2,16,2688]{2,1,0:T(8,128)(2,1)S(1)}, u32[]{:S(2)}, u32[]{:S(2)}) %collective-permute-start.21) | collective-permute-done | bytes 172064 | tf_op jit(solution)/shard_map/ppermute | solution.py:38
  99.9 2.5 %collective-permute-start.23 = (bf16[16,2688]{1,0:T(8,128)(2,1)S(1)}, bf16[16,2688]{1,0:T(8,128)(2,1)S(1)}, u32[]{:S(2)}, u32[]{:S(2)}) collective-permute-start(bf16[16,2688]{1,0:T(8,128)(2,1)S(1)} %get-tuple-element.53), channel_id=1, source_target_pairs={{0,64},{1,65},{2,66},{3,67},{4,68},{5,69},{6,70},{7,71},{8,72},{9,... | collective-permute-start | bytes 258056 | tf_op jit(solution)/shard_map/ppermute | solution.py:38
  115.5 2.4 %collective-permute-done.29.refs_4_ = bf16[1,16,5376]{2,1,0:T(8,128)(2,1)S(1)} collective-permute-done((bf16[1,16,5376]{2,1,0:T(8,128)(2,1)S(1)}, bf16[1,16,5376]{2,1,0:T(8,128)(2,1)S(1)}, u32[]{:S(2)}, u32[]{:S(2)}) %collective-permute-start.29) | collective-permute-done | bytes 172064 | tf_op jit(solution)/shard_map/ppermute | solution.py:38
  124.9 2.7 %collective-permute-done.30.refs_5_ = bf16[1,16,5376]{2,1,0:T(8,128)(2,1)S(1)} collective-permute-done((bf16[1,16,5376]{2,1,0:T(8,128)(2,1)S(1)}, bf16[1,16,5376]{2,1,0:T(8,128)(2,1)S(1)}, u32[]{:S(2)}, u32[]{:S(2)}) %collective-permute-start.30) | collective-permute-done | bytes 172064 | tf_op jit(solution)/shard_map/ppermute | solution.py:38
  128.6 3.2 %collective-permute-start.33 = (bf16[4,16,5376]{2,1,0:T(8,128)(2,1)S(1)}, bf16[4,16,5376]{2,1,0:T(8,128)(2,1)}, u32[]{:S(2)}, u32[]{:S(2)}) collective-permute-start(bf16[4,16,5376]{2,1,0:T(8,128)(2,1)S(1)} %get-tuple-element.30.refs_0_), channel_id=1, source_target_pairs={{0,4},{1,17},{2,6},{3,19},{4,8},{5,21},{6,10},{7,23},{8,12},{9,25}... | collective-permute-start | bytes 2064392 | tf_op jit(solution)/shard_map/ppermute | solution.py:38
  132.2 3.5 %convolution_convert_fusion = bf16[512,512]{1,0:T(8,128)(2,1)S(1)} fusion(bf16[2688,512]{1,0:T(8,128)(2,1)S(1)} %pad_maximum_fusion.right_ref, bf16[512,2688]{1,0:T(8,128)(2,1)} %copy-done), kind=kOutput, calls=%fused_computation.30 | convolution fusion | flops 1409548288 | bytes 6029312 | tf_op jit(solution)/shard_map/dot_general | solution.py:298
  140.3 3.8 %collective-permute-start.37 = (bf16[4,16,5376]{2,1,0:T(8,128)(2,1)}, bf16[4,16,5376]{2,1,0:T(8,128)(2,1)S(1)}, u32[]{:S(2)}, u32[]{:S(2)}) collective-permute-start(bf16[4,16,5376]{2,1,0:T(8,128)(2,1)} %collective-permute-done.33.refs_2_), channel_id=1, source_target_pairs={{0,4},{1,17},{2,6},{3,19},{4,8},{5,21},{6,10},{7,23},{8,12},{9,25}... | collective-permute-start | bytes 2064392 | tf_op jit(solution)/shard_map/ppermute | solution.py:38
  144.3 4.3 %fusion.10 = f32[512,512]{1,0:T(8,128)S(1)} fusion(bf16[2688,512]{1,0:T(8,128)(2,1)S(1)} %pad_maximum_fusion.right_ref, bf16[512,5376]{1,0:T(8,128)(2,1)} %param.10, pred[]{:T(512)S(6)} %eq.34), kind=kOutput, calls=%fused_computation.39 | convolution fusion | flops 1410662400 | bytes 9306113 | tf_op jit(solution)/shard_map/dot_general | solution.py:299
  151.5 4.2 %shard_map.139.earlier_ref = bf16[512,5376]{1,0:T(8,128)(2,1)} custom-call(s32[24]{0:T(128)S(1)} %pad_add_fusion.1.rows_ref, bf16[4,16,5376]{2,1,0:T(8,128)(2,1)S(1)} %get-tuple-element.30.refs_0_, bf16[4,16,5376]{2,1,0:T(8,128)(2,1)} %get-tuple-element.31.refs_1_, bf16[4,16,5376]{2,1,0:T(8,128)(2,1)} %collective-permute-done.33.refs_2_, ...), custom_call_target="tpu_custom_call" | custom-call | bytes 8400000 | tf_op jit(solution)/shard_map/pallas_call | solution.py:156
  155.8 3.1 %collective-permute-done.38.refs_1_ = bf16[4,16,5376]{2,1,0:T(8,128)(2,1)S(1)} collective-permute-done((bf16[4,16,5376]{2,1,0:T(8,128)(2,1)}, bf16[4,16,5376]{2,1,0:T(8,128)(2,1)S(1)}, u32[]{:S(2)}, u32[]{:S(2)}) %collective-permute-start.38) | collective-permute-done | bytes 688160 | tf_op jit(solution)/shard_map/ppermute | solution.py:38
  (136 shorter events, 70.9 us)
Async XLA Ops:
  2.7 13.0 %collective-permute-start = (bf16[80,2688]{1,0:T(8,128)(2,1)}, bf16[80,2688]{1,0:T(8,128)(2,1)S(1)}, u32[]{:S(2)}, u32[]{:S(2)}) collective-permute-start(bf16[80,2688]{1,0:T(8,128)(2,1)} %dynamic-slice_select_fusion), channel_id=1, source_target_pairs={{0,2},{1,3},{2,0},{3,1},{4,6},{5,7},{6,4},{7,5},{8,10},{9,11},{10,... | collective-permute-start | bytes 1290248 | tf_op jit(solution)/shard_map/ppermute | solution.py:38
  5.8 28.3 %collective-permute-start.5 = (bf16[512,512]{0,1:T(8,128)(2,1)S(1)}, bf16[512,512]{0,1:T(8,128)(2,1)S(1)}, u32[]{:S(2)}, u32[]{:S(2)}) collective-permute-start(bf16[512,512]{0,1:T(8,128)(2,1)S(1)} %copy.18), channel_id=1, source_target_pairs={{0,2},{1,3},{2,0},{3,1},{4,6},{5,7},{6,4},{7,5},{8,10},{9,11},{10,... | collective-permute-start | bytes 1572872 | tf_op jit(solution)/shard_map/ppermute | solution.py:38
  7.7 26.4 %collective-permute-start.4 = (bf16[192,2688]{1,0:T(8,128)(2,1)S(1)}, bf16[192,2688]{1,0:T(8,128)(2,1)S(1)}, u32[]{:S(2)}, u32[]{:S(2)}) collective-permute-start(bf16[192,2688]{1,0:T(8,128)(2,1)S(1)} %slice_select_fusion.2), channel_id=1, source_target_pairs={{0,66},{1,67},{2,64},{3,65},{4,70},{5,71},{6,68},{7,69},{8,74},{9,... | collective-permute-start | bytes 3096584 | tf_op jit(solution)/shard_map/ppermute | solution.py:38
  15.6 14.0 %collective-permute-start.3 = (bf16[80,2688]{1,0:T(8,128)(2,1)S(1)}, bf16[80,2688]{1,0:T(8,128)(2,1)S(1)}, u32[]{:S(2)}, u32[]{:S(2)}) collective-permute-start(bf16[80,2688]{1,0:T(8,128)(2,1)S(1)} %collective-permute-done), channel_id=1, source_target_pairs={{0,12},{1,49},{2,14},{3,51},{4,0},{5,53},{6,2},{7,55},{8,4},{9,57}... | collective-permute-start | bytes 1290248 | tf_op jit(solution)/shard_map/ppermute | solution.py:38
  16.5 13.2 %collective-permute-start.2 = (bf16[80,2688]{1,0:T(8,128)(2,1)S(1)}, bf16[80,2688]{1,0:T(8,128)(2,1)S(1)}, u32[]{:S(2)}, u32[]{:S(2)}) collective-permute-start(bf16[80,2688]{1,0:T(8,128)(2,1)S(1)} %collective-permute-done), channel_id=1, source_target_pairs={{0,8},{1,33},{2,10},{3,35},{4,12},{5,37},{6,14},{7,39},{8,0},{9,41... | collective-permute-start | bytes 1290248 | tf_op jit(solution)/shard_map/ppermute | solution.py:38
  17.5 13.0 %collective-permute-start.1 = (bf16[80,2688]{1,0:T(8,128)(2,1)S(1)}, bf16[80,2688]{1,0:T(8,128)(2,1)S(1)}, u32[]{:S(2)}, u32[]{:S(2)}) collective-permute-start(bf16[80,2688]{1,0:T(8,128)(2,1)S(1)} %collective-permute-done), channel_id=1, source_target_pairs={{0,4},{1,17},{2,6},{3,19},{4,8},{5,21},{6,10},{7,23},{8,12},{9,25}... | collective-permute-start | bytes 1290248 | tf_op jit(solution)/shard_map/ppermute | solution.py:38
  61.0 11.0 %collective-permute-start.18 = (bf16[8,16,2688]{2,1,0:T(8,128)(2,1)S(1)}, bf16[8,16,2688]{2,1,0:T(8,128)(2,1)S(1)}, u32[]{:S(2)}, u32[]{:S(2)}) collective-permute-start(bf16[8,16,2688]{2,1,0:T(8,128)(2,1)S(1)} %get-tuple-element.29), channel_id=1, source_target_pairs={{0,4},{1,17},{2,6},{3,19},{4,8},{5,21},{6,10},{7,23},{8,12},{9,25}... | collective-permute-start | bytes 2064392 | tf_op jit(solution)/shard_map/ppermute | solution.py:38
  61.6 30.7 %collective-permute-start.11 = (bf16[8,16,2688]{2,1,0:T(8,128)(2,1)S(1)}, bf16[8,16,2688]{2,1,0:T(8,128)(2,1)S(1)}, u32[]{:S(2)}, u32[]{:S(2)}) collective-permute-start(bf16[8,16,2688]{2,1,0:T(8,128)(2,1)S(1)} %get-tuple-element.23), channel_id=1, source_target_pairs={{0,4},{1,17},{2,6},{3,19},{4,8},{5,21},{6,10},{7,23},{8,12},{9,25}... | collective-permute-start | bytes 2064392 | tf_op jit(solution)/shard_map/ppermute | solution.py:38
  63.1 12.1 %collective-permute-start.12 = (bf16[8,16,2688]{2,1,0:T(8,128)(2,1)S(1)}, bf16[8,16,2688]{2,1,0:T(8,128)(2,1)S(1)}, u32[]{:S(2)}, u32[]{:S(2)}) collective-permute-start(bf16[8,16,2688]{2,1,0:T(8,128)(2,1)S(1)} %get-tuple-element.25), channel_id=1, source_target_pairs={{0,12},{1,49},{2,14},{3,51},{4,0},{5,53},{6,2},{7,55},{8,4},{9,57}... | collective-permute-start | bytes 2064392 | tf_op jit(solution)/shard_map/ppermute | solution.py:38
  63.6 19.0 %collective-permute-start.17 = (bf16[8,16,2688]{2,1,0:T(8,128)(2,1)S(1)}, bf16[8,16,2688]{2,1,0:T(8,128)(2,1)S(1)}, u32[]{:S(2)}, u32[]{:S(2)}) collective-permute-start(bf16[8,16,2688]{2,1,0:T(8,128)(2,1)S(1)} %get-tuple-element.27), channel_id=1, source_target_pairs={{0,12},{1,49},{2,14},{3,51},{4,0},{5,53},{6,2},{7,55},{8,4},{9,57}... | collective-permute-start | bytes 2064392 | tf_op jit(solution)/shard_map/ppermute | solution.py:38
  72.1 14.6 %collective-permute-start.19 = (bf16[8,16,2688]{2,1,0:T(8,128)(2,1)S(1)}, bf16[8,16,2688]{2,1,0:T(8,128)(2,1)S(1)}, u32[]{:S(2)}, u32[]{:S(2)}) collective-permute-start(bf16[8,16,2688]{2,1,0:T(8,128)(2,1)S(1)} %add_convert_fusion.1), channel_id=1, source_target_pairs={{0,4},{1,17},{2,6},{3,19},{4,8},{5,21},{6,10},{7,23},{8,12},{9,25}... | collective-permute-start | bytes 2064392 | tf_op jit(solution)/shard_map/ppermute | solution.py:38
  75.4 16.9 %collective-permute-start.13 = (bf16[8,16,2688]{2,1,0:T(8,128)(2,1)S(1)}, bf16[8,16,2688]{2,1,0:T(8,128)(2,1)S(1)}, u32[]{:S(2)}, u32[]{:S(2)}) collective-permute-start(bf16[8,16,2688]{2,1,0:T(8,128)(2,1)S(1)} %add_convert_fusion.3), channel_id=1, source_target_pairs={{0,12},{1,49},{2,14},{3,51},{4,0},{5,53},{6,2},{7,55},{8,4},{9,57}... | collective-permute-start | bytes 2064392 | tf_op jit(solution)/shard_map/ppermute | solution.py:38
  87.0 9.1 %collective-permute-start.20 = (bf16[2,16,2688]{2,1,0:T(8,128)(2,1)S(1)}, bf16[2,16,2688]{2,1,0:T(8,128)(2,1)S(1)}, u32[]{:S(2)}, u32[]{:S(2)}) collective-permute-start(bf16[2,16,2688]{2,1,0:T(8,128)(2,1)S(1)} %get-tuple-element.49), channel_id=1, source_target_pairs={{0,32},{1,9},{2,34},{3,11},{4,36},{5,13},{6,38},{7,15},{8,40},{9,1... | collective-permute-start | bytes 516104 | tf_op jit(solution)/shard_map/ppermute | solution.py:38
  91.4 8.5 %collective-permute-start.21 = (bf16[2,16,2688]{2,1,0:T(8,128)(2,1)S(1)}, bf16[2,16,2688]{2,1,0:T(8,128)(2,1)S(1)}, u32[]{:S(2)}, u32[]{:S(2)}) collective-permute-start(bf16[2,16,2688]{2,1,0:T(8,128)(2,1)S(1)} %get-tuple-element.51), channel_id=1, source_target_pairs={{0,16},{1,5},{2,18},{3,7},{4,20},{5,9},{6,22},{7,11},{8,24},{9,13}... | collective-permute-start | bytes 516104 | tf_op jit(solution)/shard_map/ppermute | solution.py:38
  92.7 9.7 %collective-permute-start.14 = (bf16[2,16,2688]{2,1,0:T(8,128)(2,1)S(1)}, bf16[2,16,2688]{2,1,0:T(8,128)(2,1)S(1)}, u32[]{:S(2)}, u32[]{:S(2)}) collective-permute-start(bf16[2,16,2688]{2,1,0:T(8,128)(2,1)S(1)} %get-tuple-element.46), channel_id=1, source_target_pairs={{0,32},{1,9},{2,34},{3,11},{4,36},{5,13},{6,38},{7,15},{8,40},{9,1... | collective-permute-start | bytes 516104 | tf_op jit(solution)/shard_map/ppermute | solution.py:38
  93.6 8.8 %collective-permute-start.16 = (bf16[2,16,2688]{2,1,0:T(8,128)(2,1)S(1)}, bf16[2,16,2688]{2,1,0:T(8,128)(2,1)S(1)}, u32[]{:S(2)}, u32[]{:S(2)}) collective-permute-start(bf16[2,16,2688]{2,1,0:T(8,128)(2,1)S(1)} %get-tuple-element.47), channel_id=1, source_target_pairs={{0,48},{1,13},{2,50},{3,15},{4,52},{5,1},{6,54},{7,3},{8,56},{9,5}... | collective-permute-start | bytes 516104 | tf_op jit(solution)/shard_map/ppermute | solution.py:38
  114.7 8.3 %collective-permute-start.26 = (bf16[1,16,5376]{2,1,0:T(8,128)(2,1)S(1)}, bf16[1,16,5376]{2,1,0:T(8,128)(2,1)S(1)}, u32[]{:S(2)}, u32[]{:S(2)}) collective-permute-start(bf16[1,16,5376]{2,1,0:T(8,128)(2,1)S(1)} %get-tuple-element.34.refs_0_), channel_id=1, source_target_pairs={{0,16},{1,5},{2,18},{3,7},{4,20},{5,9},{6,22},{7,11},{8,24},{9,13}... | collective-permute-start | bytes 516104 | tf_op jit(solution)/shard_map/ppermute | solution.py:38
  128.6 11.7 %collective-permute-start.33 = (bf16[4,16,5376]{2,1,0:T(8,128)(2,1)S(1)}, bf16[4,16,5376]{2,1,0:T(8,128)(2,1)}, u32[]{:S(2)}, u32[]{:S(2)}) collective-permute-start(bf16[4,16,5376]{2,1,0:T(8,128)(2,1)S(1)} %get-tuple-element.30.refs_0_), channel_id=1, source_target_pairs={{0,4},{1,17},{2,6},{3,19},{4,8},{5,21},{6,10},{7,23},{8,12},{9,25}... | collective-permute-start | bytes 2064392 | tf_op jit(solution)/shard_map/ppermute | solution.py:38
  131.8 12.5 %collective-permute-start.36 = (bf16[4,16,5376]{2,1,0:T(8,128)(2,1)}, bf16[4,16,5376]{2,1,0:T(8,128)(2,1)}, u32[]{:S(2)}, u32[]{:S(2)}) collective-permute-start(bf16[4,16,5376]{2,1,0:T(8,128)(2,1)} %get-tuple-element.31.refs_1_), channel_id=1, source_target_pairs={{0,12},{1,49},{2,14},{3,51},{4,0},{5,53},{6,2},{7,55},{8,4},{9,57}... | collective-permute-start | bytes 2064392 | tf_op jit(solution)/shard_map/ppermute | solution.py:38
  135.7 12.9 %collective-permute-start.10 = (bf16[512,512]{1,0:T(8,128)(2,1)S(1)}, bf16[512,512]{1,0:T(8,128)(2,1)S(1)}, u32[]{:S(2)}, u32[]{:S(2)}) collective-permute-start(bf16[512,512]{1,0:T(8,128)(2,1)S(1)} %convolution_convert_fusion), channel_id=1, source_target_pairs={{0,2},{1,3},{2,0},{3,1},{4,6},{5,7},{6,4},{7,5},{8,10},{9,11},{10,... | collective-permute-start | bytes 1572872 | tf_op jit(solution)/shard_map/ppermute | solution.py:38
  136.0 15.5 %collective-permute-start.35 = (bf16[4,16,5376]{2,1,0:T(8,128)(2,1)S(1)}, bf16[4,16,5376]{2,1,0:T(8,128)(2,1)S(1)}, u32[]{:S(2)}, u32[]{:S(2)}) collective-permute-start(bf16[4,16,5376]{2,1,0:T(8,128)(2,1)S(1)} %get-tuple-element.30.refs_0_), channel_id=1, source_target_pairs={{0,12},{1,49},{2,14},{3,51},{4,0},{5,53},{6,2},{7,55},{8,4},{9,57}... | collective-permute-start | bytes 2064392 | tf_op jit(solution)/shard_map/ppermute | solution.py:38
  137.2 14.4 %collective-permute-start.34 = (bf16[4,16,5376]{2,1,0:T(8,128)(2,1)}, bf16[4,16,5376]{2,1,0:T(8,128)(2,1)S(1)}, u32[]{:S(2)}, u32[]{:S(2)}) collective-permute-start(bf16[4,16,5376]{2,1,0:T(8,128)(2,1)} %get-tuple-element.31.refs_1_), channel_id=1, source_target_pairs={{0,4},{1,17},{2,6},{3,19},{4,8},{5,21},{6,10},{7,23},{8,12},{9,25}... | collective-permute-start | bytes 2064392 | tf_op jit(solution)/shard_map/ppermute | solution.py:38
  140.3 15.5 %collective-permute-start.37 = (bf16[4,16,5376]{2,1,0:T(8,128)(2,1)}, bf16[4,16,5376]{2,1,0:T(8,128)(2,1)S(1)}, u32[]{:S(2)}, u32[]{:S(2)}) collective-permute-start(bf16[4,16,5376]{2,1,0:T(8,128)(2,1)} %collective-permute-done.33.refs_2_), channel_id=1, source_target_pairs={{0,4},{1,17},{2,6},{3,19},{4,8},{5,21},{6,10},{7,23},{8,12},{9,25}... | collective-permute-start | bytes 2064392 | tf_op jit(solution)/shard_map/ppermute | solution.py:38
  144.3 14.6 %collective-permute-start.38 = (bf16[4,16,5376]{2,1,0:T(8,128)(2,1)}, bf16[4,16,5376]{2,1,0:T(8,128)(2,1)S(1)}, u32[]{:S(2)}, u32[]{:S(2)}) collective-permute-start(bf16[4,16,5376]{2,1,0:T(8,128)(2,1)} %collective-permute-done.36.refs_5_), channel_id=1, source_target_pairs={{0,12},{1,49},{2,14},{3,51},{4,0},{5,53},{6,2},{7,55},{8,4},{9,57}... | collective-permute-start | bytes 2064392 | tf_op jit(solution)/shard_map/ppermute | solution.py:38
  (21 other events, 142.3 us)

commit v6 on v5

--- a/solution.py
+++ b/solution.py
@@ -185,8 +185,8 @@
 
     near = jnp.where(zl == 0, out_proj[:, :half], out_proj[:, half:])
     share, shared = 80, 320
-    shares = lax.dynamic_slice_in_dim(out_proj, spot * share, share, 0)
-    received = flip_z(jnp.where(zl == 0, shares[:, half:], shares[:, :half]), 1, 0)
+    wanted = lax.dynamic_slice(out_proj, (spot * share, (1 - zl) * half), (share, half))
+    received = flip_z(wanted, 1, 0)
     rest = out_proj[shared:]
     direct = flip_z(jnp.where(zl == 0, rest[:, half:], rest[:, :half]), 1, 1)
     far_attention = flip_z(attention, 1, 0)

time: 161 us -> 161 us (level)
  other arithmetic: 21 us -> 19 us
  local copies, waits for them, and re-layouts: 3.07 us -> 4.87 us
    select_n x1 -> x0, other arithmetic: 2 us -> none  [local(): jnp.where(zl == 0, shares[:, half:], shares[:, :half])]
    dynamic_slice x0 -> x1, local copies, waits for them, and re-layouts: none -> 1.8 us  [local(): lax.dynamic_slice(out_proj, (spot * share, (1 - zl) * half), (share, half))]
where the time goes in v6:
time: 161 us
  waiting for transfers between devices  61.3 us (38%)
  starting transfers between devices  48.9 us (30%)
  other arithmetic  19 us (12%)
  matrix products  13.8 us (9%)
  Pallas kernels  11.4 us (7%)
  local copies, waits for them, and re-layouts  4.87 us (3%)
    ppermute x39, waiting for transfers between devices, move(): lax.ppermute(value, axes, [(flat(p), flat(target(*p))) for p in places])  61.3 us
    ppermute x39, starting transfers between devices, move(): lax.ppermute(value, axes, [(flat(p), flat(target(*p))) for p in places])  48.9 us
    pallas_call x2, Pallas kernels, place_rows(): pl.pallas_call(place_more_kernel if before else place_kernel, grid_spec=p...  5.91 us
    pallas_call x2, Pallas kernels, gradient_pieces(): pl.pallas_call(gradient_kernel, grid_spec=pltpu.PrefetchScalarGridSpec(nu...  4.56 us
    dot_general x1, matrix products, local(): lax.dot_general(near, attention, left_rows, preferred_element_type=f32)  4.38 us
    dot_general x1, matrix products, local(): lax.dot_general(pair, near, to_heads, preferred_element_type=f32)  4.33 us
    convert_element_type x1, other arithmetic, local(): pre_grad = (inv_rms * scaled - pre * inv_rms ** 3 * proj).astype(bf16)  3.95 us
    dot_general x1, matrix products, local(): lax.dot_general(pair, far, to_heads, preferred_element_type=f32)  3.48 us
  transfers between devices with their start and end apart: 39, of which 28 were waited for; matrix products, arithmetic and copies ran while one was open for 14% of the time, Pallas kernels for 4%

profile of v6, /device:TPU:6, one launch (start us, length us, event | category | flops | bytes accessed | tf_op | source)
XLA Modules:
  0.0 160.6 jit_solution(15345655802351195958)
XLA Ops:
  7.5 4.1 %collective-permute-start.4 = (bf16[192,2688]{1,0:T(8,128)(2,1)S(1)}, bf16[192,2688]{1,0:T(8,128)(2,1)S(1)}, u32[]{:S(2)}, u32[]{:S(2)}) collective-permute-start(bf16[192,2688]{1,0:T(8,128)(2,1)S(1)} %slice_select_fusion.2), channel_id=1, source_target_pairs={{0,66},{1,67},{2,64},{3,65},{4,70},{5,71},{6,68},{7,69},{8,74},{9,... | collective-permute-start | bytes 3096584 | tf_op jit(solution)/shard_map/ppermute | solution.py:38
  11.6 3.9 %collective-permute-done = bf16[80,2688]{1,0:T(8,128)(2,1)S(1)} collective-permute-done((bf16[80,2688]{1,0:T(8,128)(2,1)}, bf16[80,2688]{1,0:T(8,128)(2,1)S(1)}, u32[]{:S(2)}, u32[]{:S(2)}) %collective-permute-start) | collective-permute-done | bytes 430112 | tf_op jit(solution)/shard_map/ppermute | solution.py:38
  19.5 4.4 %fusion.11 = f32[2688,512]{1,0:T(8,128)S(1)} fusion(bf16[512,512]{1,0:T(8,128)(2,1)} %param.9, bf16[512,5376]{1,0:T(8,128)(2,1)} %param.10, pred[]{:T(512)S(6)} %eq.33), kind=kOutput, calls=%fused_computation.39 | convolution fusion | flops 1410662400 | bytes 11534337 | tf_op jit(solution)/shard_map/dot_general | solution.py:200
  23.9 5.6 %collective-permute-done.3 = bf16[80,2688]{1,0:T(8,128)(2,1)S(1)} collective-permute-done((bf16[80,2688]{1,0:T(8,128)(2,1)S(1)}, bf16[80,2688]{1,0:T(8,128)(2,1)S(1)}, u32[]{:S(2)}, u32[]{:S(2)}) %collective-permute-start.3) | collective-permute-done | bytes 430112 | tf_op jit(solution)/shard_map/ppermute | solution.py:38
  30.8 3.0 %collective-permute-done.4 = bf16[192,2688]{1,0:T(8,128)(2,1)S(1)} collective-permute-done((bf16[192,2688]{1,0:T(8,128)(2,1)S(1)}, bf16[192,2688]{1,0:T(8,128)(2,1)S(1)}, u32[]{:S(2)}, u32[]{:S(2)}) %collective-permute-start.4) | collective-permute-done | bytes 1032224 | tf_op jit(solution)/shard_map/ppermute | solution.py:38
  38.6 2.6 %collective-permute-done.6 = bf16[1344,512]{1,0:T(8,128)(2,1)} collective-permute-done((bf16[1344,512]{1,0:T(8,128)(2,1)}, bf16[1344,512]{1,0:T(8,128)(2,1)}, u32[]{:S(2)}, u32[]{:S(2)}) %collective-permute-start.6) | collective-permute-done | bytes 1376288 | tf_op jit(solution)/shard_map/ppermute | solution.py:38
  41.2 2.5 %multiply_reduce_fusion = (f32[512]{0:T(512)S(1)}, f32[512]{0:T(512)S(1)}) fusion(f32[1344,512]{1,0:T(8,128)S(1)} %slice_select_fusion.1, bf16[1344,512]{1,0:T(8,128)(2,1)} %collective-permute-done.6, f32[1344]{0:T(1024)S(1)} %dynamic_slice.26, bf16[512,1344]{0,1:T(8,128)(2,1)} %param.13), kind=kLoop, calls=%fused_computation.14 | loop fusion | flops 5504000 | bytes 5514496 | tf_op jit(solution)/shard_map/reduce_sum | solution.py:209
  45.0 3.6 %collective-permute-done.8 = f32[2,512]{1,0:T(2,128)S(1)} collective-permute-done((f32[2,512]{1,0:T(2,128)S(1)}, f32[2,512]{1,0:T(2,128)S(1)}, u32[]{:S(2)}, u32[]{:S(2)}) %collective-permute-start.8) | collective-permute-done | bytes 4128 | tf_op jit(solution)/shard_map/ppermute | solution.py:38
  48.7 4.0 %fusion.2 = (bf16[1344,512]{1,0:T(8,128)(2,1)}, bf16[512,1344]{0,1:T(8,128)(2,1)}) fusion(bf16[512,1344]{0,1:T(8,128)(2,1)} %param.13, f32[512]{0:T(512)S(1)} %bitcast.92, f32[512]{0:T(512)S(1)} %bitcast.90, f32[512]{0:T(512)S(1)} %bitcast.91, f32[1344]{0:T(1024)S(1)} %dynamic_slice.26, f32[1344,512]{1,0:T(8,128)S(1)} %slice_select_fusion.1, ...), kind=kLoop, calls=%fused_computation.10 | loop fusion | flops 9633792 | bytes 9645312 | tf_op jit(solution)/shard_map/convert_element_type | solution.py:215
  67.3 4.5 %collective-permute-done.18 = bf16[8,16,2688]{2,1,0:T(8,128)(2,1)S(1)} collective-permute-done((bf16[8,16,2688]{2,1,0:T(8,128)(2,1)S(1)}, bf16[8,16,2688]{2,1,0:T(8,128)(2,1)S(1)}, u32[]{:S(2)}, u32[]{:S(2)}) %collective-permute-start.18) | collective-permute-done | bytes 688160 | tf_op jit(solution)/shard_map/ppermute | solution.py:38
  75.3 7.1 %collective-permute-done.17 = bf16[8,16,2688]{2,1,0:T(8,128)(2,1)S(1)} collective-permute-done((bf16[8,16,2688]{2,1,0:T(8,128)(2,1)S(1)}, bf16[8,16,2688]{2,1,0:T(8,128)(2,1)S(1)}, u32[]{:S(2)}, u32[]{:S(2)}) %collective-permute-start.17) | collective-permute-done | bytes 688160 | tf_op jit(solution)/shard_map/ppermute | solution.py:38
  82.4 4.1 %collective-permute-done.19 = bf16[8,16,2688]{2,1,0:T(8,128)(2,1)S(1)} collective-permute-done((bf16[8,16,2688]{2,1,0:T(8,128)(2,1)S(1)}, bf16[8,16,2688]{2,1,0:T(8,128)(2,1)S(1)}, u32[]{:S(2)}, u32[]{:S(2)}) %collective-permute-start.19) | collective-permute-done | bytes 688160 | tf_op jit(solution)/shard_map/ppermute | solution.py:38
  86.8 3.3 %collective-permute-start.20 = (bf16[2,16,2688]{2,1,0:T(8,128)(2,1)S(1)}, bf16[2,16,2688]{2,1,0:T(8,128)(2,1)S(1)}, u32[]{:S(2)}, u32[]{:S(2)}) collective-permute-start(bf16[2,16,2688]{2,1,0:T(8,128)(2,1)S(1)} %get-tuple-element.49), channel_id=1, source_target_pairs={{0,32},{1,9},{2,34},{3,11},{4,36},{5,13},{6,38},{7,15},{8,40},{9,1... | collective-permute-start | bytes 516104 | tf_op jit(solution)/shard_map/ppermute | solution.py:38
  93.4 2.5 %collective-permute-start.16 = (bf16[2,16,2688]{2,1,0:T(8,128)(2,1)S(1)}, bf16[2,16,2688]{2,1,0:T(8,128)(2,1)S(1)}, u32[]{:S(2)}, u32[]{:S(2)}) collective-permute-start(bf16[2,16,2688]{2,1,0:T(8,128)(2,1)S(1)} %get-tuple-element.47), channel_id=1, source_target_pairs={{0,48},{1,13},{2,50},{3,15},{4,52},{5,1},{6,54},{7,3},{8,56},{9,5}... | collective-permute-start | bytes 516104 | tf_op jit(solution)/shard_map/ppermute | solution.py:38
  96.0 3.6 %collective-permute-done.21 = bf16[2,16,2688]{2,1,0:T(8,128)(2,1)S(1)} collective-permute-done((bf16[2,16,2688]{2,1,0:T(8,128)(2,1)S(1)}, bf16[2,16,2688]{2,1,0:T(8,128)(2,1)S(1)}, u32[]{:S(2)}, u32[]{:S(2)}) %collective-permute-start.21) | collective-permute-done | bytes 172064 | tf_op jit(solution)/shard_map/ppermute | solution.py:38
  99.7 2.5 %collective-permute-start.23 = (bf16[16,2688]{1,0:T(8,128)(2,1)S(1)}, bf16[16,2688]{1,0:T(8,128)(2,1)S(1)}, u32[]{:S(2)}, u32[]{:S(2)}) collective-permute-start(bf16[16,2688]{1,0:T(8,128)(2,1)S(1)} %get-tuple-element.53), channel_id=1, source_target_pairs={{0,64},{1,65},{2,66},{3,67},{4,68},{5,69},{6,70},{7,71},{8,72},{9,... | collective-permute-start | bytes 258056 | tf_op jit(solution)/shard_map/ppermute | solution.py:38
  115.3 2.4 %collective-permute-done.29.refs_4_ = bf16[1,16,5376]{2,1,0:T(8,128)(2,1)S(1)} collective-permute-done((bf16[1,16,5376]{2,1,0:T(8,128)(2,1)S(1)}, bf16[1,16,5376]{2,1,0:T(8,128)(2,1)S(1)}, u32[]{:S(2)}, u32[]{:S(2)}) %collective-permute-start.29) | collective-permute-done | bytes 172064 | tf_op jit(solution)/shard_map/ppermute | solution.py:38
  124.7 2.7 %collective-permute-done.30.refs_5_ = bf16[1,16,5376]{2,1,0:T(8,128)(2,1)S(1)} collective-permute-done((bf16[1,16,5376]{2,1,0:T(8,128)(2,1)S(1)}, bf16[1,16,5376]{2,1,0:T(8,128)(2,1)S(1)}, u32[]{:S(2)}, u32[]{:S(2)}) %collective-permute-start.30) | collective-permute-done | bytes 172064 | tf_op jit(solution)/shard_map/ppermute | solution.py:38
  128.4 3.2 %collective-permute-start.33 = (bf16[4,16,5376]{2,1,0:T(8,128)(2,1)S(1)}, bf16[4,16,5376]{2,1,0:T(8,128)(2,1)}, u32[]{:S(2)}, u32[]{:S(2)}) collective-permute-start(bf16[4,16,5376]{2,1,0:T(8,128)(2,1)S(1)} %get-tuple-element.30.refs_0_), channel_id=1, source_target_pairs={{0,4},{1,17},{2,6},{3,19},{4,8},{5,21},{6,10},{7,23},{8,12},{9,25}... | collective-permute-start | bytes 2064392 | tf_op jit(solution)/shard_map/ppermute | solution.py:38
  132.0 3.5 %convolution_convert_fusion = bf16[512,512]{1,0:T(8,128)(2,1)S(1)} fusion(bf16[2688,512]{1,0:T(8,128)(2,1)S(1)} %pad_maximum_fusion.right_ref, bf16[512,2688]{1,0:T(8,128)(2,1)} %copy-done), kind=kOutput, calls=%fused_computation.30 | convolution fusion | flops 1409548288 | bytes 6029312 | tf_op jit(solution)/shard_map/dot_general | solution.py:298
  140.1 3.8 %collective-permute-start.37 = (bf16[4,16,5376]{2,1,0:T(8,128)(2,1)}, bf16[4,16,5376]{2,1,0:T(8,128)(2,1)S(1)}, u32[]{:S(2)}, u32[]{:S(2)}) collective-permute-start(bf16[4,16,5376]{2,1,0:T(8,128)(2,1)} %collective-permute-done.33.refs_2_), channel_id=1, source_target_pairs={{0,4},{1,17},{2,6},{3,19},{4,8},{5,21},{6,10},{7,23},{8,12},{9,25}... | collective-permute-start | bytes 2064392 | tf_op jit(solution)/shard_map/ppermute | solution.py:38
  144.1 4.3 %fusion.10 = f32[512,512]{1,0:T(8,128)S(1)} fusion(bf16[2688,512]{1,0:T(8,128)(2,1)S(1)} %pad_maximum_fusion.right_ref, bf16[512,5376]{1,0:T(8,128)(2,1)} %param.10, pred[]{:T(512)S(6)} %eq.33), kind=kOutput, calls=%fused_computation.38 | convolution fusion | flops 1410662400 | bytes 9306113 | tf_op jit(solution)/shard_map/dot_general | solution.py:299
  151.3 4.2 %shard_map.139.earlier_ref = bf16[512,5376]{1,0:T(8,128)(2,1)} custom-call(s32[24]{0:T(128)S(1)} %pad_add_fusion.1.rows_ref, bf16[4,16,5376]{2,1,0:T(8,128)(2,1)S(1)} %get-tuple-element.30.refs_0_, bf16[4,16,5376]{2,1,0:T(8,128)(2,1)} %get-tuple-element.31.refs_1_, bf16[4,16,5376]{2,1,0:T(8,128)(2,1)} %collective-permute-done.33.refs_2_, ...), custom_call_target="tpu_custom_call" | custom-call | bytes 8400000 | tf_op jit(solution)/shard_map/pallas_call | solution.py:156
  155.6 3.1 %collective-permute-done.38.refs_1_ = bf16[4,16,5376]{2,1,0:T(8,128)(2,1)S(1)} collective-permute-done((bf16[4,16,5376]{2,1,0:T(8,128)(2,1)}, bf16[4,16,5376]{2,1,0:T(8,128)(2,1)S(1)}, u32[]{:S(2)}, u32[]{:S(2)}) %collective-permute-start.38) | collective-permute-done | bytes 688160 | tf_op jit(solution)/shard_map/ppermute | solution.py:38
  (136 shorter events, 70.7 us)
Async XLA Ops:
  2.5 13.0 %collective-permute-start = (bf16[80,2688]{1,0:T(8,128)(2,1)}, bf16[80,2688]{1,0:T(8,128)(2,1)S(1)}, u32[]{:S(2)}, u32[]{:S(2)}) collective-permute-start(bf16[80,2688]{1,0:T(8,128)(2,1)} %dynamic_slice.27), channel_id=1, source_target_pairs={{0,2},{1,3},{2,0},{3,1},{4,6},{5,7},{6,4},{7,5},{8,10},{9,11},{10,... | collective-permute-start | bytes 1290248 | tf_op jit(solution)/shard_map/ppermute | solution.py:38
  5.6 28.3 %collective-permute-start.5 = (bf16[512,512]{0,1:T(8,128)(2,1)S(1)}, bf16[512,512]{0,1:T(8,128)(2,1)S(1)}, u32[]{:S(2)}, u32[]{:S(2)}) collective-permute-start(bf16[512,512]{0,1:T(8,128)(2,1)S(1)} %copy.18), channel_id=1, source_target_pairs={{0,2},{1,3},{2,0},{3,1},{4,6},{5,7},{6,4},{7,5},{8,10},{9,11},{10,... | collective-permute-start | bytes 1572872 | tf_op jit(solution)/shard_map/ppermute | solution.py:38
  7.5 26.4 %collective-permute-start.4 = (bf16[192,2688]{1,0:T(8,128)(2,1)S(1)}, bf16[192,2688]{1,0:T(8,128)(2,1)S(1)}, u32[]{:S(2)}, u32[]{:S(2)}) collective-permute-start(bf16[192,2688]{1,0:T(8,128)(2,1)S(1)} %slice_select_fusion.2), channel_id=1, source_target_pairs={{0,66},{1,67},{2,64},{3,65},{4,70},{5,71},{6,68},{7,69},{8,74},{9,... | collective-permute-start | bytes 3096584 | tf_op jit(solution)/shard_map/ppermute | solution.py:38
  15.4 14.0 %collective-permute-start.3 = (bf16[80,2688]{1,0:T(8,128)(2,1)S(1)}, bf16[80,2688]{1,0:T(8,128)(2,1)S(1)}, u32[]{:S(2)}, u32[]{:S(2)}) collective-permute-start(bf16[80,2688]{1,0:T(8,128)(2,1)S(1)} %collective-permute-done), channel_id=1, source_target_pairs={{0,12},{1,49},{2,14},{3,51},{4,0},{5,53},{6,2},{7,55},{8,4},{9,57}... | collective-permute-start | bytes 1290248 | tf_op jit(solution)/shard_map/ppermute | solution.py:38
  16.3 13.2 %collective-permute-start.2 = (bf16[80,2688]{1,0:T(8,128)(2,1)S(1)}, bf16[80,2688]{1,0:T(8,128)(2,1)S(1)}, u32[]{:S(2)}, u32[]{:S(2)}) collective-permute-start(bf16[80,2688]{1,0:T(8,128)(2,1)S(1)} %collective-permute-done), channel_id=1, source_target_pairs={{0,8},{1,33},{2,10},{3,35},{4,12},{5,37},{6,14},{7,39},{8,0},{9,41... | collective-permute-start | bytes 1290248 | tf_op jit(solution)/shard_map/ppermute | solution.py:38
  17.3 13.0 %collective-permute-start.1 = (bf16[80,2688]{1,0:T(8,128)(2,1)S(1)}, bf16[80,2688]{1,0:T(8,128)(2,1)S(1)}, u32[]{:S(2)}, u32[]{:S(2)}) collective-permute-start(bf16[80,2688]{1,0:T(8,128)(2,1)S(1)} %collective-permute-done), channel_id=1, source_target_pairs={{0,4},{1,17},{2,6},{3,19},{4,8},{5,21},{6,10},{7,23},{8,12},{9,25}... | collective-permute-start | bytes 1290248 | tf_op jit(solution)/shard_map/ppermute | solution.py:38
  60.8 11.0 %collective-permute-start.18 = (bf16[8,16,2688]{2,1,0:T(8,128)(2,1)S(1)}, bf16[8,16,2688]{2,1,0:T(8,128)(2,1)S(1)}, u32[]{:S(2)}, u32[]{:S(2)}) collective-permute-start(bf16[8,16,2688]{2,1,0:T(8,128)(2,1)S(1)} %get-tuple-element.29), channel_id=1, source_target_pairs={{0,4},{1,17},{2,6},{3,19},{4,8},{5,21},{6,10},{7,23},{8,12},{9,25}... | collective-permute-start | bytes 2064392 | tf_op jit(solution)/shard_map/ppermute | solution.py:38
  61.4 30.7 %collective-permute-start.11 = (bf16[8,16,2688]{2,1,0:T(8,128)(2,1)S(1)}, bf16[8,16,2688]{2,1,0:T(8,128)(2,1)S(1)}, u32[]{:S(2)}, u32[]{:S(2)}) collective-permute-start(bf16[8,16,2688]{2,1,0:T(8,128)(2,1)S(1)} %get-tuple-element.23), channel_id=1, source_target_pairs={{0,4},{1,17},{2,6},{3,19},{4,8},{5,21},{6,10},{7,23},{8,12},{9,25}... | collective-permute-start | bytes 2064392 | tf_op jit(solution)/shard_map/ppermute | solution.py:38
  62.9 12.1 %collective-permute-start.12 = (bf16[8,16,2688]{2,1,0:T(8,128)(2,1)S(1)}, bf16[8,16,2688]{2,1,0:T(8,128)(2,1)S(1)}, u32[]{:S(2)}, u32[]{:S(2)}) collective-permute-start(bf16[8,16,2688]{2,1,0:T(8,128)(2,1)S(1)} %get-tuple-element.25), channel_id=1, source_target_pairs={{0,12},{1,49},{2,14},{3,51},{4,0},{5,53},{6,2},{7,55},{8,4},{9,57}... | collective-permute-start | bytes 2064392 | tf_op jit(solution)/shard_map/ppermute | solution.py:38
  63.4 19.0 %collective-permute-start.17 = (bf16[8,16,2688]{2,1,0:T(8,128)(2,1)S(1)}, bf16[8,16,2688]{2,1,0:T(8,128)(2,1)S(1)}, u32[]{:S(2)}, u32[]{:S(2)}) collective-permute-start(bf16[8,16,2688]{2,1,0:T(8,128)(2,1)S(1)} %get-tuple-element.27), channel_id=1, source_target_pairs={{0,12},{1,49},{2,14},{3,51},{4,0},{5,53},{6,2},{7,55},{8,4},{9,57}... | collective-permute-start | bytes 2064392 | tf_op jit(solution)/shard_map/ppermute | solution.py:38
  71.9 14.6 %collective-permute-start.19 = (bf16[8,16,2688]{2,1,0:T(8,128)(2,1)S(1)}, bf16[8,16,2688]{2,1,0:T(8,128)(2,1)S(1)}, u32[]{:S(2)}, u32[]{:S(2)}) collective-permute-start(bf16[8,16,2688]{2,1,0:T(8,128)(2,1)S(1)} %add_convert_fusion.1), channel_id=1, source_target_pairs={{0,4},{1,17},{2,6},{3,19},{4,8},{5,21},{6,10},{7,23},{8,12},{9,25}... | collective-permute-start | bytes 2064392 | tf_op jit(solution)/shard_map/ppermute | solution.py:38
  75.2 16.9 %collective-permute-start.13 = (bf16[8,16,2688]{2,1,0:T(8,128)(2,1)S(1)}, bf16[8,16,2688]{2,1,0:T(8,128)(2,1)S(1)}, u32[]{:S(2)}, u32[]{:S(2)}) collective-permute-start(bf16[8,16,2688]{2,1,0:T(8,128)(2,1)S(1)} %add_convert_fusion.3), channel_id=1, source_target_pairs={{0,12},{1,49},{2,14},{3,51},{4,0},{5,53},{6,2},{7,55},{8,4},{9,57}... | collective-permute-start | bytes 2064392 | tf_op jit(solution)/shard_map/ppermute | solution.py:38
  86.8 9.1 %collective-permute-start.20 = (bf16[2,16,2688]{2,1,0:T(8,128)(2,1)S(1)}, bf16[2,16,2688]{2,1,0:T(8,128)(2,1)S(1)}, u32[]{:S(2)}, u32[]{:S(2)}) collective-permute-start(bf16[2,16,2688]{2,1,0:T(8,128)(2,1)S(1)} %get-tuple-element.49), channel_id=1, source_target_pairs={{0,32},{1,9},{2,34},{3,11},{4,36},{5,13},{6,38},{7,15},{8,40},{9,1... | collective-permute-start | bytes 516104 | tf_op jit(solution)/shard_map/ppermute | solution.py:38
  91.2 8.5 %collective-permute-start.21 = (bf16[2,16,2688]{2,1,0:T(8,128)(2,1)S(1)}, bf16[2,16,2688]{2,1,0:T(8,128)(2,1)S(1)}, u32[]{:S(2)}, u32[]{:S(2)}) collective-permute-start(bf16[2,16,2688]{2,1,0:T(8,128)(2,1)S(1)} %get-tuple-element.51), channel_id=1, source_target_pairs={{0,16},{1,5},{2,18},{3,7},{4,20},{5,9},{6,22},{7,11},{8,24},{9,13}... | collective-permute-start | bytes 516104 | tf_op jit(solution)/shard_map/ppermute | solution.py:38
  92.5 9.7 %collective-permute-start.14 = (bf16[2,16,2688]{2,1,0:T(8,128)(2,1)S(1)}, bf16[2,16,2688]{2,1,0:T(8,128)(2,1)S(1)}, u32[]{:S(2)}, u32[]{:S(2)}) collective-permute-start(bf16[2,16,2688]{2,1,0:T(8,128)(2,1)S(1)} %get-tuple-element.46), channel_id=1, source_target_pairs={{0,32},{1,9},{2,34},{3,11},{4,36},{5,13},{6,38},{7,15},{8,40},{9,1... | collective-permute-start | bytes 516104 | tf_op jit(solution)/shard_map/ppermute | solution.py:38
  93.4 8.8 %collective-permute-start.16 = (bf16[2,16,2688]{2,1,0:T(8,128)(2,1)S(1)}, bf16[2,16,2688]{2,1,0:T(8,128)(2,1)S(1)}, u32[]{:S(2)}, u32[]{:S(2)}) collective-permute-start(bf16[2,16,2688]{2,1,0:T(8,128)(2,1)S(1)} %get-tuple-element.47), channel_id=1, source_target_pairs={{0,48},{1,13},{2,50},{3,15},{4,52},{5,1},{6,54},{7,3},{8,56},{9,5}... | collective-permute-start | bytes 516104 | tf_op jit(solution)/shard_map/ppermute | solution.py:38
  114.5 8.3 %collective-permute-start.26 = (bf16[1,16,5376]{2,1,0:T(8,128)(2,1)S(1)}, bf16[1,16,5376]{2,1,0:T(8,128)(2,1)S(1)}, u32[]{:S(2)}, u32[]{:S(2)}) collective-permute-start(bf16[1,16,5376]{2,1,0:T(8,128)(2,1)S(1)} %get-tuple-element.34.refs_0_), channel_id=1, source_target_pairs={{0,16},{1,5},{2,18},{3,7},{4,20},{5,9},{6,22},{7,11},{8,24},{9,13}... | collective-permute-start | bytes 516104 | tf_op jit(solution)/shard_map/ppermute | solution.py:38
  128.4 11.7 %collective-permute-start.33 = (bf16[4,16,5376]{2,1,0:T(8,128)(2,1)S(1)}, bf16[4,16,5376]{2,1,0:T(8,128)(2,1)}, u32[]{:S(2)}, u32[]{:S(2)}) collective-permute-start(bf16[4,16,5376]{2,1,0:T(8,128)(2,1)S(1)} %get-tuple-element.30.refs_0_), channel_id=1, source_target_pairs={{0,4},{1,17},{2,6},{3,19},{4,8},{5,21},{6,10},{7,23},{8,12},{9,25}... | collective-permute-start | bytes 2064392 | tf_op jit(solution)/shard_map/ppermute | solution.py:38
  131.6 12.5 %collective-permute-start.36 = (bf16[4,16,5376]{2,1,0:T(8,128)(2,1)}, bf16[4,16,5376]{2,1,0:T(8,128)(2,1)}, u32[]{:S(2)}, u32[]{:S(2)}) collective-permute-start(bf16[4,16,5376]{2,1,0:T(8,128)(2,1)} %get-tuple-element.31.refs_1_), channel_id=1, source_target_pairs={{0,12},{1,49},{2,14},{3,51},{4,0},{5,53},{6,2},{7,55},{8,4},{9,57}... | collective-permute-start | bytes 2064392 | tf_op jit(solution)/shard_map/ppermute | solution.py:38
  135.5 12.9 %collective-permute-start.10 = (bf16[512,512]{1,0:T(8,128)(2,1)S(1)}, bf16[512,512]{1,0:T(8,128)(2,1)S(1)}, u32[]{:S(2)}, u32[]{:S(2)}) collective-permute-start(bf16[512,512]{1,0:T(8,128)(2,1)S(1)} %convolution_convert_fusion), channel_id=1, source_target_pairs={{0,2},{1,3},{2,0},{3,1},{4,6},{5,7},{6,4},{7,5},{8,10},{9,11},{10,... | collective-permute-start | bytes 1572872 | tf_op jit(solution)/shard_map/ppermute | solution.py:38
  135.8 15.5 %collective-permute-start.35 = (bf16[4,16,5376]{2,1,0:T(8,128)(2,1)S(1)}, bf16[4,16,5376]{2,1,0:T(8,128)(2,1)S(1)}, u32[]{:S(2)}, u32[]{:S(2)}) collective-permute-start(bf16[4,16,5376]{2,1,0:T(8,128)(2,1)S(1)} %get-tuple-element.30.refs_0_), channel_id=1, source_target_pairs={{0,12},{1,49},{2,14},{3,51},{4,0},{5,53},{6,2},{7,55},{8,4},{9,57}... | collective-permute-start | bytes 2064392 | tf_op jit(solution)/shard_map/ppermute | solution.py:38
  137.0 14.4 %collective-permute-start.34 = (bf16[4,16,5376]{2,1,0:T(8,128)(2,1)}, bf16[4,16,5376]{2,1,0:T(8,128)(2,1)S(1)}, u32[]{:S(2)}, u32[]{:S(2)}) collective-permute-start(bf16[4,16,5376]{2,1,0:T(8,128)(2,1)} %get-tuple-element.31.refs_1_), channel_id=1, source_target_pairs={{0,4},{1,17},{2,6},{3,19},{4,8},{5,21},{6,10},{7,23},{8,12},{9,25}... | collective-permute-start | bytes 2064392 | tf_op jit(solution)/shard_map/ppermute | solution.py:38
  140.1 15.5 %collective-permute-start.37 = (bf16[4,16,5376]{2,1,0:T(8,128)(2,1)}, bf16[4,16,5376]{2,1,0:T(8,128)(2,1)S(1)}, u32[]{:S(2)}, u32[]{:S(2)}) collective-permute-start(bf16[4,16,5376]{2,1,0:T(8,128)(2,1)} %collective-permute-done.33.refs_2_), channel_id=1, source_target_pairs={{0,4},{1,17},{2,6},{3,19},{4,8},{5,21},{6,10},{7,23},{8,12},{9,25}... | collective-permute-start | bytes 2064392 | tf_op jit(solution)/shard_map/ppermute | solution.py:38
  144.1 14.6 %collective-permute-start.38 = (bf16[4,16,5376]{2,1,0:T(8,128)(2,1)}, bf16[4,16,5376]{2,1,0:T(8,128)(2,1)S(1)}, u32[]{:S(2)}, u32[]{:S(2)}) collective-permute-start(bf16[4,16,5376]{2,1,0:T(8,128)(2,1)} %collective-permute-done.36.refs_5_), channel_id=1, source_target_pairs={{0,12},{1,49},{2,14},{3,51},{4,0},{5,53},{6,2},{7,55},{8,4},{9,57}... | collective-permute-start | bytes 2064392 | tf_op jit(solution)/shard_map/ppermute | solution.py:38
  (21 other events, 142.3 us)
